TPU v7x, 512 devices: a whole 4x4x16 slice. The times are simulated.
512 devices in a mesh: seq: 32 (over x, y, core), head: 16 (over z).
Axes of the slice: x: 4, y: 4, z: 16, core: 2. Of those that a mesh axis runs over, the one named last changes fastest.
Arguments:
- query_data: bfloat16 [16384, 2048], P(('seq', 'head')), may hold values from -120 to 120
- key_data: bfloat16 [16384, 2048], P(('seq', 'head')), may hold values from -4 to 4
- value_data: bfloat16 [16384, 2048], P(('seq', 'head')), may hold values from -6 to 6
- output_data: bfloat16 [16384, 2048], P(('seq', 'head')), may hold values from -4 to 4
- output_grad: bfloat16 [16384, 2048], P(('seq', 'head')), may hold values from -6 to 6
- key_lists: int32 [32, 16], replicated, may hold values from 0 to 31, as said below
- key_counts: int32 [32], replicated, may hold values from 1 to 16, as said below
- block_order: int32 [32], replicated, may hold values from 0 to 31, as said below
Outputs:
- query_grad: bfloat16 [16384, 2048], P(('seq', 'head'))
- key_grad: bfloat16 [16384, 2048], P(('seq', 'head'))
- value_grad: bfloat16 [16384, 2048], P(('seq', 'head'))
Inputs may be any that keep to these rules, and one draw needn't show every extreme that they name: `key_lists`: row i names sequence blocks: entry 0 is i itself; entries 1 to key_counts[i] - 1 are distinct earlier blocks, each stored on a different device of seq and none on the device that stores block i (device of stored block p: p); the entries after them repeat i. `key_counts`: block 0 uses 1 entry and block 31 uses 16. `block_order`: A permutation of the sequence blocks.
All inputs are finite; a program needn't handle non-finite values.
Results may differ from a plain program's by a relative error of at most 0.011.
Values may be sent and summed in bfloat16 or wider, within the bound.
No kernel may reach another device: no remote copies, remote signals or barrier semaphores. Data moves between devices by JAX's collectives and lax.ppermute only.
A program may use at most 64 MiB of HBM per device.

v0:
```python
import math

import jax
import jax.numpy as jnp
from jax import lax
from jax.sharding import PartitionSpec as P

HD = 128
BLK = 512


LOW_SCORE = -1e30


def scores_for(queries, keys_sel, scale):
    return (
        jnp.einsum("grhd,gchd->ghrc", queries, keys_sel, preferred_element_type=jnp.float32) * scale
    )


def on_device(
    query_data, key_data, value_data, output_data, output_grad, key_lists, key_counts, block_order
):
    query_here, key_here, value_here, output_here, grad_here = (
        lax.all_to_all(query_data, "head", split_axis=1, concat_axis=0, tiled=True),
        lax.all_to_all(key_data, "head", split_axis=1, concat_axis=0, tiled=True),
        lax.all_to_all(value_data, "head", split_axis=1, concat_axis=0, tiled=True),
        lax.all_to_all(output_data, "head", split_axis=1, concat_axis=0, tiled=True),
        lax.all_to_all(output_grad, "head", split_axis=1, concat_axis=0, tiled=True),
    )
    row_count, head_span = query_here.shape
    head_count = head_span // HD
    own_blocks = row_count // BLK
    n_blocks = block_order.shape[0]
    scale = 1.0 / math.sqrt(HD)
    batch_size = 2
    device = lax.axis_index("seq")
    mine = lax.dynamic_slice_in_dim(block_order, device * own_blocks, own_blocks)
    lists_stored = key_lists[block_order]
    counts_stored = key_counts[block_order]
    entry_used = jnp.arange(key_lists.shape[1], dtype=jnp.int32)[None, :] < counts_stored[:, None]
    matches = (lists_stored[:, :, None] == mine[None, None, :]) & entry_used[:, :, None]
    named = jnp.any(matches, axis=1)
    active = jnp.any(named, axis=1)
    slot_block = jnp.sum(
        named.astype(jnp.int32) * jnp.arange(own_blocks, dtype=jnp.int32)[None, :], axis=1
    )
    diagonal = block_order == mine[slot_block]
    n_active = jnp.sum(active.astype(jnp.int32))
    visit_order = jnp.argsort(jnp.where(active, 0, 1), stable=True)
    n_batches = (n_active + batch_size - 1) // batch_size
    keys_own = key_here.reshape(own_blocks, BLK, head_count, HD)
    values_own = value_here.reshape(own_blocks, BLK, head_count, HD)
    query_all = lax.all_gather(query_here, "seq", axis=0, tiled=True)
    query_slots = query_all.reshape(n_blocks, BLK, head_count, HD)
    positions = jnp.arange(BLK, dtype=jnp.int32)
    causal = positions[None, :] <= positions[:, None]

    def select(counter):
        slots = lax.dynamic_slice_in_dim(visit_order, counter * batch_size, batch_size)
        valid = counter * batch_size + jnp.arange(batch_size, dtype=jnp.int32) < n_active
        allowed = valid[:, None, None, None] & (
            (~diagonal[slots])[:, None, None, None] | causal[None, None]
        )
        return (slots, valid, allowed)

    def first_pass(counter, carry):
        maxima_all, totals_all = carry
        slots, valid, allowed = select(counter)
        scores = scores_for(query_slots[slots], keys_own[slot_block[slots]], scale)
        maxima = jnp.max(jnp.where(allowed, scores, LOW_SCORE), axis=3)
        totals = jnp.sum(jnp.where(allowed, jnp.exp(scores - maxima[..., None]), 0.0), axis=3)
        return (maxima_all.at[slots].set(maxima), totals_all.at[slots].set(totals))

    start = (
        jnp.full((n_blocks, head_count, BLK), LOW_SCORE, jnp.float32),
        jnp.zeros((n_blocks, head_count, BLK), jnp.float32),
    )
    maxima_all, totals_all = lax.fori_loop(0, n_batches, first_pass, start)
    maxima_back, totals_back = (
        lax.all_to_all(maxima_all, "seq", split_axis=0, concat_axis=0, tiled=True),
        lax.all_to_all(totals_all, "seq", split_axis=0, concat_axis=0, tiled=True),
    )
    maxima_back = maxima_back.reshape(-1, own_blocks, head_count, BLK)
    totals_back = totals_back.reshape(-1, own_blocks, head_count, BLK)
    highest = jnp.max(maxima_back, axis=0)
    summed = jnp.sum(totals_back * jnp.exp(maxima_back - highest[None]), axis=0)
    log_norm = highest + jnp.log(summed)
    products = grad_here.astype(jnp.float32) * output_here.astype(jnp.float32)
    row_dot = jnp.transpose(
        jnp.sum(products.reshape(own_blocks, BLK, head_count, HD), axis=3), (0, 2, 1)
    )
    grad_all = lax.all_gather(grad_here, "seq", axis=0, tiled=True)
    log_all, row_dot_all = (
        lax.all_gather(log_norm, "seq", axis=0, tiled=True),
        lax.all_gather(row_dot, "seq", axis=0, tiled=True),
    )
    grad_slots = grad_all.reshape(n_blocks, BLK, head_count, HD)

    def second_pass(counter, carry):
        key_total, value_total, query_parts = carry
        slots, valid, allowed = select(counter)
        which = slot_block[slots]
        queries = query_slots[slots]
        keys_sel = keys_own[which]
        values_sel = values_own[which]
        grads = grad_slots[slots]
        scores = scores_for(queries, keys_sel, scale)
        probs = jnp.where(allowed, jnp.exp(scores - log_all[slots][..., None]), 0.0)
        probs_low = probs.astype(jnp.bfloat16)
        value_terms = jnp.einsum(
            "ghrc,grhd->gchd", probs_low, grads, preferred_element_type=jnp.float32
        )
        dprob = jnp.einsum("grhd,gchd->ghrc", grads, values_sel, preferred_element_type=jnp.float32)
        dscore_low = (probs * (dprob - row_dot_all[slots][..., None]) * scale).astype(jnp.bfloat16)
        key_terms = jnp.einsum(
            "ghrc,grhd->gchd", dscore_low, queries, preferred_element_type=jnp.float32
        )
        query_terms = jnp.einsum(
            "ghrc,gchd->grhd", dscore_low, keys_sel, preferred_element_type=jnp.float32
        ).astype(jnp.bfloat16)
        weight = valid.astype(jnp.float32)[:, None, None, None]
        key_total = key_total.at[which].add(key_terms * weight)
        value_total = value_total.at[which].add(value_terms * weight)
        query_parts = query_parts.at[slots].set(query_terms.reshape(batch_size, BLK, head_span))
        return (key_total, value_total, query_parts)

    start = (
        jnp.zeros((own_blocks, BLK, head_count, HD), jnp.float32),
        jnp.zeros((own_blocks, BLK, head_count, HD), jnp.float32),
        jnp.zeros((n_blocks, BLK, head_span), jnp.bfloat16),
    )
    key_total, value_total, query_parts = lax.fori_loop(0, n_batches, second_pass, start)
    returned = lax.all_to_all(query_parts, "seq", split_axis=0, concat_axis=0, tiled=True)
    query_sum = jnp.sum(returned, axis=0, dtype=jnp.float32)
    query_grad = query_sum.astype(jnp.bfloat16)
    key_grad = key_total.reshape(row_count, head_span).astype(jnp.bfloat16)
    value_grad = value_total.reshape(row_count, head_span).astype(jnp.bfloat16)
    return (
        lax.all_to_all(query_grad, "head", split_axis=0, concat_axis=1, tiled=True),
        lax.all_to_all(key_grad, "head", split_axis=0, concat_axis=1, tiled=True),
        lax.all_to_all(value_grad, "head", split_axis=0, concat_axis=1, tiled=True),
    )


def solution(mesh):
    placed = (
        P(("seq", "head"), None),
        P(("seq", "head"), None),
        P(("seq", "head"), None),
        P(("seq", "head"), None),
        P(("seq", "head"), None),
        P(),
        P(),
        P(),
    )
    return jax.shard_map(
        on_device,
        mesh=mesh,
        in_specs=placed,
        out_specs=(P(("seq", "head"), None), P(("seq", "head"), None), P(("seq", "head"), None)),
        check_vma=False,
    )
```

profile of v0, /device:TPU:24, one launch (start us, length us, event | category | flops | bytes accessed | tf_op | source)
XLA Modules:
  0.0 595.5 jit_solution(14810625607046341303)
XLA Ops:
  8.1 29.8 %all_to_all.149 = bf16[32,16,128]{2,0,1:T(8,128)(2,1)} all-to-all(bf16[32,16,128]{2,0,1:T(8,128)(2,1)S(1)} %copy_bitcast_fusion.7), channel_id=1, replica_groups=mesh['seq'=32,'head'=16] {'head'}, dimensions={1} | all-to-all | bytes 262144 | tf_op jit(solution)/shard_map/all_to_all | solution.py:25
  38.9 17.8 %all_to_all.150 = bf16[32,16,128]{2,0,1:T(8,128)(2,1)} all-to-all(bf16[32,16,128]{2,0,1:T(8,128)(2,1)S(1)} %copy_bitcast_fusion.5), channel_id=1, replica_groups=mesh['seq'=32,'head'=16] {'head'}, dimensions={1} | all-to-all | bytes 262144 | tf_op jit(solution)/shard_map/all_to_all | solution.py:29
  58.3 4.2 all-to-all-start.1
  71.6 4.9 all-to-all-done.1
  76.4 7.0 %all-to-all-start.6 = ((bf16[32,16,128]{2,0,1:T(8,128)(2,1)}), bf16[32,16,128]{2,0,1:T(8,128)(2,1)S(1)}, u32[]{:S(2)}, u32[]{:S(2)}) async-start(bf16[32,16,128]{2,0,1:T(8,128)(2,1)} %copy_bitcast_fusion.3), calls=%async_computation.6 | async-start | bytes 262144 | tf_op jit(solution)/shard_map/all_to_all | solution.py:28
  83.5 8.5 %all-gather.5.cloned.1.call-done = bf16[16384,128]{1,0:T(8,128)(2,1)} async-done(((bf16[512,128]{1,0:T(8,128)(2,1)}), bf16[16384,128]{1,0:T(8,128)(2,1)}) %all-gather.5.cloned.1.call-update) | async-done | bytes 4194320 | tf_op jit(solution)/shard_map/all_gather | solution.py:54
  92.0 77.0 %while.30 = (s32[]{:T(128)}, f32[32,1,512]{2,0,1:T(8,128)S(1)}, f32[32,1,512]{2,0,1:T(8,128)S(1)}, s32[]{:T(128)}, s32[32]{0:T(128)}, /*index=5*/s32[]{:T(128)},...) while((s32[]{:T(128)}, f32[32,1,512]{2,0,1:T(8,128)S(1)}, ...), condition=%wide.region_8.9_spmd.clone, body=%wide.region_3.8_spmd.clone.sunk | while | flops 140246032 | bytes 5939457 | solution.py:79
  94.1 2.8 gather_fusion.1
  102.6 2.8 gather_fusion.1
  111.1 2.9 gather_fusion.1
  119.7 2.8 gather_fusion.1
  128.3 2.8 gather_fusion.1
  136.8 2.8 gather_fusion.1
  145.3 3.0 gather_fusion.1
  154.0 2.9 gather_fusion.1
  162.5 2.8 gather_fusion.1
  169.7 22.3 %all-to-all-start.3 = ((f32[32,1,512]{2,1,0:T(1,128)}), f32[32,1,512]{2,1,0:T(1,128)S(1)}, u32[]{:S(2)}, u32[]{:S(2)}) async-start(f32[32,1,512]{2,1,0:T(1,128)} %copy.70), calls=%async_computation.3 | async-start | bytes 131072 | tf_op jit(solution)/shard_map/all_to_all | solution.py:82
  192.7 5.0 all-to-all-done.3
  197.7 5.6 all-to-all-start.2
  204.0 5.1 all-to-all-done.2
  209.1 12.3 %all-to-all-start.5 = ((bf16[32,16,128]{2,0,1:T(8,128)(2,1)}), bf16[32,16,128]{2,0,1:T(8,128)(2,1)S(1)}, u32[]{:S(2)}, u32[]{:S(2)}) async-start(bf16[32,16,128]{2,0,1:T(8,128)(2,1)} %copy_bitcast_fusion.4), calls=%async_computation.5 | async-start | bytes 262144 | tf_op jit(solution)/shard_map/all_to_all | solution.py:27
  221.7 23.1 %all_gather.15 = f32[32,1,512]{2,1,0:T(1,128)S(1)} all-gather(f32[1,1,512]{2,1,0:T(1,128)S(1)} %transpose.44), channel_id=1, replica_groups=mesh['seq'=32,'head'=16] {'seq'}, dimensions={0}, use_global_device_ids=true | all-gather | bytes 67584 | tf_op jit(solution)/shard_map/all_gather | solution.py:96
  245.0 22.3 %all-gather.1 = f32[32,1,512]{2,1,0:T(1,128)S(1)} all-gather(f32[1,1,512]{2,1,0:T(1,128)S(1)} %bitcast.195), channel_id=2, replica_groups=mesh['seq'=32,'head'=16] {'seq'}, dimensions={0}, use_global_device_ids=true | all-gather | bytes 67584 | tf_op jit(solution)/shard_map/all_gather | solution.py:95
  267.4 2.9 broadcast_in_dim.42
  270.3 161.1 %while.31 = (s32[]{:T(128)}, f32[1,512,1,128]{3,1,2,0:T(8,128)S(1)}, f32[1,512,1,128]{3,1,2,0:T(8,128)S(1)}, bf16[32,512,128]{2,1,0:T(8,128)(2,1)}, s32[]{:T(128...) while((s32[]{:T(128)}, ...), condition=%wide.region_16.17_spmd.clone, body=%wide.region_12.16_spmd.clone.sunk | while | flops 677250048 | bytes 19821064 | solution.py:133
  274.1 2.8 gather_fusion.6
  276.9 2.8 gather_fusion.3
  286.0 2.3 scatter_fusion.4
  292.0 2.8 gather_fusion.6
  294.8 2.8 gather_fusion.3
  303.9 2.3 scatter_fusion.4
  309.9 2.8 gather_fusion.6
  312.7 2.8 gather_fusion.3
  315.6 1.7 exponential_select_fusion.2
  321.8 2.2 scatter_fusion.4
  327.8 2.8 gather_fusion.6
  330.6 2.8 gather_fusion.3
  333.5 1.7 exponential_select_fusion.2
  339.7 2.2 scatter_fusion.4
  345.7 2.8 gather_fusion.6
  348.5 2.8 gather_fusion.3
  357.5 2.2 scatter_fusion.4
  363.6 2.8 gather_fusion.6
  366.4 2.8 gather_fusion.3
  369.2 1.7 exponential_select_fusion.2
  375.4 2.2 scatter_fusion.4
  381.5 2.8 gather_fusion.6
  384.3 2.8 gather_fusion.3
  393.3 2.2 scatter_fusion.4
  399.4 2.8 gather_fusion.6
  402.1 2.8 gather_fusion.3
  405.0 1.7 exponential_select_fusion.2
  411.2 2.2 scatter_fusion.4
  417.2 2.8 gather_fusion.6
  420.0 2.8 gather_fusion.3
  429.1 2.3 scatter_fusion.4
  431.4 24.9 %all_to_all.151 = bf16[16,32,128]{2,1,0:T(8,128)(2,1)S(1)} all-to-all(bf16[16,32,128]{2,1,0:T(8,128)(2,1)S(1)} %bitcast.191), channel_id=1, replica_groups=mesh['seq'=32,'head'=16] {'head'}, dimensions={0} | all-to-all | bytes 262144 | tf_op jit(solution)/shard_map/all_to_all | solution.py:141
  456.3 42.2 %all-to-all-start.7 = ((bf16[32,512,128]{2,1,0:T(8,128)(2,1)}), bf16[32,512,128]{2,1,0:T(8,128)(2,1)}, u32[]{:S(2)}, u32[]{:S(2)}) async-start(bf16[32,512,128]{2,1,0:T(8,128)(2,1)} %get-tuple-element.228), calls=%async_computation.7 | async-start | bytes 8388608 | tf_op jit(solution)/shard_map/all_to_all | solution.py:134
  499.2 50.2 %all-to-all-done.7 = bf16[32,512,128]{2,1,0:T(8,128)(2,1)} async-done(((bf16[32,512,128]{2,1,0:T(8,128)(2,1)}), bf16[32,512,128]{2,1,0:T(8,128)(2,1)}, u32[]{:S(2)}, u32[]{:S(2)}) %all-to-all-start.7) | async-done | bytes 4194336 | tf_op jit(solution)/shard_map/all_to_all | solution.py:134
  549.4 4.0 all-to-all-start.10
  553.4 3.5 reduce_sum.61
  556.9 9.8 %all-to-all-done.10 = bf16[16,32,128]{2,1,0:T(8,128)(2,1)S(1)} async-done(((bf16[16,32,128]{2,1,0:T(8,128)(2,1)}), bf16[16,32,128]{2,1,0:T(8,128)(2,1)S(1)}, u32[]{:S(2)}, u32[]{:S(2)}) %all-to-all-start.10) | async-done | bytes 131104 | tf_op jit(solution)/shard_map/all_to_all | solution.py:142
  566.8 6.5 %all-to-all-start.8 = ((bf16[16,32,128]{2,1,0:T(8,128)(2,1)}), bf16[16,32,128]{2,1,0:T(8,128)(2,1)S(1)}, u32[]{:S(2)}, u32[]{:S(2)}) async-start(bf16[16,32,128]{2,1,0:T(8,128)(2,1)} %bitcast.14), calls=%async_computation.8 | async-start | bytes 262144 | tf_op jit(solution)/shard_map/all_to_all | solution.py:140
  574.6 13.4 %all-to-all-done.8 = bf16[16,32,128]{2,1,0:T(8,128)(2,1)S(1)} async-done(((bf16[16,32,128]{2,1,0:T(8,128)(2,1)}), bf16[16,32,128]{2,1,0:T(8,128)(2,1)S(1)}, u32[]{:S(2)}, u32[]{:S(2)}) %all-to-all-start.8) | async-done | bytes 131104 | tf_op jit(solution)/shard_map/all_to_all | solution.py:140
  (319 shorter events, 151.2 us)
Async XLA Ops:
  7.2 0.9 copy-start
  7.2 63.1 %copy-start.5 = (s32[32]{0:T(128)S(1)}, s32[32]{0:T(128)}, u32[]{:S(2)}) copy-start(s32[32]{0:T(128)} %param.19) | copy-start | bytes 388
  7.2 58.0 %copy-start.1 = (s32[32]{0:T(128)S(1)}, s32[32]{0:T(128)}, u32[]{:S(2)}) copy-start(s32[32]{0:T(128)} %param.18) | copy-start | bytes 388
  7.2 63.7 %copy-start.3 = (bf16[32,2048]{1,0:T(8,128)(2,1)S(1)}, bf16[32,2048]{1,0:T(8,128)(2,1)}, u32[]{:S(2)}) copy-start(bf16[32,2048]{1,0:T(8,128)(2,1)} %param.15) | copy-start | bytes 393220
  7.2 84.7 %all-gather.5.cloned.1.call-start = ((), (), s32[]{:S(2)}) async-start(), calls=%async_computation.11 | async-start | bytes 4325376 | tf_op jit(solution)/shard_map/all_gather | solution.py:54
  37.9 229.4 %all-gather.7.cloned.1.call-start = ((), (), s32[]{:S(2)}) async-start(), calls=%async_computation.12 | async-start | bytes 4325376 | tf_op jit(solution)/shard_map/all_gather | solution.py:93
  58.3 18.1 %all-to-all-start.1 = ((bf16[32,16,128]{2,0,1:T(8,128)(2,1)}), bf16[32,16,128]{2,0,1:T(8,128)(2,1)}, u32[]{:S(2)}, u32[]{:S(2)}) async-start(bf16[32,16,128]{2,0,1:T(8,128)(2,1)} %copy_bitcast_fusion.6), calls=%async_computation.1 | async-start | bytes 262144 | tf_op jit(solution)/shard_map/all_to_all | solution.py:26
  76.4 93.3 %all-to-all-start.6 = ((bf16[32,16,128]{2,0,1:T(8,128)(2,1)}), bf16[32,16,128]{2,0,1:T(8,128)(2,1)S(1)}, u32[]{:S(2)}, u32[]{:S(2)}) async-start(bf16[32,16,128]{2,0,1:T(8,128)(2,1)} %copy_bitcast_fusion.3), calls=%async_computation.6 | async-start | bytes 262144 | tf_op jit(solution)/shard_map/all_to_all | solution.py:28
  92.0 111.4 %copy-start.4 = (bf16[32,2048]{1,0:T(8,128)(2,1)S(1)}, bf16[32,2048]{1,0:T(8,128)(2,1)}, u32[]{:S(2)}) copy-start(bf16[32,2048]{1,0:T(8,128)(2,1)} %param.14) | copy-start | bytes 393220
  92.0 129.5 %copy-start.2 = (bf16[32,16,128]{2,0,1:T(8,128)(2,1)S(1)}, bf16[32,16,128]{2,0,1:T(8,128)(2,1)}, u32[]{:S(2)}) copy-start(bf16[32,16,128]{2,0,1:T(8,128)(2,1)} %all_to_all.150) | copy-start | bytes 393220
  169.7 28.0 %all-to-all-start.3 = ((f32[32,1,512]{2,1,0:T(1,128)}), f32[32,1,512]{2,1,0:T(1,128)S(1)}, u32[]{:S(2)}, u32[]{:S(2)}) async-start(f32[32,1,512]{2,1,0:T(1,128)} %copy.70), calls=%async_computation.3 | async-start | bytes 131072 | tf_op jit(solution)/shard_map/all_to_all | solution.py:82
  197.7 11.4 %all-to-all-start.2 = ((f32[32,1,512]{2,1,0:T(1,128)}), f32[32,1,512]{2,1,0:T(1,128)S(1)}, u32[]{:S(2)}, u32[]{:S(2)}) async-start(f32[32,1,512]{2,1,0:T(1,128)} %copy.69), calls=%async_computation.2 | async-start | bytes 131072 | tf_op jit(solution)/shard_map/all_to_all | solution.py:81
  209.1 58.2 %all-to-all-start.5 = ((bf16[32,16,128]{2,0,1:T(8,128)(2,1)}), bf16[32,16,128]{2,0,1:T(8,128)(2,1)S(1)}, u32[]{:S(2)}, u32[]{:S(2)}) async-start(bf16[32,16,128]{2,0,1:T(8,128)(2,1)} %copy_bitcast_fusion.4), calls=%async_computation.5 | async-start | bytes 262144 | tf_op jit(solution)/shard_map/all_to_all | solution.py:27
  456.3 93.1 %all-to-all-start.7 = ((bf16[32,512,128]{2,1,0:T(8,128)(2,1)}), bf16[32,512,128]{2,1,0:T(8,128)(2,1)}, u32[]{:S(2)}, u32[]{:S(2)}) async-start(bf16[32,512,128]{2,1,0:T(8,128)(2,1)} %get-tuple-element.228), calls=%async_computation.7 | async-start | bytes 8388608 | tf_op jit(solution)/shard_map/all_to_all | solution.py:134
  549.4 17.3 %all-to-all-start.10 = ((bf16[16,32,128]{2,1,0:T(8,128)(2,1)}), bf16[16,32,128]{2,1,0:T(8,128)(2,1)S(1)}, u32[]{:S(2)}, u32[]{:S(2)}) async-start(bf16[16,32,128]{2,1,0:T(8,128)(2,1)} %bitcast.18), calls=%async_computation.10 | async-start | bytes 262144 | tf_op jit(solution)/shard_map/all_to_all | solution.py:142
  566.8 21.2 %all-to-all-start.8 = ((bf16[16,32,128]{2,1,0:T(8,128)(2,1)}), bf16[16,32,128]{2,1,0:T(8,128)(2,1)S(1)}, u32[]{:S(2)}, u32[]{:S(2)}) async-start(bf16[16,32,128]{2,1,0:T(8,128)(2,1)} %bitcast.14), calls=%async_computation.8 | async-start | bytes 262144 | tf_op jit(solution)/shard_map/all_to_all | solution.py:140
Sparse Core Ops, SparseCore 0:
  38.1 53.8 all-gather.4
  95.1 60.8 all-gather.6
where the time goes:
time: 601 us; the launch traced here: 596 us
  local copies, waits for them, and re-layouts  153 us (25%)
  blocking collectives  118 us (20%)
  starting transfers between devices  104 us (17%)
  waiting for transfers between devices  96.9 us (16%)
  other arithmetic  55.4 us (9%)
  matrix products  51.3 us (9%)
  between operations  14.9 us (2%)
    all_to_all x1, waiting for transfers between devices, on_device(): lax.all_to_all(query_parts, 'seq', split_axis=0, concat_axis=0, tiled=True)  50.2 us
    all_to_all x1, starting transfers between devices, on_device(): lax.all_to_all(query_parts, 'seq', split_axis=0, concat_axis=0, tiled=True)  42.2 us
    all_to_all x1, blocking collectives, on_device(): lax.all_to_all(query_data, 'head', split_axis=1, concat_axis=0, tiled=True)  29.8 us
    dot_general x18, matrix products, scores_for(): jnp.einsum('grhd,gchd->ghrc', queries, keys_sel, preferred_element_type=j...  29 us
    gather x9, local copies, waits for them, and re-layouts, first_pass(): scores = scores_for(query_slots[slots], keys_own[slot_block[slots]], scale)  25.4 us
    gather x9, local copies, waits for them, and re-layouts, second_pass(): queries = query_slots[slots]  25.1 us
    gather x9, local copies, waits for them, and re-layouts, second_pass(): grads = grad_slots[slots]  25 us
    all_to_all x1, blocking collectives, on_device(): lax.all_to_all(key_grad, 'head', split_axis=0, concat_axis=1, tiled=True)  24.9 us
  transfers between devices with their start and end apart: 10, of which 7 were waited for; matrix products, arithmetic and copies ran while one was open for 16% of the time, Pallas kernels for 0%

commit v1 on v0

v1 whole, which is shorter than its diff:
```python
import math

import jax
import jax.numpy as jnp
from jax import lax
from jax.experimental import pallas as pl
from jax.experimental.pallas import tpu as pltpu
from jax.sharding import Mesh, PartitionSpec as P

HD = 128
BLK = 512
HEADS = 16
ROWS = BLK // HEADS
NX, NY, NC = 4, 4, 2
NQ = NY * NC
NK = NX
NPAIR = NQ * NK
QD_ROWS = 2 * BLK + 16
CHUNK = 256
SCALE = 1.0 / math.sqrt(HD)
SCALE2 = SCALE * math.log2(math.e)
LOW = -1e30
VMEM = 48 * 1024 * 1024


def dot(a, b, contract):
    return lax.dot_general(a, b, ((contract[:1], contract[1:]), ((), ())), preferred_element_type=jnp.float32)


def query_place(code, meta):
    slot = code // NK
    return ((meta[1] - slot % NY) & (NY - 1)) * NC + (meta[2] ^ (slot // NY))


def probs_kernel(pairs, meta, qd, kv, probs, tops, stats):
    t = pl.program_id(0)
    code = pairs[t]
    place = query_place(code, meta)

    @pl.when(t == 0)
    def _():
        stats[:, 0, :] = jnp.full((NQ, BLK), LOW, jnp.float32)
        stats[:, 1, :] = jnp.zeros((NQ, BLK), jnp.float32)

    def visit(diagonal):
        keys = kv[code % NK, :BLK, :]
        for start in range(0, BLK, CHUNK):
            part = slice(start, start + CHUNK)
            scores = dot(keys, qd[0, part, :], (1, 1))
            if diagonal:
                key_row = lax.broadcasted_iota(jnp.int32, scores.shape, 0)
                query_row = lax.broadcasted_iota(jnp.int32, scores.shape, 1) + start
                scores = jnp.where(key_row <= query_row, scores, LOW)
            top = jnp.max(scores, axis=0, keepdims=True) * SCALE2
            values = jnp.exp2(scores * SCALE2 - top)
            total = jnp.sum(values, axis=0, keepdims=True)
            probs[0, :, part] = values.astype(jnp.bfloat16)
            tops[0, :, part] = top
            old_top, old_total = stats[place, 0:1, part], stats[place, 1:2, part]
            new_top = jnp.maximum(old_top, top)
            stats[place, 0:1, part] = new_top
            stats[place, 1:2, part] = old_total * jnp.exp2(old_top - new_top) + total * jnp.exp2(top - new_top)

    @pl.when(t == 0)
    def _():
        visit(True)

    @pl.when((t != 0) & (t < meta[0]))
    def _():
        visit(False)


def dscore_kernel(pairs, meta, qd, kv, probs, tops, stats, dscore, dquery, keys_t, total):
    t = pl.program_id(0)
    code = pairs[t]
    place = query_place(code, meta)
    key = code % NK

    @pl.when(t == 0)
    def _():
        total[...] = jnp.zeros_like(total)
        for i in range(NK):
            keys_t[i] = jnp.transpose(kv[i, :BLK, :])

    @pl.when(t < meta[0])
    def _():
        pieces = qd[0, 2 * BLK :, :].astype(jnp.float32)
        row_dot = pieces[0:4] + pieces[4:8] + pieces[8:12]
        row_dot = jnp.concatenate([row_dot[i : i + 1] for i in range(4)], axis=1)
        weight = jnp.exp2(tops[0] - stats[place, 0:1, :])
        values = kv[key, BLK:, :]
        for start in range(0, BLK, CHUNK):
            part = slice(start, start + CHUNK)
            dprob = dot(values, qd[0, BLK + start : BLK + start + CHUNK, :], (1, 1))
            low = (probs[0, :, part].astype(jnp.float32) * (dprob - row_dot[:, part])).astype(jnp.bfloat16)
            dscore[0, :, part] = low
            total[place, :, part] += dot(keys_t[key], low, (1, 0)) * weight[:, part]

    @pl.when(t == meta[0] - 1)
    def _():
        for i in range(NQ):
            dquery[i] = jnp.transpose(total[i]).astype(jnp.bfloat16)


def log_norms(stats_all):
    tops, sums = stats_all[:, :, 0, :], stats_all[:, :, 1, :]
    top = jnp.max(tops, axis=0)
    return top + jnp.log2(jnp.sum(sums * jnp.exp2(tops - top[None]), axis=0))


def key_kernel(pairs, meta, qd, probs, dscore, tops, stats_all, out, norms, total):
    t = pl.program_id(0)
    code = pairs[t]
    place = query_place(code, meta)
    key = code % NK

    @pl.when(t == 0)
    def _():
        total[...] = jnp.zeros_like(total)
        norms[:, 0, :] = log_norms(stats_all[...])

    @pl.when(t < meta[0])
    def _():
        weight = jnp.exp2(tops[0] - norms[place])
        weight = jnp.transpose(jnp.broadcast_to(weight, (HD, BLK)))
        queries = (qd[0, :BLK, :].astype(jnp.float32) * (weight * SCALE)).astype(jnp.bfloat16)
        grads = (qd[0, BLK : 2 * BLK, :].astype(jnp.float32) * weight).astype(jnp.bfloat16)
        total[key, 0] += dot(dscore[0], queries, (1, 0))
        total[key, 1] += dot(probs[0], grads, (1, 0))

    @pl.when(t == meta[0] - 1)
    def _():
        out[...] = total[...].astype(jnp.bfloat16)


def finish_kernel(meta, dquery, stats_all, own, first, second, third, out):
    place = meta[1] * NC + meta[2]
    tops, sums = stats_all[:, place, 0, :], stats_all[:, place, 1, :]
    top = jnp.max(tops, axis=0, keepdims=True)
    norm = top + jnp.log2(jnp.sum(sums * jnp.exp2(tops - top), axis=0, keepdims=True))
    weight = jnp.transpose(jnp.exp2(tops - norm) * SCALE)
    query_grad = dquery[0].astype(jnp.float32) * weight[:, 0:1]
    for i in range(1, NQ):
        query_grad += dquery[i].astype(jnp.float32) * weight[:, i : i + 1]
    out[:, 0:ROWS, :] = query_grad.astype(jnp.bfloat16).reshape(HEADS, ROWS, HD)
    for i in range(2):
        grad = (own[0, i].astype(jnp.float32) + first[i].astype(jnp.float32)) + (
            second[i].astype(jnp.float32) + third[i].astype(jnp.float32)
        )
        out[:, (i + 1) * ROWS : (i + 2) * ROWS, :] = grad.astype(jnp.bfloat16).reshape(HEADS, ROWS, HD)


def params():
    return pltpu.CompilerParams(vmem_limit_bytes=VMEM)


def by_query(rows=QD_ROWS):
    return pl.BlockSpec((1, rows, HD), lambda t, pairs, meta: (pairs[t] // NK, 0, 0))


def by_pair(*shape):
    return pl.BlockSpec((1, *shape), lambda t, pairs, meta: (jnp.minimum(t, meta[0] - 1), 0, 0))


def whole(*shape):
    return pl.BlockSpec(shape, lambda *_: (0,) * len(shape))


def over_pairs(kernel, pairs, meta, operands, in_specs, out_specs, out_shape, scratch=()):
    return pl.pallas_call(
        kernel,
        grid_spec=pltpu.PrefetchScalarGridSpec(
            num_scalar_prefetch=2,
            grid=(NPAIR,),
            in_specs=in_specs,
            out_specs=out_specs,
            scratch_shapes=scratch,
        ),
        out_shape=out_shape,
        compiler_params=params(),
    )(pairs, meta, *operands)


def pair_list(key_lists, key_counts, block_order, x, y, c):
    slot = jnp.arange(NQ, dtype=jnp.int32)
    query_at = x * NQ + ((y - slot % NY) % NY) * NC + (c ^ (slot // NY))
    key_at = ((x - jnp.arange(NK, dtype=jnp.int32)) % NX) * NQ + y * NC + c
    query_blocks, key_blocks = block_order[query_at], block_order[key_at]
    lists, counts = key_lists[query_blocks], key_counts[query_blocks]
    used = jnp.arange(key_lists.shape[1], dtype=jnp.int32)[None, :] < counts[:, None]
    named = jnp.any((lists[:, None, :] == key_blocks[None, :, None]) & used[:, None, :], axis=2)
    named = named.reshape(NPAIR)
    code = jnp.arange(NPAIR, dtype=jnp.int32)
    rank = jnp.sum((code[None, :] < code[:, None]) & named[None, :], axis=1)
    count = jnp.sum(named.astype(jnp.int32))
    wanted = jnp.minimum(code, count - 1)
    pairs = jnp.sum(jnp.where(named[None, :] & (rank[None, :] == wanted[:, None]), code[None, :], 0), axis=1)
    return pairs.astype(jnp.int32), count


def shifted(array, axis, by, size):
    return lax.ppermute(array, axis, [(i, (i + by) % size) for i in range(size)])


def on_device(query_data, key_data, value_data, output_data, output_grad, key_lists, key_counts, block_order):
    x, y, c = lax.axis_index("x"), lax.axis_index("y"), lax.axis_index("c")

    def heads(array):
        return jnp.transpose(array.reshape(ROWS, HEADS, HD), (1, 0, 2))

    products = output_grad.astype(jnp.float32) * output_data.astype(jnp.float32)
    row_dot = jnp.transpose(jnp.sum(products.reshape(ROWS, HEADS, HD), axis=2))
    high = lax.reduce_precision(row_dot, 8, 7)
    middle = lax.reduce_precision(row_dot - high, 8, 7)
    pieces = jnp.stack([high, middle, row_dot - high - middle], axis=1).astype(jnp.bfloat16)
    pieces = jnp.pad(pieces, ((0, 0), (0, 13), (0, HD - ROWS)))
    packed = jnp.concatenate(
        [heads(query_data), heads(output_grad), heads(key_data), heads(value_data), pieces], axis=1
    )
    packed = lax.all_to_all(packed, "h", 0, 0, tiled=True)

    def rows(i):
        return packed[:, i * ROWS : (i + 1) * ROWS, :].reshape(BLK, HD)

    pieces = jnp.transpose(packed[:, 4 * ROWS : 4 * ROWS + 3, :ROWS], (1, 0, 2)).reshape(12, HD)
    qd = jnp.concatenate([rows(0), rows(1), pieces, jnp.zeros((4, HD), jnp.bfloat16)], axis=0)
    kv = jnp.concatenate([rows(2), rows(3)], axis=0)

    pairs, count = pair_list(key_lists, key_counts, block_order, x, y, c)
    meta = jnp.stack([count, y, c]).astype(jnp.int32)

    kv_all = jnp.stack([kv] + [shifted(kv, "x", i, NX) for i in range(1, NX)])
    qd_own = jnp.stack([qd] + [shifted(qd, "y", i, NY) for i in range(1, NY)])
    qd_all = jnp.concatenate([qd_own, shifted(qd_own, "c", 1, NC)], axis=0)

    bf16, f32 = jnp.bfloat16, jnp.float32
    shape = jax.ShapeDtypeStruct
    square, line = shape((NPAIR, BLK, BLK), bf16), shape((NPAIR, 1, BLK), f32)
    probs, tops, stats = over_pairs(
        probs_kernel, pairs, meta, (qd_all, kv_all),
        [by_query(), whole(NK, 2 * BLK, HD)],
        [by_pair(BLK, BLK), by_pair(1, BLK), whole(NQ, 2, BLK)],
        [square, line, shape((NQ, 2, BLK), f32)],
    )
    stats_all = lax.all_to_all(
        jnp.broadcast_to(stats[None], (NQ, NQ, 2, BLK)), ("y", "c"), 0, 0, tiled=True
    )
    dscore, dquery = over_pairs(
        dscore_kernel, pairs, meta, (qd_all, kv_all, probs, tops, stats),
        [by_query(), whole(NK, 2 * BLK, HD), by_pair(BLK, BLK), by_pair(1, BLK), whole(NQ, 2, BLK)],
        [by_pair(BLK, BLK), whole(NQ, BLK, HD)],
        [square, shape((NQ, BLK, HD), bf16)],
        [pltpu.VMEM((NK, HD, BLK), bf16), pltpu.VMEM((NQ, HD, BLK), f32)],
    )
    dquery = lax.all_to_all(dquery, ("y", "c"), 0, 0, tiled=True)
    dkv = over_pairs(
        key_kernel, pairs, meta, (qd_all, probs, dscore, tops, stats_all),
        [by_query(), by_pair(BLK, BLK), by_pair(BLK, BLK), by_pair(1, BLK), whole(NQ, NQ, 2, BLK)],
        whole(NK, 2, BLK, HD),
        shape((NK, 2, BLK, HD), bf16),
        [pltpu.VMEM((NQ, 1, BLK), f32), pltpu.VMEM((NK, 2, BLK, HD), f32)],
    )
    arrived = [shifted(dkv[i], "x", -i, NX) for i in range(1, NX)]

    part = whole(2, BLK, HD)
    grads = pl.pallas_call(
        finish_kernel,
        grid_spec=pltpu.PrefetchScalarGridSpec(
            num_scalar_prefetch=1,
            grid=(1,),
            in_specs=[whole(NQ, BLK, HD), whole(NQ, NQ, 2, BLK), whole(1, 2, BLK, HD), part, part, part],
            out_specs=whole(HEADS, 3 * ROWS, HD),
        ),
        out_shape=shape((HEADS, 3 * ROWS, HD), bf16),
        compiler_params=params(),
    )(meta, dquery, stats_all, dkv, *arrived)
    grads = lax.all_to_all(grads, "h", 0, 0, tiled=True)

    def tokens(i):
        part = grads[:, i * ROWS : (i + 1) * ROWS, :]
        return jnp.transpose(part, (1, 0, 2)).reshape(ROWS, HEADS * HD)

    return tokens(0), tokens(1), tokens(2)


def solution(mesh):
    wide = Mesh(mesh.devices.reshape(NX, NY, NC, HEADS), ("x", "y", "c", "h"))
    split = P(("x", "y", "c", "h"), None)
    return jax.shard_map(
        on_device,
        mesh=wide,
        in_specs=(split,) * 5 + (P(),) * 3,
        out_specs=(split,) * 3,
        check_vma=False,
    )
```

time: 601 us -> 207 us (0.34)
  the two profiles are of different devices: /device:TPU:24 before, /device:TPU:16 now
where the time goes in v1:
time: 207 us; the launch traced here: 205 us
  starting transfers between devices  62.9 us (30%)
  waiting for transfers between devices  47.1 us (23%)
  Pallas kernels  41.4 us (20%)
  blocking collectives  34.8 us (17%)
  local copies, waits for them, and re-layouts  12.1 us (6%)
  other arithmetic  5.21 us (3%)
    pallas_call x3, Pallas kernels, over_pairs(): pl.pallas_call(kernel, grid_spec=pltpu.PrefetchScalarGridSpec(num_scalar_...  38.6 us
    all_to_all x1, blocking collectives, on_device(): grads = lax.all_to_all(grads, 'h', 0, 0, tiled=True)  34.8 us
    ppermute x10, starting transfers between devices, shifted(): lax.ppermute(array, axis, [(i, (i + by) % size) for i in range(size)])  28.5 us
    all_to_all x1, waiting for transfers between devices, on_device(): packed = lax.all_to_all(packed, 'h', 0, 0, tiled=True)  26 us
    ppermute x10, waiting for transfers between devices, shifted(): lax.ppermute(array, axis, [(i, (i + by) % size) for i in range(size)])  21.1 us
    all_to_all x1, starting transfers between devices, on_device(): packed = lax.all_to_all(packed, 'h', 0, 0, tiled=True)  15.2 us
    all_to_all x1, starting transfers between devices, on_device(): dquery = lax.all_to_all(dquery, ('y', 'c'), 0, 0, tiled=True)  9.85 us
    all_to_all x1, starting transfers between devices, on_device(): lax.all_to_all(jnp.broadcast_to(stats[None], (NQ, NQ, 2, BLK)), ('y', 'c'...  9.38 us
  transfers between devices with their start and end apart: 13, of which 7 were waited for; matrix products, arithmetic and copies ran while one was open for 3% of the time, Pallas kernels for 14%

profile of v1, /device:TPU:16, one launch (start us, length us, event | category | flops | bytes accessed | tf_op | source)
XLA Modules:
  0.0 205.2 jit_solution(7229603107659472323)
XLA Ops:
  0.6 0.0 copy-start
  0.6 0.9 copy.49
  1.6 0.9 copy.50
  2.5 0.9 copy.51
  3.5 0.9 copy.52
  4.4 1.0 multiply_bitcast_fusion
  5.4 0.0 copy-start.4
  5.5 0.1 reduce_sum.39
  5.6 0.1 copy.45
  5.8 1.0 copy.40
  6.8 15.2 %all-to-all-start = ((bf16[16,144,128]{2,1,0:T(8,128)(2,1)}), bf16[16,144,128]{2,1,0:T(8,128)(2,1)S(1)}, u32[]{:S(2)}, u32[]{:S(2)}) async-start(bf16[16,144,128]{2,1,0:T(8,128)(2,1)} %copy.40), calls=%async_computation | async-start | bytes 1179648 | tf_op jit(solution)/shard_map/all_to_all | solution.py:220
  22.0 0.1 copy.37
  22.1 0.6 gather_fusion
  22.8 0.6 gather_fusion.2
  23.5 0.6 gather_fusion.1
  24.0 0.6 gather_fusion.3
  24.7 0.1 iota_compare_fusion.1
  24.8 0.2 and_reduce_fusion
  25.0 0.1 copy.38
  25.1 0.1 and.101
  25.2 0.6 convert_reduce_fusion.1
  26.5 0.1 convert_reduce_fusion
  26.6 0.2 select_reduce_fusion.pairs
  26.8 26.0 %all-to-all-done = bf16[16,144,128]{2,1,0:T(8,128)(2,1)S(1)} async-done(((bf16[16,144,128]{2,1,0:T(8,128)(2,1)}), bf16[16,144,128]{2,1,0:T(8,128)(2,1)S(1)}, u32[]{:S(2)}, u32[]{:S(2)}) %all-to-all-start) | async-done | bytes 589856 | tf_op jit(solution)/shard_map/all_to_all | solution.py:220
  52.9 0.7 fusion.18
  53.6 4.7 %collective-permute-start.6 = (bf16[1024,128]{1,0:T(8,128)(2,1)S(1)}, bf16[1024,128]{1,0:T(8,128)(2,1)S(1)}, u32[]{:S(2)}, u32[]{:S(2)}) collective-permute-start(bf16[1024,128]{1,0:T(8,128)(2,1)S(1)} %get-tuple-element.24), channel_id=1, source_target_pairs={{0,384},{128,0},{256,128},{384,256},{1,385},{129,1},{257,129},{385... | collective-permute-start | bytes 786440 | tf_op jit(solution)/shard_map/ppermute | solution.py:202
  58.3 0.7 pad_add_fusion.meta
  59.0 0.1 reshape.256
  59.1 0.1 concatenate.14
  59.2 3.2 %collective-permute-start = (bf16[1040,128]{1,0:T(8,128)(2,1)S(1)}, bf16[1040,128]{1,0:T(8,128)(2,1)S(1)}, u32[]{:S(2)}, u32[]{:S(2)}) collective-permute-start(bf16[1040,128]{1,0:T(8,128)(2,1)S(1)} %concatenate.14), channel_id=1, source_target_pairs={{0,32},{32,64},{64,96},{96,0},{1,33},{33,65},{65,97},{97,1},{2,34}... | collective-permute-start | bytes 798728 | tf_op jit(solution)/shard_map/ppermute | solution.py:202
  62.4 2.5 %collective-permute-start.1 = (bf16[1040,128]{1,0:T(8,128)(2,1)S(1)}, bf16[1040,128]{1,0:T(8,128)(2,1)S(1)}, u32[]{:S(2)}, u32[]{:S(2)}) collective-permute-start(bf16[1040,128]{1,0:T(8,128)(2,1)S(1)} %concatenate.14), channel_id=1, source_target_pairs={{0,64},{32,96},{64,0},{96,32},{1,65},{33,97},{65,1},{97,33},{2,66}... | collective-permute-start | bytes 798728 | tf_op jit(solution)/shard_map/ppermute | solution.py:202
  64.9 3.0 %collective-permute-start.2 = (bf16[1040,128]{1,0:T(8,128)(2,1)S(1)}, bf16[1040,128]{1,0:T(8,128)(2,1)S(1)}, u32[]{:S(2)}, u32[]{:S(2)}) collective-permute-start(bf16[1040,128]{1,0:T(8,128)(2,1)S(1)} %concatenate.14), channel_id=1, source_target_pairs={{0,96},{32,0},{64,32},{96,64},{1,97},{33,1},{65,33},{97,65},{2,98}... | collective-permute-start | bytes 798728 | tf_op jit(solution)/shard_map/ppermute | solution.py:202
  67.9 2.7 %collective-permute-start.5 = (bf16[1024,128]{1,0:T(8,128)(2,1)S(1)}, bf16[1024,128]{1,0:T(8,128)(2,1)S(1)}, u32[]{:S(2)}, u32[]{:S(2)}) collective-permute-start(bf16[1024,128]{1,0:T(8,128)(2,1)S(1)} %get-tuple-element.24), channel_id=1, source_target_pairs={{0,256},{128,384},{256,0},{384,128},{1,257},{129,385},{257,1},{385... | collective-permute-start | bytes 786440 | tf_op jit(solution)/shard_map/ppermute | solution.py:202
  70.6 2.8 %collective-permute-start.4 = (bf16[1024,128]{1,0:T(8,128)(2,1)S(1)}, bf16[1024,128]{1,0:T(8,128)(2,1)S(1)}, u32[]{:S(2)}, u32[]{:S(2)}) collective-permute-start(bf16[1024,128]{1,0:T(8,128)(2,1)S(1)} %get-tuple-element.24), channel_id=1, source_target_pairs={{0,128},{128,256},{256,384},{384,0},{1,129},{129,257},{257,385},{3... | collective-permute-start | bytes 786440 | tf_op jit(solution)/shard_map/ppermute | solution.py:202
  73.5 4.2 %collective-permute-done.5 = bf16[1024,128]{1,0:T(8,128)(2,1)S(1)} collective-permute-done((bf16[1024,128]{1,0:T(8,128)(2,1)S(1)}, bf16[1024,128]{1,0:T(8,128)(2,1)S(1)}, u32[]{:S(2)}, u32[]{:S(2)}) %collective-permute-start.5) | collective-permute-done | bytes 262176 | tf_op jit(solution)/shard_map/ppermute | solution.py:202
  77.7 2.8 %collective-permute-done.4 = bf16[1024,128]{1,0:T(8,128)(2,1)S(1)} collective-permute-done((bf16[1024,128]{1,0:T(8,128)(2,1)S(1)}, bf16[1024,128]{1,0:T(8,128)(2,1)S(1)}, u32[]{:S(2)}, u32[]{:S(2)}) %collective-permute-start.4) | collective-permute-done | bytes 262176 | tf_op jit(solution)/shard_map/ppermute | solution.py:202
  80.5 1.2 pad_maximum_fusion.1.kv
  81.7 0.0 collective-permute-done.1
  81.7 0.0 collective-permute-done.2
  81.7 0.1 pad_maximum_fusion
  81.8 1.9 collective-permute-start.3
  83.9 2.5 %collective-permute-done.3 = bf16[4,1040,128]{2,1,0:T(8,128)(2,1)S(1)} collective-permute-done((bf16[4,1040,128]{2,1,0:T(8,128)(2,1)S(1)}, bf16[4,1040,128]{2,1,0:T(8,128)(2,1)S(1)}, u32[]{:S(2)}, u32[]{:S(2)}) %collective-permute-start.3) | collective-permute-done | bytes 1064992 | tf_op jit(solution)/shard_map/ppermute | solution.py:202
  86.4 0.1 constant_dynamic-update-slice_fusion.qd
  86.6 10.0 %shard_map.103 = (bf16[32,512,512]{2,1,0:T(8,128)(2,1)}, f32[32,1,512]{2,1,0:T(1,128)S(1)}, f32[8,2,512]{2,1,0:T(2,128)S(1)}) custom-call(s32[32]{0:T(128)S(1)} %select_reduce_fusion.pairs, s32[3]{0:T(128)S(1)} %pad_add_fusion.meta, bf16[8,1040,128]{2,1,0:T(8,128)(2,1)S(1)} %constant_dynamic-update-slice_fusion.qd, ...), custom_call_target="tpu_custom_call" | custom-call | tf_op jit(solution)/shard_map/pallas_call | solution.py:170
  96.5 0.8 broadcast_in_dim.12
  97.3 9.4 %all-to-all-start.2 = ((f32[8,8,2,512]{3,2,1,0:T(2,128)}), f32[8,8,2,512]{3,2,1,0:T(2,128)S(1)}, u32[]{:S(2)}, u32[]{:S(2)}) async-start(f32[8,8,2,512]{3,2,1,0:T(2,128)} %broadcast_in_dim.12), calls=%async_computation.2 | async-start | bytes 524288 | tf_op jit(solution)/shard_map/all_to_all | solution.py:245
  106.7 15.6 %shard_map.104 = (bf16[32,512,512]{2,1,0:T(8,128)(2,1)}, bf16[8,512,128]{2,1,0:T(8,128)(2,1)S(1)}) custom-call(s32[32]{0:T(128)S(1)} %select_reduce_fusion.pairs, s32[3]{0:T(128)S(1)} %pad_add_fusion.meta, bf16[8,1040,128]{2,1,0:T(8,128)(2,1)S(1)} %constant_dynamic-update-slice_fusion.qd, bf16[4,1024,128]{2,1,0:T(8,128)(2,1)S(1)} %pad_maximum_fusion.1.kv, ...), custom_call_target="tpu_custom_call" | custom-call | tf_op jit(solution)/shard_map/pallas_call | solution.py:170
  122.2 1.0 copy-done.1
  123.2 0.0 all-to-all-done.2.stats_all
  123.2 9.8 %all-to-all-start.1 = ((bf16[8,512,128]{2,1,0:T(8,128)(2,1)}), bf16[8,512,128]{2,1,0:T(8,128)(2,1)}, u32[]{:S(2)}, u32[]{:S(2)}) async-start(bf16[8,512,128]{2,1,0:T(8,128)(2,1)} %copy-done.1), calls=%async_computation.1 | async-start | bytes 2097152 | tf_op jit(solution)/shard_map/all_to_all | solution.py:255
  133.1 13.1 %shard_map.105.own = bf16[4,2,512,128]{3,2,1,0:T(8,128)(2,1)S(1)} custom-call(s32[32]{0:T(128)S(1)} %select_reduce_fusion.pairs, s32[3]{0:T(128)S(1)} %pad_add_fusion.meta, bf16[8,1040,128]{2,1,0:T(8,128)(2,1)S(1)} %constant_dynamic-update-slice_fusion.qd, bf16[32,512,512]{2,1,0:T(8,128)(2,1)} %get-tuple-element.8.probs, ...), custom_call_target="tpu_custom_call" | custom-call | tf_op jit(solution)/shard_map/pallas_call | solution.py:170
  146.2 0.1 slice_bitcast_fusion
  146.2 1.9 collective-permute-start.7
  148.2 1.9 collective-permute-start.8
  150.1 3.9 %collective-permute-start.9 = (bf16[2,512,128]{2,1,0:T(8,128)(2,1)S(1)}, bf16[2,512,128]{2,1,0:T(8,128)(2,1)S(1)}, u32[]{:S(2)}, u32[]{:S(2)}) collective-permute-start(bf16[2,512,128]{2,1,0:T(8,128)(2,1)S(1)} %get-tuple-element.13), channel_id=1, source_target_pairs={{0,128},{128,256},{256,384},{384,0},{1,129},{129,257},{257,385},{3... | collective-permute-start | bytes 786440 | tf_op jit(solution)/shard_map/ppermute | solution.py:202
  154.0 3.3 %collective-permute-done.7.first = bf16[2,512,128]{2,1,0:T(8,128)(2,1)S(1)} collective-permute-done((bf16[2,512,128]{2,1,0:T(8,128)(2,1)S(1)}, bf16[2,512,128]{2,1,0:T(8,128)(2,1)S(1)}, u32[]{:S(2)}, u32[]{:S(2)}) %collective-permute-start.7) | collective-permute-done | bytes 262176 | tf_op jit(solution)/shard_map/ppermute | solution.py:202
  157.3 3.5 %collective-permute-done.8.second = bf16[2,512,128]{2,1,0:T(8,128)(2,1)S(1)} collective-permute-done((bf16[2,512,128]{2,1,0:T(8,128)(2,1)S(1)}, bf16[2,512,128]{2,1,0:T(8,128)(2,1)S(1)}, u32[]{:S(2)}, u32[]{:S(2)}) %collective-permute-start.8) | collective-permute-done | bytes 262176 | tf_op jit(solution)/shard_map/ppermute | solution.py:202
  160.8 4.8 %collective-permute-done.9.third = bf16[2,512,128]{2,1,0:T(8,128)(2,1)S(1)} collective-permute-done((bf16[2,512,128]{2,1,0:T(8,128)(2,1)S(1)}, bf16[2,512,128]{2,1,0:T(8,128)(2,1)S(1)}, u32[]{:S(2)}, u32[]{:S(2)}) %collective-permute-start.9) | collective-permute-done | bytes 262176 | tf_op jit(solution)/shard_map/ppermute | solution.py:202
  165.6 0.0 all-to-all-done.1.dquery
  165.6 2.8 %shard_map.106 = bf16[16,96,128]{2,1,0:T(8,128)(2,1)S(1)} custom-call(s32[3]{0:T(128)S(1)} %pad_add_fusion.meta, bf16[8,512,128]{2,1,0:T(8,128)(2,1)} %all-to-all-done.1.dquery, f32[8,8,2,512]{3,2,1,0:T(2,128)S(1)} %all-to-all-done.2.stats_all, bf16[4,2,512,128]{3,2,1,0:T(8,128)(2,1)S(1)} %shard_map.105.own, ...), custom_call_target="tpu_custom_call" | custom-call | tf_op jit(solution)/shard_map/pallas_call | solution.py:266
  168.3 34.8 %all_to_all.20 = bf16[16,96,128]{2,1,0:T(8,128)(2,1)S(1)} all-to-all(bf16[16,96,128]{2,1,0:T(8,128)(2,1)S(1)} %shard_map.106), channel_id=1, replica_groups=mesh['x'=4,'y'=4,'c'=2,'h'=16] {'h'}, dimensions={0} | all-to-all | bytes 786432 | tf_op jit(solution)/shard_map/all_to_all | solution.py:277
  203.2 0.7 copy.59
  203.9 0.7 copy.58
  204.5 0.7 copy.57
  (32 shorter events, 0.4 us)
Async XLA Ops:
  0.6 21.5 %copy-start = (s32[32]{0:T(128)S(1)}, s32[32]{0:T(128)}, u32[]{:S(2)}) copy-start(s32[32]{0:T(128)} %param.15) | copy-start | bytes 388
  5.4 16.6 %copy-start.4 = (s32[32,16]{0,1:T(8,128)S(1)}, s32[32,16]{0,1:T(8,128)}, u32[]{:S(2)}) copy-start(s32[32,16]{0,1:T(8,128)} %param.13) | copy-start | bytes 6148
  5.7 18.3 %copy-start.2 = (s32[32]{0:T(128)S(1)}, s32[32]{0:T(128)}, u32[]{:S(2)}) copy-start(s32[32]{0:T(128)} %param.14) | copy-start | bytes 388
  6.8 46.0 %all-to-all-start = ((bf16[16,144,128]{2,1,0:T(8,128)(2,1)}), bf16[16,144,128]{2,1,0:T(8,128)(2,1)S(1)}, u32[]{:S(2)}, u32[]{:S(2)}) async-start(bf16[16,144,128]{2,1,0:T(8,128)(2,1)} %copy.40), calls=%async_computation | async-start | bytes 1179648 | tf_op jit(solution)/shard_map/all_to_all | solution.py:220
  53.6 17.0 %collective-permute-start.6 = (bf16[1024,128]{1,0:T(8,128)(2,1)S(1)}, bf16[1024,128]{1,0:T(8,128)(2,1)S(1)}, u32[]{:S(2)}, u32[]{:S(2)}) collective-permute-start(bf16[1024,128]{1,0:T(8,128)(2,1)S(1)} %get-tuple-element.24), channel_id=1, source_target_pairs={{0,384},{128,0},{256,128},{384,256},{1,385},{129,1},{257,129},{385... | collective-permute-start | bytes 786440 | tf_op jit(solution)/shard_map/ppermute | solution.py:202
  59.2 22.5 %collective-permute-start = (bf16[1040,128]{1,0:T(8,128)(2,1)S(1)}, bf16[1040,128]{1,0:T(8,128)(2,1)S(1)}, u32[]{:S(2)}, u32[]{:S(2)}) collective-permute-start(bf16[1040,128]{1,0:T(8,128)(2,1)S(1)} %concatenate.14), channel_id=1, source_target_pairs={{0,32},{32,64},{64,96},{96,0},{1,33},{33,65},{65,97},{97,1},{2,34}... | collective-permute-start | bytes 798728 | tf_op jit(solution)/shard_map/ppermute | solution.py:202
  62.4 19.3 %collective-permute-start.1 = (bf16[1040,128]{1,0:T(8,128)(2,1)S(1)}, bf16[1040,128]{1,0:T(8,128)(2,1)S(1)}, u32[]{:S(2)}, u32[]{:S(2)}) collective-permute-start(bf16[1040,128]{1,0:T(8,128)(2,1)S(1)} %concatenate.14), channel_id=1, source_target_pairs={{0,64},{32,96},{64,0},{96,32},{1,65},{33,97},{65,1},{97,33},{2,66}... | collective-permute-start | bytes 798728 | tf_op jit(solution)/shard_map/ppermute | solution.py:202
  64.9 16.7 %collective-permute-start.2 = (bf16[1040,128]{1,0:T(8,128)(2,1)S(1)}, bf16[1040,128]{1,0:T(8,128)(2,1)S(1)}, u32[]{:S(2)}, u32[]{:S(2)}) collective-permute-start(bf16[1040,128]{1,0:T(8,128)(2,1)S(1)} %concatenate.14), channel_id=1, source_target_pairs={{0,96},{32,0},{64,32},{96,64},{1,97},{33,1},{65,33},{97,65},{2,98}... | collective-permute-start | bytes 798728 | tf_op jit(solution)/shard_map/ppermute | solution.py:202
  67.9 9.8 %collective-permute-start.5 = (bf16[1024,128]{1,0:T(8,128)(2,1)S(1)}, bf16[1024,128]{1,0:T(8,128)(2,1)S(1)}, u32[]{:S(2)}, u32[]{:S(2)}) collective-permute-start(bf16[1024,128]{1,0:T(8,128)(2,1)S(1)} %get-tuple-element.24), channel_id=1, source_target_pairs={{0,256},{128,384},{256,0},{384,128},{1,257},{129,385},{257,1},{385... | collective-permute-start | bytes 786440 | tf_op jit(solution)/shard_map/ppermute | solution.py:202
  70.6 9.9 %copy-start.3 = (bf16[1024,128]{1,0:T(8,128)(2,1)}, bf16[1024,128]{1,0:T(8,128)(2,1)S(1)}, u32[]{:S(2)}) copy-start(bf16[1024,128]{1,0:T(8,128)(2,1)S(1)} %collective-permute-done.6) | copy-start | bytes 786436
  70.6 9.8 %collective-permute-start.4 = (bf16[1024,128]{1,0:T(8,128)(2,1)S(1)}, bf16[1024,128]{1,0:T(8,128)(2,1)S(1)}, u32[]{:S(2)}, u32[]{:S(2)}) collective-permute-start(bf16[1024,128]{1,0:T(8,128)(2,1)S(1)} %get-tuple-element.24), channel_id=1, source_target_pairs={{0,128},{128,256},{256,384},{384,0},{1,129},{129,257},{257,385},{3... | collective-permute-start | bytes 786440 | tf_op jit(solution)/shard_map/ppermute | solution.py:202
  81.8 4.6 %collective-permute-start.3 = (bf16[4,1040,128]{2,1,0:T(8,128)(2,1)S(1)}, bf16[4,1040,128]{2,1,0:T(8,128)(2,1)S(1)}, u32[]{:S(2)}, u32[]{:S(2)}) collective-permute-start(bf16[4,1040,128]{2,1,0:T(8,128)(2,1)S(1)} %pad_maximum_fusion), channel_id=1, source_target_pairs={{0,16},{16,0},{1,17},{17,1},{2,18},{18,2},{3,19},{19,3},{4,20},{20... | collective-permute-start | bytes 3194888 | tf_op jit(solution)/shard_map/ppermute | solution.py:202
  97.3 25.9 %all-to-all-start.2 = ((f32[8,8,2,512]{3,2,1,0:T(2,128)}), f32[8,8,2,512]{3,2,1,0:T(2,128)S(1)}, u32[]{:S(2)}, u32[]{:S(2)}) async-start(f32[8,8,2,512]{3,2,1,0:T(2,128)} %broadcast_in_dim.12), calls=%async_computation.2 | async-start | bytes 524288 | tf_op jit(solution)/shard_map/all_to_all | solution.py:245
  122.2 1.0 copy-start.1
  123.2 42.3 %all-to-all-start.1 = ((bf16[8,512,128]{2,1,0:T(8,128)(2,1)}), bf16[8,512,128]{2,1,0:T(8,128)(2,1)}, u32[]{:S(2)}, u32[]{:S(2)}) async-start(bf16[8,512,128]{2,1,0:T(8,128)(2,1)} %copy-done.1), calls=%async_computation.1 | async-start | bytes 2097152 | tf_op jit(solution)/shard_map/all_to_all | solution.py:255
  146.2 11.0 %collective-permute-start.7 = (bf16[2,512,128]{2,1,0:T(8,128)(2,1)S(1)}, bf16[2,512,128]{2,1,0:T(8,128)(2,1)S(1)}, u32[]{:S(2)}, u32[]{:S(2)}) collective-permute-start(bf16[2,512,128]{2,1,0:T(8,128)(2,1)S(1)} %get-tuple-element.15), channel_id=1, source_target_pairs={{0,384},{128,0},{256,128},{384,256},{1,385},{129,1},{257,129},{385... | collective-permute-start | bytes 786440 | tf_op jit(solution)/shard_map/ppermute | solution.py:202
  148.2 12.6 %collective-permute-start.8 = (bf16[2,512,128]{2,1,0:T(8,128)(2,1)S(1)}, bf16[2,512,128]{2,1,0:T(8,128)(2,1)S(1)}, u32[]{:S(2)}, u32[]{:S(2)}) collective-permute-start(bf16[2,512,128]{2,1,0:T(8,128)(2,1)S(1)} %get-tuple-element.14), channel_id=1, source_target_pairs={{0,256},{128,384},{256,0},{384,128},{1,257},{129,385},{257,1},{385... | collective-permute-start | bytes 786440 | tf_op jit(solution)/shard_map/ppermute | solution.py:202
  150.1 15.4 %collective-permute-start.9 = (bf16[2,512,128]{2,1,0:T(8,128)(2,1)S(1)}, bf16[2,512,128]{2,1,0:T(8,128)(2,1)S(1)}, u32[]{:S(2)}, u32[]{:S(2)}) collective-permute-start(bf16[2,512,128]{2,1,0:T(8,128)(2,1)S(1)} %get-tuple-element.13), channel_id=1, source_target_pairs={{0,128},{128,256},{256,384},{384,0},{1,129},{129,257},{257,385},{3... | collective-permute-start | bytes 786440 | tf_op jit(solution)/shard_map/ppermute | solution.py:202

commit v2 on v1

v2 whole, which is shorter than its diff:
```python
import functools
import math

import jax
import jax.numpy as jnp
from jax import lax
from jax.experimental import pallas as pl
from jax.experimental.pallas import tpu as pltpu
from jax.sharding import Mesh, PartitionSpec as P

HD = 128
BLK = 512
HEADS = 16
ROWS = BLK // HEADS
NX, NY, NC = 4, 4, 2
NQ = NY * NC
NK = NX
NPAIR = NQ * NK
QD_ROWS = 2 * BLK + 16
UNROLL = 4
DEPTH = 3
SHIFTS = (0, 3, 1, 2)
SCALE = 1.0 / math.sqrt(HD)
SCALE2 = SCALE * math.log2(math.e)
LOW = -1e30
VMEM = 48 * 1024 * 1024


def dot(a, b, contract):
    return lax.dot_general(a, b, ((contract[:1], contract[1:]), ((), ())), preferred_element_type=jnp.float32)


def query_place(code, meta):
    slot = code % NQ
    return ((meta[1] - slot % NY) & (NY - 1)) * NC + (meta[2] ^ (slot // NY))


def fetch_queries(own, other, qd, sems):
    return [
        pltpu.make_async_copy(own, qd.at[pl.ds(0, NY)], sems.at[0]),
        pltpu.make_async_copy(other, qd.at[pl.ds(NY, NY)], sems.at[1]),
    ]


def fetch_keys(blocks, kv, sems):
    return [pltpu.make_async_copy(block, kv.at[i], sems.at[i]) for i, block in enumerate(blocks)]


def probs_kernel(
    pairs, meta, own, other, kv0, kv1, kv2, kv3, probs, tops, stats, qd, kv, held, sems, key_sems, out_sems
):
    fetches = fetch_queries(own, other, qd, sems) + fetch_keys((kv0, kv1, kv2, kv3), kv, key_sems)
    for fetch in fetches:
        fetch.start()
    stats[:, 0, :] = jnp.full((NQ, BLK), LOW, jnp.float32)
    stats[:, 1, :] = jnp.zeros((NQ, BLK), jnp.float32)
    for fetch in fetches:
        fetch.wait()
    count = meta[0]
    steps = (count + UNROLL - 1) // UNROLL

    def store(step):
        return pltpu.make_async_copy(
            held.at[step & 1], probs.at[pl.ds(step * UNROLL, UNROLL)], out_sems.at[step & 1]
        )

    def visit(step, first):
        @pl.when(step >= 2)
        def _():
            store(step).wait()

        found = []
        for u in range(UNROLL):
            code = pairs[step * UNROLL + u]
            scores = dot(kv[code // NQ, :BLK, :], qd[code % NQ, :BLK, :], (1, 1))
            if first and u == 0:
                key_row = lax.broadcasted_iota(jnp.int32, scores.shape, 0)
                query_row = lax.broadcasted_iota(jnp.int32, scores.shape, 1)
                scores = jnp.where(key_row <= query_row, scores, LOW)
            found.append((scores, jnp.max(scores, axis=0, keepdims=True) * SCALE2))
        for u, (scores, top) in enumerate(found):
            t = step * UNROLL + u
            place = query_place(pairs[t], meta)
            values = jnp.exp2(scores * SCALE2 - top)
            total = jnp.sum(values, axis=0, keepdims=True)
            held[step & 1, u] = values.astype(jnp.bfloat16)
            tops[t] = top
            top = jnp.where(t < count, top, LOW)
            total = jnp.where(t < count, total, 0.0)
            old_top, old_total = stats[place, 0:1, :], stats[place, 1:2, :]
            new_top = jnp.maximum(old_top, top)
            stats[place, 0:1, :] = new_top
            stats[place, 1:2, :] = old_total * jnp.exp2(old_top - new_top) + total * jnp.exp2(top - new_top)
        store(step).start()

    visit(0, True)

    def body(step, _):
        visit(step, False)
        return 0

    lax.fori_loop(1, steps, body, 0)
    store(steps - 1).wait()

    @pl.when(steps >= 2)
    def _():
        store(steps - 2).wait()


def dscore_kernel(
    pairs, meta, own, other, kv0, kv1, kv2, kv3, probs, tops, stats, dscore, dquery,
    qd, kv, keys_t, total, read, held, sems, key_sems, in_sems, out_sems,
):
    count = meta[0]
    steps = (count + UNROLL - 1) // UNROLL

    def load(step):
        return pltpu.make_async_copy(
            probs.at[pl.ds(step * UNROLL, UNROLL)], read.at[step & 1], in_sems.at[step & 1]
        )

    def store(step):
        return pltpu.make_async_copy(
            held.at[step & 1], dscore.at[pl.ds(step * UNROLL, UNROLL)], out_sems.at[step & 1]
        )

    key_fetches = fetch_keys((kv0, kv1, kv2, kv3), kv, key_sems)
    fetches = fetch_queries(own, other, qd, sems)
    for fetch in key_fetches + fetches:
        fetch.start()
    load(0).start()
    total[...] = jnp.zeros_like(total)
    for i, fetch in enumerate(key_fetches):
        fetch.wait()
        keys_t[i] = jnp.transpose(kv[i, :BLK, :])
    for fetch in fetches:
        fetch.wait()

    def body(step, _):
        load(step).wait()

        @pl.when(step + 1 < steps)
        def _():
            load(step + 1).start()

        @pl.when(step >= 2)
        def _():
            store(step).wait()

        for u in range(UNROLL):
            t = step * UNROLL + u
            code = pairs[t]
            place, key, query = query_place(code, meta), code // NQ, code % NQ
            pieces = qd[query, 2 * BLK :, :].astype(jnp.float32)
            row_dot = pieces[0:4] + pieces[4:8] + pieces[8:12]
            row_dot = jnp.concatenate([row_dot[i : i + 1] for i in range(4)], axis=1)
            weight = jnp.where(t < count, jnp.exp2(tops[t] - stats[place, 0:1, :]), 0.0)
            dprob = dot(kv[key, BLK:, :], qd[query, BLK : 2 * BLK, :], (1, 1))
            low = (read[step & 1, u].astype(jnp.float32) * (dprob - row_dot)).astype(jnp.bfloat16)
            held[step & 1, u] = low
            total[place] += dot(keys_t[key], low, (1, 0)) * weight
        store(step).start()
        return 0

    lax.fori_loop(0, steps, body, 0)
    for i in range(NQ):
        dquery[i] = jnp.transpose(total[i]).astype(jnp.bfloat16)
    store(steps - 1).wait()

    @pl.when(steps >= 2)
    def _():
        store(steps - 2).wait()


def log_norms(stats_all):
    tops, sums = stats_all[:, :, 0, :], stats_all[:, :, 1, :]
    top = jnp.max(tops, axis=0)
    return top + jnp.log2(jnp.sum(sums * jnp.exp2(tops - top[None]), axis=0))


def key_kernel(
    late, pairs, meta, own, other, probs, dscore, tops, stats_all, out,
    qd, norms, total, p_read, d_read, sems, p_sems, d_sems,
):
    begin, end = (0, meta[3]) if late else (meta[3], meta[0])
    steps = (end - begin + UNROLL - 1) // UNROLL

    def loads(step):
        slot = lax.rem(step, DEPTH)
        copies = []
        for u in range(UNROLL):
            t = jnp.minimum(begin + step * UNROLL + u, end - 1)
            copies.append(pltpu.make_async_copy(probs.at[t], p_read.at[slot, u], p_sems.at[slot, u]))
            copies.append(pltpu.make_async_copy(dscore.at[t], d_read.at[slot, u], d_sems.at[slot, u]))
        return copies

    def prefetch(step):
        @pl.when(step < steps)
        def _():
            for copy in loads(step):
                copy.start()

    fetches = fetch_queries(own, other, qd, sems)
    for fetch in fetches:
        fetch.start()
    for step in range(DEPTH - 1):
        prefetch(step)
    total[...] = jnp.zeros_like(total)
    norms[:, 0, :] = log_norms(stats_all[...])
    for fetch in fetches:
        fetch.wait()

    def body(step, _):
        slot = lax.rem(step, DEPTH)
        for copy in loads(step):
            copy.wait()
        prefetch(step + DEPTH - 1)
        found = []
        for u in range(UNROLL):
            t = begin + step * UNROLL + u
            code = pairs[jnp.minimum(t, end - 1)]
            place, key, query = query_place(code, meta), code // NQ, code % NQ
            weight = jnp.where(t < end, jnp.exp2(tops[jnp.minimum(t, end - 1)] - norms[place]), 0.0)
            weight = jnp.transpose(jnp.broadcast_to(weight, (HD, BLK)))
            queries = (qd[query, :BLK, :].astype(jnp.float32) * (weight * SCALE)).astype(jnp.bfloat16)
            grads = (qd[query, BLK : 2 * BLK, :].astype(jnp.float32) * weight).astype(jnp.bfloat16)
            found.append((key & 1, dot(d_read[slot, u], queries, (1, 0)), dot(p_read[slot, u], grads, (1, 0))))
        for key, key_part, value_part in found:
            total[key, 0] += key_part
            total[key, 1] += value_part
        return 0

    lax.fori_loop(0, steps, body, 0)
    out[...] = total[...].astype(jnp.bfloat16)


def finish_kernel(meta, dquery, stats_all, own, first, second, third, out):
    place = meta[1] * NC + meta[2]
    tops, sums = stats_all[:, place, 0, :], stats_all[:, place, 1, :]
    top = jnp.max(tops, axis=0, keepdims=True)
    norm = top + jnp.log2(jnp.sum(sums * jnp.exp2(tops - top), axis=0, keepdims=True))
    weight = jnp.transpose(jnp.exp2(tops - norm) * SCALE)
    query_grad = dquery[0].astype(jnp.float32) * weight[:, 0:1]
    for i in range(1, NQ):
        query_grad += dquery[i].astype(jnp.float32) * weight[:, i : i + 1]
    out[:, 0:ROWS, :] = query_grad.astype(jnp.bfloat16).reshape(HEADS, ROWS, HD)
    for i in range(2):
        grad = (own[0, i].astype(jnp.float32) + first[i].astype(jnp.float32)) + (
            second[i].astype(jnp.float32) + third[i].astype(jnp.float32)
        )
        out[:, (i + 1) * ROWS : (i + 2) * ROWS, :] = grad.astype(jnp.bfloat16).reshape(HEADS, ROWS, HD)


def params():
    return pltpu.CompilerParams(vmem_limit_bytes=VMEM)


def whole(*shape):
    return pl.BlockSpec(shape, lambda *_: (0,) * len(shape))


def over_pairs(kernel, pairs, meta, operands, in_specs, out_specs, out_shape, scratch):
    return pl.pallas_call(
        kernel,
        grid_spec=pltpu.PrefetchScalarGridSpec(
            num_scalar_prefetch=2,
            grid=(1,),
            in_specs=in_specs,
            out_specs=out_specs,
            scratch_shapes=scratch,
        ),
        out_shape=out_shape,
        compiler_params=params(),
    )(pairs, meta, *operands)


def pair_list(key_lists, key_counts, block_order, x, y, c):
    slot = jnp.arange(NQ, dtype=jnp.int32)
    query_at = x * NQ + ((y - slot % NY) % NY) * NC + (c ^ (slot // NY))
    key_at = ((x - jnp.array(SHIFTS, jnp.int32)) % NX) * NQ + y * NC + c
    query_blocks, key_blocks = block_order[query_at], block_order[key_at]
    lists, counts = key_lists[query_blocks], key_counts[query_blocks]
    used = jnp.arange(key_lists.shape[1], dtype=jnp.int32)[None, :] < counts[:, None]
    named = jnp.any((lists[None, :, :] == key_blocks[:, None, None]) & used[None, :, :], axis=2)
    named = named.reshape(NPAIR)
    code = jnp.arange(NPAIR, dtype=jnp.int32)
    rank = jnp.sum((code[None, :] < code[:, None]) & named[None, :], axis=1)
    count = jnp.sum(named.astype(jnp.int32))
    wanted = jnp.minimum(code, count - 1)
    pairs = jnp.sum(jnp.where(named[None, :] & (rank[None, :] == wanted[:, None]), code[None, :], 0), axis=1)
    return pairs.astype(jnp.int32), count, jnp.sum(named[: 2 * NQ].astype(jnp.int32))


def shifted(array, axis, by, size):
    return lax.ppermute(array, axis, [(i, (i + by) % size) for i in range(size)])


def on_device(query_data, key_data, value_data, output_data, output_grad, key_lists, key_counts, block_order):
    x, y, c = lax.axis_index("x"), lax.axis_index("y"), lax.axis_index("c")

    def heads(array):
        return jnp.transpose(array.reshape(ROWS, HEADS, HD), (1, 0, 2))

    products = output_grad.astype(jnp.float32) * output_data.astype(jnp.float32)
    row_dot = jnp.transpose(jnp.sum(products.reshape(ROWS, HEADS, HD), axis=2))
    high = lax.reduce_precision(row_dot, 8, 7)
    middle = lax.reduce_precision(row_dot - high, 8, 7)
    pieces = jnp.stack([high, middle, row_dot - high - middle], axis=1).astype(jnp.bfloat16)
    pieces = jnp.pad(pieces, ((0, 0), (0, 13), (0, HD - ROWS)))
    def regrouped(*parts):
        return lax.all_to_all(jnp.concatenate(parts, axis=1), "h", 0, 0, tiled=True)

    def rows(packed, i):
        return packed[:, i * ROWS : (i + 1) * ROWS, :].reshape(BLK, HD)

    packed = regrouped(heads(query_data), heads(output_grad), pieces)
    pieces = jnp.transpose(packed[:, 2 * ROWS : 2 * ROWS + 3, :ROWS], (1, 0, 2)).reshape(12, HD)
    qd = jnp.concatenate([rows(packed, 0), rows(packed, 1), pieces, jnp.zeros((4, HD), jnp.bfloat16)], axis=0)
    packed = regrouped(heads(key_data), heads(value_data))
    kv = jnp.concatenate([rows(packed, 0), rows(packed, 1)], axis=0)

    pairs, count, early = pair_list(key_lists, key_counts, block_order, x, y, c)
    meta = jnp.stack([count, y, c, early]).astype(jnp.int32)

    own = jnp.stack([qd] + [shifted(qd, "y", i, NY) for i in range(1, NY)])
    queries = (own, shifted(own, "c", 1, NC))
    keys = tuple(shifted(kv, "x", i, NX) if i else kv for i in SHIFTS)

    bf16, f32 = jnp.bfloat16, jnp.float32
    shape, anywhere, vmem = jax.ShapeDtypeStruct, pl.BlockSpec(memory_space=pl.ANY), pl.BlockSpec(memory_space=pltpu.VMEM)
    square, line = shape((NPAIR, BLK, BLK), bf16), shape((NPAIR, 1, BLK), f32)
    qd_scratch, kv_scratch = pltpu.VMEM((NQ, QD_ROWS, HD), bf16), pltpu.VMEM((NK, 2 * BLK, HD), bf16)
    dma = pltpu.SemaphoreType.DMA
    probs, tops, stats = over_pairs(
        probs_kernel, pairs, meta, (*queries, *keys),
        [anywhere] * 6,
        [anywhere, vmem, vmem],
        [square, line, shape((NQ, 2, BLK), f32)],
        [qd_scratch, kv_scratch, pltpu.VMEM((2, UNROLL, BLK, BLK), bf16), dma((2,)), dma((NK,)), dma((2,))],
    )
    stats_all = lax.all_to_all(
        jnp.broadcast_to(stats[None], (NQ, NQ, 2, BLK)), ("y", "c"), 0, 0, tiled=True
    )
    dscore, dquery = over_pairs(
        dscore_kernel, pairs, meta, (*queries, *keys, probs, tops, stats),
        [anywhere] * 7 + [vmem] * 2,
        [anywhere, vmem],
        [square, shape((NQ, BLK, HD), bf16)],
        [
            qd_scratch, kv_scratch, pltpu.VMEM((NK, HD, BLK), bf16), pltpu.VMEM((NQ, HD, BLK), f32),
            pltpu.VMEM((2, UNROLL, BLK, BLK), bf16), pltpu.VMEM((2, UNROLL, BLK, BLK), bf16),
            dma((2,)), dma((NK,)), dma((2,)), dma((2,)),
        ],
    )
    dquery = lax.all_to_all(dquery, ("y", "c"), 0, 0, tiled=True)

    def key_grads(late):
        return over_pairs(
            functools.partial(key_kernel, late), pairs, meta, (*queries, probs, dscore, tops, stats_all),
            [anywhere] * 4 + [vmem] * 2,
            vmem,
            shape((2, 2, BLK, HD), bf16),
            [
                qd_scratch, pltpu.VMEM((NQ, 1, BLK), f32), pltpu.VMEM((2, 2, BLK, HD), f32),
                pltpu.VMEM((DEPTH, UNROLL, BLK, BLK), bf16), pltpu.VMEM((DEPTH, UNROLL, BLK, BLK), bf16),
                dma((2,)), dma((DEPTH, UNROLL)), dma((DEPTH, UNROLL)),
            ],
        )

    sent_first, sent_last = key_grads(False), key_grads(True)
    arrived = [shifted(sent_first[i], "x", -SHIFTS[2 + i], NX) for i in range(2)]
    arrived.append(shifted(sent_last[1], "x", -SHIFTS[1], NX))

    part = whole(2, BLK, HD)
    grads = pl.pallas_call(
        finish_kernel,
        grid_spec=pltpu.PrefetchScalarGridSpec(
            num_scalar_prefetch=1,
            grid=(1,),
            in_specs=[whole(NQ, BLK, HD), whole(NQ, NQ, 2, BLK), whole(1, 2, BLK, HD), part, part, part],
            out_specs=whole(HEADS, 3 * ROWS, HD),
        ),
        out_shape=shape((HEADS, 3 * ROWS, HD), bf16),
        compiler_params=params(),
    )(meta, dquery, stats_all, sent_last, *arrived)
    grads = lax.all_to_all(grads, "h", 0, 0, tiled=True)

    def tokens(i):
        part = grads[:, i * ROWS : (i + 1) * ROWS, :]
        return jnp.transpose(part, (1, 0, 2)).reshape(ROWS, HEADS * HD)

    return tokens(0), tokens(1), tokens(2)


def solution(mesh):
    wide = Mesh(mesh.devices.reshape(NX, NY, NC, HEADS), ("x", "y", "c", "h"))
    split = P(("x", "y", "c", "h"), None)
    return jax.shard_map(
        on_device,
        mesh=wide,
        in_specs=(split,) * 5 + (P(),) * 3,
        out_specs=(split,) * 3,
        check_vma=False,
    )
```

time: 207 us -> 196 us (0.947)
  Pallas kernels: 41.4 us -> 25.4 us
  starting transfers between devices: 62.9 us -> 70.4 us
  waiting for transfers between devices: 47.1 us -> 43.8 us
    pallas_call x3 -> x4, Pallas kernels: 38.6 us -> 22.6 us  [over_pairs(): pl.pallas_call(kernel, grid_spec=pltpu.PrefetchScalarGridSpec(num_scalar_...]
    all_to_all x1 -> x2, waiting for transfers between devices: 26 us -> 19.2 us  [regrouped(): return lax.all_to_all(jnp.concatenate(parts, axis=1), 'h', 0, 0, tiled=True)]
    all_to_all x1 -> x2, starting transfers between devices: 15.2 us -> 21.5 us  [regrouped(): return lax.all_to_all(jnp.concatenate(parts, axis=1), 'h', 0, 0, tiled=True)]
    ppermute x10, waiting for transfers between devices: 21.1 us -> 24.6 us  [shifted(): lax.ppermute(array, axis, [(i, (i + by) % size) for i in range(size)])]
    ppermute x10, starting transfers between devices: 28.5 us -> 31.1 us  [shifted(): lax.ppermute(array, axis, [(i, (i + by) % size) for i in range(size)])]
    unnamed x26 -> x36, local copies, waits for them, and re-layouts: 5.16 us -> 5.52 us
  transfers between devices with their start and end apart: 13 -> 14, of which waited for: 7 -> 6; matrix products, arithmetic and copies ran while one was open for 3% -> 4% of each run, Pallas kernels for 14% -> 9%
where the time goes in v2:
time: 196 us; the launch traced here: 195 us
  starting transfers between devices  70.4 us (36%)
  waiting for transfers between devices  43.8 us (22%)
  blocking collectives  35.8 us (18%)
  Pallas kernels  25.4 us (13%)
  local copies, waits for them, and re-layouts  12 us (6%)
  other arithmetic  5.44 us (3%)
    all_to_all x1, blocking collectives, on_device(): grads = lax.all_to_all(grads, 'h', 0, 0, tiled=True)  35.8 us
    ppermute x10, starting transfers between devices, shifted(): lax.ppermute(array, axis, [(i, (i + by) % size) for i in range(size)])  31.1 us
    ppermute x10, waiting for transfers between devices, shifted(): lax.ppermute(array, axis, [(i, (i + by) % size) for i in range(size)])  24.6 us
    pallas_call x4, Pallas kernels, over_pairs(): pl.pallas_call(kernel, grid_spec=pltpu.PrefetchScalarGridSpec(num_scalar_...  22.6 us
    all_to_all x2, starting transfers between devices, regrouped(): return lax.all_to_all(jnp.concatenate(parts, axis=1), 'h', 0, 0, tiled=True)  21.5 us
    all_to_all x2, waiting for transfers between devices, regrouped(): return lax.all_to_all(jnp.concatenate(parts, axis=1), 'h', 0, 0, tiled=True)  19.2 us
    all_to_all x1, starting transfers between devices, on_device(): lax.all_to_all(jnp.broadcast_to(stats[None], (NQ, NQ, 2, BLK)), ('y', 'c'...  9.48 us
    all_to_all x1, starting transfers between devices, on_device(): dquery = lax.all_to_all(dquery, ('y', 'c'), 0, 0, tiled=True)  8.26 us
  transfers between devices with their start and end apart: 14, of which 6 were waited for; matrix products, arithmetic and copies ran while one was open for 4% of the time, Pallas kernels for 9%

profile of v2, /device:TPU:16, one launch (start us, length us, event | category | flops | bytes accessed | tf_op | source)
XLA Modules:
  0.0 194.5 jit_solution(11956157714813176867)
XLA Ops:
  0.6 0.0 copy-start
  0.7 1.0 multiply_bitcast_fusion
  1.8 0.1 reduce_sum.49
  2.0 0.1 copy.51
  2.1 0.0 copy-start.8
  2.2 0.0 copy-start.12
  2.2 0.8 copy.44
  3.0 15.3 %all-to-all-start = ((bf16[16,80,128]{2,1,0:T(8,128)(2,1)}), bf16[16,80,128]{2,1,0:T(8,128)(2,1)S(1)}, u32[]{:S(2)}, u32[]{:S(2)}) async-start(bf16[16,80,128]{2,1,0:T(8,128)(2,1)} %copy.44), calls=%async_computation | async-start | bytes 655360 | tf_op jit(solution)/shard_map/all_to_all | solution.py:311
  18.4 0.6 gather_fusion
  19.1 0.0 copy-start.13
  19.1 0.7 pad_maximum_fusion.1
  19.9 19.2 %all-to-all-done = bf16[16,80,128]{2,1,0:T(8,128)(2,1)S(1)} async-done(((bf16[16,80,128]{2,1,0:T(8,128)(2,1)}), bf16[16,80,128]{2,1,0:T(8,128)(2,1)S(1)}, u32[]{:S(2)}, u32[]{:S(2)}) %all-to-all-start) | async-done | bytes 327712 | tf_op jit(solution)/shard_map/all_to_all | solution.py:311
  39.1 6.2 %all-to-all-start.1 = ((bf16[16,64,128]{2,1,0:T(8,128)(2,1)}), bf16[16,64,128]{2,1,0:T(8,128)(2,1)S(1)}, u32[]{:S(2)}, u32[]{:S(2)}) async-start(bf16[16,64,128]{2,1,0:T(8,128)(2,1)} %pad_maximum_fusion.1), calls=%async_computation.1 | async-start | bytes 524288 | tf_op jit(solution)/shard_map/all_to_all | solution.py:311
  45.3 0.1 reshape.198
  45.4 0.1 concatenate.13
  45.5 2.3 %collective-permute-start.2 = (bf16[1040,128]{1,0:T(8,128)(2,1)S(1)}, bf16[1040,128]{1,0:T(8,128)(2,1)S(1)}, u32[]{:S(2)}, u32[]{:S(2)}) collective-permute-start(bf16[1040,128]{1,0:T(8,128)(2,1)S(1)} %concatenate.13), channel_id=1, source_target_pairs={{0,96},{32,0},{64,32},{96,64},{1,97},{33,1},{65,33},{97,65},{2,98}... | collective-permute-start | bytes 798728 | tf_op jit(solution)/shard_map/ppermute | solution.py:295
  47.9 4.8 %collective-permute-start.1 = (bf16[1040,128]{1,0:T(8,128)(2,1)S(1)}, bf16[1040,128]{1,0:T(8,128)(2,1)S(1)}, u32[]{:S(2)}, u32[]{:S(2)}) collective-permute-start(bf16[1040,128]{1,0:T(8,128)(2,1)S(1)} %concatenate.13), channel_id=1, source_target_pairs={{0,64},{32,96},{64,0},{96,32},{1,65},{33,97},{65,1},{97,33},{2,66}... | collective-permute-start | bytes 798728 | tf_op jit(solution)/shard_map/ppermute | solution.py:295
  52.7 1.9 collective-permute-start
  54.6 0.1 copy.42
  54.7 0.6 gather_fusion.2
  55.4 0.6 gather_fusion.1
  55.9 0.6 gather_fusion.3
  56.6 0.1 iota_compare_fusion.2
  56.6 0.1 collective-permute-done.2
  56.7 3.9 %collective-permute-done.1 = bf16[1040,128]{1,0:T(8,128)(2,1)S(1)} collective-permute-done((bf16[1040,128]{1,0:T(8,128)(2,1)S(1)}, bf16[1040,128]{1,0:T(8,128)(2,1)S(1)}, u32[]{:S(2)}, u32[]{:S(2)}) %collective-permute-start.1) | collective-permute-done | bytes 266272 | tf_op jit(solution)/shard_map/ppermute | solution.py:295
  60.6 3.8 %collective-permute-done = bf16[1040,128]{1,0:T(8,128)(2,1)S(1)} collective-permute-done((bf16[1040,128]{1,0:T(8,128)(2,1)S(1)}, bf16[1040,128]{1,0:T(8,128)(2,1)S(1)}, u32[]{:S(2)}, u32[]{:S(2)}) %collective-permute-start) | collective-permute-done | bytes 266272 | tf_op jit(solution)/shard_map/ppermute | solution.py:295
  64.4 0.1 pad_maximum_fusion.own
  64.5 1.9 collective-permute-start.3
  66.5 0.2 and_reduce_fusion
  66.7 0.7 convert_reduce_fusion.1
  68.0 0.6 fusion.7
  68.7 0.0 all-to-all-done.1
  68.7 4.7 %collective-permute-start.4 = (bf16[1024,128]{1,0:T(8,128)(2,1)S(1)}, bf16[1024,128]{1,0:T(8,128)(2,1)S(1)}, u32[]{:S(2)}, u32[]{:S(2)}) collective-permute-start(bf16[1024,128]{1,0:T(8,128)(2,1)S(1)} %pad_maximum_fusion.2.kv0), channel_id=1, source_target_pairs={{0,384},{128,0},{256,128},{384,256},{1,385},{129,1},{257,129},{385... | collective-permute-start | bytes 786440 | tf_op jit(solution)/shard_map/ppermute | solution.py:295
  73.4 1.9 collective-permute-start.5
  75.3 4.2 %collective-permute-start.6 = (bf16[1024,128]{1,0:T(8,128)(2,1)S(1)}, bf16[1024,128]{1,0:T(8,128)(2,1)S(1)}, u32[]{:S(2)}, u32[]{:S(2)}) collective-permute-start(bf16[1024,128]{1,0:T(8,128)(2,1)S(1)} %pad_maximum_fusion.2.kv0), channel_id=1, source_target_pairs={{0,256},{128,384},{256,0},{384,128},{1,257},{129,385},{257,1},{385... | collective-permute-start | bytes 786440 | tf_op jit(solution)/shard_map/ppermute | solution.py:295
  79.5 1.3 pad_add_fusion.meta
  80.9 0.1 and.88
  80.9 0.1 convert_reduce_fusion
  81.1 0.2 select_reduce_fusion.pairs
  81.3 9.3 %collective-permute-done.5.kv2 = bf16[1024,128]{1,0:T(8,128)(2,1)S(1)} collective-permute-done((bf16[1024,128]{1,0:T(8,128)(2,1)S(1)}, bf16[1024,128]{1,0:T(8,128)(2,1)S(1)}, u32[]{:S(2)}, u32[]{:S(2)}) %collective-permute-start.5) | collective-permute-done | bytes 262176 | tf_op jit(solution)/shard_map/ppermute | solution.py:295
  90.6 5.2 %shard_map.112 = (bf16[32,512,512]{2,1,0:T(8,128)(2,1)}, f32[32,1,512]{2,1,0:T(1,128)S(1)}, f32[8,2,512]{2,1,0:T(2,128)S(1)}) custom-call(s32[32]{0:T(128)S(1)} %select_reduce_fusion.pairs, s32[4]{0:T(128)S(1)} %pad_add_fusion.meta, bf16[4,1040,128]{2,1,0:T(8,128)(2,1)S(1)} %pad_maximum_fusion.own, bf16[4,1040,128]{2,1,0:T(8,128)(2,1)S(1)} %collective-permute-done.3.other, ...), custom_call_target="tpu_custom_call" | custom-call | tf_op jit(solution)/shard_map/pallas_call | solution.py:263
  95.8 0.8 broadcast_in_dim.15
  96.5 9.5 %all-to-all-start.3 = ((f32[8,8,2,512]{3,2,1,0:T(2,128)}), f32[8,8,2,512]{3,2,1,0:T(2,128)S(1)}, u32[]{:S(2)}, u32[]{:S(2)}) async-start(f32[8,8,2,512]{3,2,1,0:T(2,128)} %broadcast_in_dim.15), calls=%async_computation.3 | async-start | bytes 524288 | tf_op jit(solution)/shard_map/all_to_all | solution.py:341
  106.0 0.9 copy-done.2
  106.9 6.7 %shard_map.113 = (bf16[32,512,512]{2,1,0:T(8,128)(2,1)}, bf16[8,512,128]{2,1,0:T(8,128)(2,1)S(1)}) custom-call(s32[32]{0:T(128)S(1)} %select_reduce_fusion.pairs, s32[4]{0:T(128)S(1)} %pad_add_fusion.meta, bf16[4,1040,128]{2,1,0:T(8,128)(2,1)S(1)} %pad_maximum_fusion.own, bf16[4,1040,128]{2,1,0:T(8,128)(2,1)S(1)} %collective-permute-done.3.other, ...), custom_call_target="tpu_custom_call" | custom-call | tf_op jit(solution)/shard_map/pallas_call | solution.py:263
  113.7 1.0 copy-done.3
  114.6 8.3 %all-to-all-start.2 = ((bf16[8,512,128]{2,1,0:T(8,128)(2,1)}), bf16[8,512,128]{2,1,0:T(8,128)(2,1)}, u32[]{:S(2)}, u32[]{:S(2)}) async-start(bf16[8,512,128]{2,1,0:T(8,128)(2,1)} %copy-done.3), calls=%async_computation.2 | async-start | bytes 2097152 | tf_op jit(solution)/shard_map/all_to_all | solution.py:355
  122.9 4.8 %shard_map.115 = bf16[2,2,512,128]{3,2,1,0:T(8,128)(2,1)S(1)} custom-call(s32[32]{0:T(128)S(1)} %select_reduce_fusion.pairs, s32[4]{0:T(128)S(1)} %pad_add_fusion.meta, bf16[4,1040,128]{2,1,0:T(8,128)(2,1)S(1)} %pad_maximum_fusion.own, bf16[4,1040,128]{2,1,0:T(8,128)(2,1)S(1)} %collective-permute-done.3.other, bf16[32,512,512]{2,1,0:T(8,128)(2,1)} %get-tuple-element.8.probs, ...), custom_call_target="tpu_custom_call" | custom-call | tf_op jit(solution)/shard_map/pallas_call | solution.py:263
  127.7 1.9 collective-permute-start.7
  129.6 4.1 %collective-permute-start.8 = (bf16[2,512,128]{2,1,0:T(8,128)(2,1)S(1)}, bf16[2,512,128]{2,1,0:T(8,128)(2,1)S(1)}, u32[]{:S(2)}, u32[]{:S(2)}) collective-permute-start(bf16[2,512,128]{2,1,0:T(8,128)(2,1)S(1)} %get-tuple-element.13), channel_id=1, source_target_pairs={{0,256},{128,384},{256,0},{384,128},{1,257},{129,385},{257,1},{385... | collective-permute-start | bytes 786440 | tf_op jit(solution)/shard_map/ppermute | solution.py:295
  133.7 6.0 %shard_map.114.own = bf16[2,2,512,128]{3,2,1,0:T(8,128)(2,1)S(1)} custom-call(s32[32]{0:T(128)S(1)} %select_reduce_fusion.pairs, s32[4]{0:T(128)S(1)} %pad_add_fusion.meta, bf16[4,1040,128]{2,1,0:T(8,128)(2,1)S(1)} %pad_maximum_fusion.own, bf16[4,1040,128]{2,1,0:T(8,128)(2,1)S(1)} %collective-permute-done.3.other, ...), custom_call_target="tpu_custom_call" | custom-call | tf_op jit(solution)/shard_map/pallas_call | solution.py:263
  139.7 3.3 %collective-permute-start.9 = (bf16[2,512,128]{2,1,0:T(8,128)(2,1)S(1)}, bf16[2,512,128]{2,1,0:T(8,128)(2,1)S(1)}, u32[]{:S(2)}, u32[]{:S(2)}) collective-permute-start(bf16[2,512,128]{2,1,0:T(8,128)(2,1)S(1)} %slice_bitcast_fusion), channel_id=1, source_target_pairs={{0,128},{128,256},{256,384},{384,0},{1,129},{129,257},{257,385},{3... | collective-permute-start | bytes 786440 | tf_op jit(solution)/shard_map/ppermute | solution.py:295
  143.1 0.0 collective-permute-done.7.first
  143.1 0.7 copy-done.4
  143.8 0.7 copy-done.6
  144.5 7.5 %collective-permute-done.9.third = bf16[2,512,128]{2,1,0:T(8,128)(2,1)S(1)} collective-permute-done((bf16[2,512,128]{2,1,0:T(8,128)(2,1)S(1)}, bf16[2,512,128]{2,1,0:T(8,128)(2,1)S(1)}, u32[]{:S(2)}, u32[]{:S(2)}) %collective-permute-start.9) | collective-permute-done | bytes 262176 | tf_op jit(solution)/shard_map/ppermute | solution.py:295
  152.0 0.0 all-to-all-done.2.dquery
  152.0 0.9 copy-done.5
  153.0 0.9 copy-done.7
  153.9 2.8 %shard_map.116 = bf16[16,96,128]{2,1,0:T(8,128)(2,1)S(1)} custom-call(s32[4]{0:T(128)S(1)} %pad_add_fusion.meta, bf16[8,512,128]{2,1,0:T(8,128)(2,1)} %all-to-all-done.2.dquery, f32[8,8,2,512]{3,2,1,0:T(2,128)S(1)} %all-to-all-done.3.stats_all, bf16[2,2,512,128]{3,2,1,0:T(8,128)(2,1)S(1)} %shard_map.114.own, bf16[2,512,128]{2,1,0:T(8,128)(2,1)S(1)} %copy-done.5, ...), custom_call_target="tpu_custom_call" | custom-call | tf_op jit(solution)/shard_map/pallas_call | solution.py:375
  156.7 35.8 %all_to_all.25 = bf16[16,96,128]{2,1,0:T(8,128)(2,1)S(1)} all-to-all(bf16[16,96,128]{2,1,0:T(8,128)(2,1)S(1)} %shard_map.116), channel_id=1, replica_groups=mesh['x'=4,'y'=4,'c'=2,'h'=16] {'h'}, dimensions={0} | all-to-all | bytes 786432 | tf_op jit(solution)/shard_map/all_to_all | solution.py:386
  192.5 0.7 copy.67
  193.1 0.7 copy.66
  193.8 0.7 copy.65
  (48 shorter events, 0.5 us)
Async XLA Ops:
  0.6 18.4 %copy-start = (bf16[32,2048]{1,0:T(8,128)(2,1)S(1)}, bf16[32,2048]{1,0:T(8,128)(2,1)}, u32[]{:S(2)}) copy-start(bf16[32,2048]{1,0:T(8,128)(2,1)} %param.10) | copy-start | bytes 393220
  0.6 1.4 copy-start.10
  0.7 1.4 copy-start.11
  2.1 16.3 %copy-start.8 = (s32[32]{0:T(128)S(1)}, s32[32]{0:T(128)}, u32[]{:S(2)}) copy-start(s32[32]{0:T(128)} %param.16) | copy-start | bytes 388
  2.2 16.9 %copy-start.12 = (bf16[32,2048]{1,0:T(8,128)(2,1)S(1)}, bf16[32,2048]{1,0:T(8,128)(2,1)}, u32[]{:S(2)}) copy-start(bf16[32,2048]{1,0:T(8,128)(2,1)} %param.11) | copy-start | bytes 393220
  3.0 16.9 %copy-start.14 = (s32[4]{0:T(128)S(1)}, s32[4]{0:T(128)}, u32[]{:S(2)}) copy-start(s32[4]{0:T(128)} %constant.90) | copy-start | bytes 52
  3.0 36.1 %all-to-all-start = ((bf16[16,80,128]{2,1,0:T(8,128)(2,1)}), bf16[16,80,128]{2,1,0:T(8,128)(2,1)S(1)}, u32[]{:S(2)}, u32[]{:S(2)}) async-start(bf16[16,80,128]{2,1,0:T(8,128)(2,1)} %copy.44), calls=%async_computation | async-start | bytes 655360 | tf_op jit(solution)/shard_map/all_to_all | solution.py:311
  19.1 35.5 %copy-start.13 = (s32[32,16]{0,1:T(8,128)S(1)}, s32[32,16]{0,1:T(8,128)}, u32[]{:S(2)}) copy-start(s32[32,16]{0,1:T(8,128)} %param.14) | copy-start | bytes 6148
  19.9 36.1 %copy-start.9 = (s32[32]{0:T(128)S(1)}, s32[32]{0:T(128)}, u32[]{:S(2)}) copy-start(s32[32]{0:T(128)} %param.15) | copy-start | bytes 388
  39.1 29.6 %all-to-all-start.1 = ((bf16[16,64,128]{2,1,0:T(8,128)(2,1)}), bf16[16,64,128]{2,1,0:T(8,128)(2,1)S(1)}, u32[]{:S(2)}, u32[]{:S(2)}) async-start(bf16[16,64,128]{2,1,0:T(8,128)(2,1)} %pad_maximum_fusion.1), calls=%async_computation.1 | async-start | bytes 524288 | tf_op jit(solution)/shard_map/all_to_all | solution.py:311
  45.5 11.2 %collective-permute-start.2 = (bf16[1040,128]{1,0:T(8,128)(2,1)S(1)}, bf16[1040,128]{1,0:T(8,128)(2,1)S(1)}, u32[]{:S(2)}, u32[]{:S(2)}) collective-permute-start(bf16[1040,128]{1,0:T(8,128)(2,1)S(1)} %concatenate.13), channel_id=1, source_target_pairs={{0,96},{32,0},{64,32},{96,64},{1,97},{33,1},{65,33},{97,65},{2,98}... | collective-permute-start | bytes 798728 | tf_op jit(solution)/shard_map/ppermute | solution.py:295
  47.9 12.7 %collective-permute-start.1 = (bf16[1040,128]{1,0:T(8,128)(2,1)S(1)}, bf16[1040,128]{1,0:T(8,128)(2,1)S(1)}, u32[]{:S(2)}, u32[]{:S(2)}) collective-permute-start(bf16[1040,128]{1,0:T(8,128)(2,1)S(1)} %concatenate.13), channel_id=1, source_target_pairs={{0,64},{32,96},{64,0},{96,32},{1,65},{33,97},{65,1},{97,33},{2,66}... | collective-permute-start | bytes 798728 | tf_op jit(solution)/shard_map/ppermute | solution.py:295
  52.7 11.7 %collective-permute-start = (bf16[1040,128]{1,0:T(8,128)(2,1)S(1)}, bf16[1040,128]{1,0:T(8,128)(2,1)S(1)}, u32[]{:S(2)}, u32[]{:S(2)}) collective-permute-start(bf16[1040,128]{1,0:T(8,128)(2,1)S(1)} %concatenate.13), channel_id=1, source_target_pairs={{0,32},{32,64},{64,96},{96,0},{1,33},{33,65},{65,97},{97,1},{2,34}... | collective-permute-start | bytes 798728 | tf_op jit(solution)/shard_map/ppermute | solution.py:295
  64.5 26.0 %collective-permute-start.3 = (bf16[4,1040,128]{2,1,0:T(8,128)(2,1)S(1)}, bf16[4,1040,128]{2,1,0:T(8,128)(2,1)S(1)}, u32[]{:S(2)}, u32[]{:S(2)}) collective-permute-start(bf16[4,1040,128]{2,1,0:T(8,128)(2,1)S(1)} %pad_maximum_fusion.own), channel_id=1, source_target_pairs={{0,16},{16,0},{1,17},{17,1},{2,18},{18,2},{3,19},{19,3},{4,20},{20... | collective-permute-start | bytes 3194888 | tf_op jit(solution)/shard_map/ppermute | solution.py:295
  68.7 12.5 %collective-permute-start.4 = (bf16[1024,128]{1,0:T(8,128)(2,1)S(1)}, bf16[1024,128]{1,0:T(8,128)(2,1)S(1)}, u32[]{:S(2)}, u32[]{:S(2)}) collective-permute-start(bf16[1024,128]{1,0:T(8,128)(2,1)S(1)} %pad_maximum_fusion.2.kv0), channel_id=1, source_target_pairs={{0,384},{128,0},{256,128},{384,256},{1,385},{129,1},{257,129},{385... | collective-permute-start | bytes 786440 | tf_op jit(solution)/shard_map/ppermute | solution.py:295
  73.4 17.2 %collective-permute-start.5 = (bf16[1024,128]{1,0:T(8,128)(2,1)S(1)}, bf16[1024,128]{1,0:T(8,128)(2,1)S(1)}, u32[]{:S(2)}, u32[]{:S(2)}) collective-permute-start(bf16[1024,128]{1,0:T(8,128)(2,1)S(1)} %pad_maximum_fusion.2.kv0), channel_id=1, source_target_pairs={{0,128},{128,256},{256,384},{384,0},{1,129},{129,257},{257,385},{3... | collective-permute-start | bytes 786440 | tf_op jit(solution)/shard_map/ppermute | solution.py:295
  75.3 15.2 %collective-permute-start.6 = (bf16[1024,128]{1,0:T(8,128)(2,1)S(1)}, bf16[1024,128]{1,0:T(8,128)(2,1)S(1)}, u32[]{:S(2)}, u32[]{:S(2)}) collective-permute-start(bf16[1024,128]{1,0:T(8,128)(2,1)S(1)} %pad_maximum_fusion.2.kv0), channel_id=1, source_target_pairs={{0,256},{128,384},{256,0},{384,128},{1,257},{129,385},{257,1},{385... | collective-permute-start | bytes 786440 | tf_op jit(solution)/shard_map/ppermute | solution.py:295
  90.5 5.2 %copy-start.1 = (bf16[1024,128]{1,0:T(8,128)(2,1)}, bf16[1024,128]{1,0:T(8,128)(2,1)S(1)}, u32[]{:S(2)}) copy-start(bf16[1024,128]{1,0:T(8,128)(2,1)S(1)} %collective-permute-done.6.kv3) | copy-start | bytes 786436
  96.5 18.1 %all-to-all-start.3 = ((f32[8,8,2,512]{3,2,1,0:T(2,128)}), f32[8,8,2,512]{3,2,1,0:T(2,128)S(1)}, u32[]{:S(2)}, u32[]{:S(2)}) async-start(f32[8,8,2,512]{3,2,1,0:T(2,128)} %broadcast_in_dim.15), calls=%async_computation.3 | async-start | bytes 524288 | tf_op jit(solution)/shard_map/all_to_all | solution.py:341
  106.0 0.9 copy-start.2
  113.6 1.0 copy-start.3
  114.6 37.4 %all-to-all-start.2 = ((bf16[8,512,128]{2,1,0:T(8,128)(2,1)}), bf16[8,512,128]{2,1,0:T(8,128)(2,1)}, u32[]{:S(2)}, u32[]{:S(2)}) async-start(bf16[8,512,128]{2,1,0:T(8,128)(2,1)} %copy-done.3), calls=%async_computation.2 | async-start | bytes 2097152 | tf_op jit(solution)/shard_map/all_to_all | solution.py:355
  127.7 15.4 %collective-permute-start.7 = (bf16[2,512,128]{2,1,0:T(8,128)(2,1)S(1)}, bf16[2,512,128]{2,1,0:T(8,128)(2,1)S(1)}, u32[]{:S(2)}, u32[]{:S(2)}) collective-permute-start(bf16[2,512,128]{2,1,0:T(8,128)(2,1)S(1)} %get-tuple-element.14), channel_id=1, source_target_pairs={{0,384},{128,0},{256,128},{384,256},{1,385},{129,1},{257,129},{385... | collective-permute-start | bytes 786440 | tf_op jit(solution)/shard_map/ppermute | solution.py:295
  129.6 14.2 %collective-permute-start.8 = (bf16[2,512,128]{2,1,0:T(8,128)(2,1)S(1)}, bf16[2,512,128]{2,1,0:T(8,128)(2,1)S(1)}, u32[]{:S(2)}, u32[]{:S(2)}) collective-permute-start(bf16[2,512,128]{2,1,0:T(8,128)(2,1)S(1)} %get-tuple-element.13), channel_id=1, source_target_pairs={{0,256},{128,384},{256,0},{384,128},{1,257},{129,385},{257,1},{385... | collective-permute-start | bytes 786440 | tf_op jit(solution)/shard_map/ppermute | solution.py:295
  139.7 12.2 %collective-permute-start.9 = (bf16[2,512,128]{2,1,0:T(8,128)(2,1)S(1)}, bf16[2,512,128]{2,1,0:T(8,128)(2,1)S(1)}, u32[]{:S(2)}, u32[]{:S(2)}) collective-permute-start(bf16[2,512,128]{2,1,0:T(8,128)(2,1)S(1)} %slice_bitcast_fusion), channel_id=1, source_target_pairs={{0,128},{128,256},{256,384},{384,0},{1,129},{129,257},{257,385},{3... | collective-permute-start | bytes 786440 | tf_op jit(solution)/shard_map/ppermute | solution.py:295
  143.1 0.7 copy-start.4
  143.8 0.7 copy-start.6
  152.0 1.0 copy-start.5
  153.0 0.9 copy-start.7

commit v3 on v2

--- a/solution.py
+++ b/solution.py
@@ -16,23 +16,31 @@
 NQ = NY * NC
 NK = NX
 NPAIR = NQ * NK
+PACKED = 4 * ROWS + 16
 QD_ROWS = 2 * BLK + 16
 UNROLL = 4
 DEPTH = 3
-SHIFTS = (0, 3, 1, 2)
 SCALE = 1.0 / math.sqrt(HD)
 SCALE2 = SCALE * math.log2(math.e)
 LOW = -1e30
-VMEM = 48 * 1024 * 1024
+MIB = 1024 * 1024
 
 
 def dot(a, b, contract):
     return lax.dot_general(a, b, ((contract[:1], contract[1:]), ((), ())), preferred_element_type=jnp.float32)
 
 
+def query_slot(code, meta):
+    return (code & NY) | ((code + meta[1]) & (NY - 1))
+
+
 def query_place(code, meta):
-    slot = code % NQ
-    return ((meta[1] - slot % NY) & (NY - 1)) * NC + (meta[2] ^ (slot // NY))
+    slot = query_slot(code, meta)
+    return (slot & (NY - 1)) * NC + (meta[2] ^ (slot // NY))
+
+
+def fetch_keys(blocks, kv, sems):
+    return [pltpu.make_async_copy(block, kv.at[i], sems.at[i]) for i, block in enumerate(blocks)]
 
 
 def fetch_queries(own, other, qd, sems):
@@ -42,10 +50,6 @@
     ]
 
 
-def fetch_keys(blocks, kv, sems):
-    return [pltpu.make_async_copy(block, kv.at[i], sems.at[i]) for i, block in enumerate(blocks)]
-
-
 def probs_kernel(
     pairs, meta, own, other, kv0, kv1, kv2, kv3, probs, tops, stats, qd, kv, held, sems, key_sems, out_sems
 ):
@@ -72,7 +76,7 @@
         found = []
         for u in range(UNROLL):
             code = pairs[step * UNROLL + u]
-            scores = dot(kv[code // NQ, :BLK, :], qd[code % NQ, :BLK, :], (1, 1))
+            scores = dot(kv[code // NQ, :BLK, :], qd[query_slot(code, meta), :BLK, :], (1, 1))
             if first and u == 0:
                 key_row = lax.broadcasted_iota(jnp.int32, scores.shape, 0)
                 query_row = lax.broadcasted_iota(jnp.int32, scores.shape, 1)
@@ -109,7 +113,7 @@
 
 def dscore_kernel(
     pairs, meta, own, other, kv0, kv1, kv2, kv3, probs, tops, stats, dscore, dquery,
-    qd, kv, keys_t, total, read, held, sems, key_sems, in_sems, out_sems,
+    qd, kv, keys_t, total, read, held, dquery_held, sems, key_sems, in_sems, out_sems, dquery_sems,
 ):
     count = meta[0]
     steps = (count + UNROLL - 1) // UNROLL
@@ -150,7 +154,7 @@
         for u in range(UNROLL):
             t = step * UNROLL + u
             code = pairs[t]
-            place, key, query = query_place(code, meta), code // NQ, code % NQ
+            place, key, query = query_place(code, meta), code // NQ, query_slot(code, meta)
             pieces = qd[query, 2 * BLK :, :].astype(jnp.float32)
             row_dot = pieces[0:4] + pieces[4:8] + pieces[8:12]
             row_dot = jnp.concatenate([row_dot[i : i + 1] for i in range(4)], axis=1)
@@ -163,8 +167,12 @@
         return 0
 
     lax.fori_loop(0, steps, body, 0)
+    sent = [pltpu.make_async_copy(dquery_held.at[i], dquery.at[i], dquery_sems.at[i]) for i in range(NQ)]
     for i in range(NQ):
-        dquery[i] = jnp.transpose(total[i]).astype(jnp.bfloat16)
+        dquery_held[i] = jnp.transpose(total[i]).astype(jnp.bfloat16)
+        sent[i].start()
+    for copy in sent:
+        copy.wait()
     store(steps - 1).wait()
 
     @pl.when(steps >= 2)
@@ -179,8 +187,8 @@
 
 
 def key_kernel(
-    late, pairs, meta, own, other, probs, dscore, tops, stats_all, out,
-    qd, norms, total, p_read, d_read, sems, p_sems, d_sems,
+    late, pairs, meta, own, other, probs, dscore, tops, stats_all, out0, out1,
+    qd, norms, total, held, p_read, d_read, sems, p_sems, d_sems, out_sems,
 ):
     begin, end = (0, meta[3]) if late else (meta[3], meta[0])
     steps = (end - begin + UNROLL - 1) // UNROLL
@@ -219,7 +227,7 @@
         for u in range(UNROLL):
             t = begin + step * UNROLL + u
             code = pairs[jnp.minimum(t, end - 1)]
-            place, key, query = query_place(code, meta), code // NQ, code % NQ
+            place, key, query = query_place(code, meta), code // NQ, query_slot(code, meta)
             weight = jnp.where(t < end, jnp.exp2(tops[jnp.minimum(t, end - 1)] - norms[place]), 0.0)
             weight = jnp.transpose(jnp.broadcast_to(weight, (HD, BLK)))
             queries = (qd[query, :BLK, :].astype(jnp.float32) * (weight * SCALE)).astype(jnp.bfloat16)
@@ -231,10 +239,52 @@
         return 0
 
     lax.fori_loop(0, steps, body, 0)
-    out[...] = total[...].astype(jnp.bfloat16)
-
-
-def finish_kernel(meta, dquery, stats_all, own, first, second, third, out):
+    sent = [pltpu.make_async_copy(held.at[i], out, out_sems.at[i]) for i, out in enumerate((out0, out1))]
+    for i in range(2):
+        held[i] = total[i].astype(jnp.bfloat16)
+        sent[i].start()
+    for copy in sent:
+        copy.wait()
+
+
+def pack_kernel(query, key, value, output, grad, out):
+    lane = lax.broadcasted_iota(jnp.int32, (ROWS, HD), 1)
+    row_dot = jnp.zeros((ROWS, HD), jnp.float32)
+    for h in range(HEADS):
+        part = slice(h * HD, (h + 1) * HD)
+        for i, array in enumerate((query, grad, key, value)):
+            out[h, i * ROWS : (i + 1) * ROWS, :] = array[:, part]
+        products = grad[:, part].astype(jnp.float32) * output[:, part].astype(jnp.float32)
+        row_dot = jnp.where(lane == h, jnp.sum(products, axis=1, keepdims=True), row_dot)
+    row_dot = jnp.concatenate([row_dot, jnp.zeros((HD - ROWS, HD), jnp.float32)], axis=0)
+    row_dot = jnp.transpose(row_dot)[:HEADS]
+    high = row_dot.astype(jnp.bfloat16).astype(jnp.float32)
+    middle = (row_dot - high).astype(jnp.bfloat16).astype(jnp.float32)
+    row = lax.broadcasted_iota(jnp.int32, (HEADS, 16, HD), 1)
+    pieces = jnp.zeros((HEADS, 16, HD), jnp.float32)
+    for i, piece in enumerate((high, middle, row_dot - high - middle)):
+        pieces = jnp.where(row == i, piece[:, None, :], pieces)
+    out[:, 4 * ROWS :, :] = pieces.astype(jnp.bfloat16)
+
+
+def finish_kernel(meta, dquery_in, stats_in, own_in, first, second, third, out, dquery, stats_all, parts, sems):
+    fetches = [
+        pltpu.make_async_copy(source, parts.at[i], sems.at[i])
+        for i, source in enumerate((own_in, first, second, third))
+    ]
+    fetches.append(pltpu.make_async_copy(stats_in, stats_all, sems.at[4]))
+    fetches.append(pltpu.make_async_copy(dquery_in, dquery, sems.at[5]))
+    for fetch in fetches:
+        fetch.start()
+    for fetch in fetches[:4]:
+        fetch.wait()
+    for i in range(2):
+        grad = (parts[0, i].astype(jnp.float32) + parts[1, i].astype(jnp.float32)) + (
+            parts[2, i].astype(jnp.float32) + parts[3, i].astype(jnp.float32)
+        )
+        out[:, (i + 1) * ROWS : (i + 2) * ROWS, :] = grad.astype(jnp.bfloat16).reshape(HEADS, ROWS, HD)
+    for fetch in fetches[4:]:
+        fetch.wait()
     place = meta[1] * NC + meta[2]
     tops, sums = stats_all[:, place, 0, :], stats_all[:, place, 1, :]
     top = jnp.max(tops, axis=0, keepdims=True)
@@ -244,22 +294,17 @@
     for i in range(1, NQ):
         query_grad += dquery[i].astype(jnp.float32) * weight[:, i : i + 1]
     out[:, 0:ROWS, :] = query_grad.astype(jnp.bfloat16).reshape(HEADS, ROWS, HD)
-    for i in range(2):
-        grad = (own[0, i].astype(jnp.float32) + first[i].astype(jnp.float32)) + (
-            second[i].astype(jnp.float32) + third[i].astype(jnp.float32)
-        )
-        out[:, (i + 1) * ROWS : (i + 2) * ROWS, :] = grad.astype(jnp.bfloat16).reshape(HEADS, ROWS, HD)
-
-
-def params():
-    return pltpu.CompilerParams(vmem_limit_bytes=VMEM)
-
-
-def whole(*shape):
-    return pl.BlockSpec(shape, lambda *_: (0,) * len(shape))
-
-
-def over_pairs(kernel, pairs, meta, operands, in_specs, out_specs, out_shape, scratch):
+
+
+def in_hbm(array):
+    return pltpu.with_memory_space_constraint(array, pltpu.HBM)
+
+
+def params(mib):
+    return pltpu.CompilerParams(vmem_limit_bytes=mib * MIB)
+
+
+def over_pairs(kernel, mib, pairs, meta, operands, in_specs, out_specs, out_shape, scratch):
     return pl.pallas_call(
         kernel,
         grid_spec=pltpu.PrefetchScalarGridSpec(
@@ -270,14 +315,14 @@
             scratch_shapes=scratch,
         ),
         out_shape=out_shape,
-        compiler_params=params(),
+        compiler_params=params(mib),
     )(pairs, meta, *operands)
 
 
 def pair_list(key_lists, key_counts, block_order, x, y, c):
     slot = jnp.arange(NQ, dtype=jnp.int32)
-    query_at = x * NQ + ((y - slot % NY) % NY) * NC + (c ^ (slot // NY))
-    key_at = ((x - jnp.array(SHIFTS, jnp.int32)) % NX) * NQ + y * NC + c
+    query_at = x * NQ + ((y + slot) % NY) * NC + (c ^ (slot // NY))
+    key_at = ((x - jnp.arange(NK, dtype=jnp.int32)) % NX) * NQ + y * NC + c
     query_blocks, key_blocks = block_order[query_at], block_order[key_at]
     lists, counts = key_lists[query_blocks], key_counts[query_blocks]
     used = jnp.arange(key_lists.shape[1], dtype=jnp.int32)[None, :] < counts[:, None]
@@ -298,41 +343,39 @@
 def on_device(query_data, key_data, value_data, output_data, output_grad, key_lists, key_counts, block_order):
     x, y, c = lax.axis_index("x"), lax.axis_index("y"), lax.axis_index("c")
 
-    def heads(array):
-        return jnp.transpose(array.reshape(ROWS, HEADS, HD), (1, 0, 2))
-
-    products = output_grad.astype(jnp.float32) * output_data.astype(jnp.float32)
-    row_dot = jnp.transpose(jnp.sum(products.reshape(ROWS, HEADS, HD), axis=2))
-    high = lax.reduce_precision(row_dot, 8, 7)
-    middle = lax.reduce_precision(row_dot - high, 8, 7)
-    pieces = jnp.stack([high, middle, row_dot - high - middle], axis=1).astype(jnp.bfloat16)
-    pieces = jnp.pad(pieces, ((0, 0), (0, 13), (0, HD - ROWS)))
-    def regrouped(*parts):
-        return lax.all_to_all(jnp.concatenate(parts, axis=1), "h", 0, 0, tiled=True)
-
-    def rows(packed, i):
+    bf16, f32 = jnp.bfloat16, jnp.float32
+    shape, vmem = jax.ShapeDtypeStruct, pl.BlockSpec(memory_space=pltpu.VMEM)
+    anywhere = pl.BlockSpec(memory_space=pltpu.HBM)
+    dma = pltpu.SemaphoreType.DMA
+
+    packed = pl.pallas_call(
+        pack_kernel,
+        in_specs=[vmem] * 5,
+        out_specs=vmem,
+        out_shape=shape((HEADS, PACKED, HD), bf16),
+        compiler_params=params(8),
+    )(query_data, key_data, value_data, output_data, output_grad)
+    packed = lax.all_to_all(packed, "h", 0, 0, tiled=True)
+
+    def rows(i):
         return packed[:, i * ROWS : (i + 1) * ROWS, :].reshape(BLK, HD)
 
-    packed = regrouped(heads(query_data), heads(output_grad), pieces)
-    pieces = jnp.transpose(packed[:, 2 * ROWS : 2 * ROWS + 3, :ROWS], (1, 0, 2)).reshape(12, HD)
-    qd = jnp.concatenate([rows(packed, 0), rows(packed, 1), pieces, jnp.zeros((4, HD), jnp.bfloat16)], axis=0)
-    packed = regrouped(heads(key_data), heads(value_data))
-    kv = jnp.concatenate([rows(packed, 0), rows(packed, 1)], axis=0)
+    pieces = jnp.transpose(packed[:, 4 * ROWS : 4 * ROWS + 3, :ROWS], (1, 0, 2)).reshape(12, HD)
+    qd = jnp.concatenate([rows(0), rows(1), pieces, jnp.zeros((4, HD), bf16)], axis=0)
+    kv = jnp.concatenate([rows(2), rows(3)], axis=0)
 
     pairs, count, early = pair_list(key_lists, key_counts, block_order, x, y, c)
     meta = jnp.stack([count, y, c, early]).astype(jnp.int32)
 
-    own = jnp.stack([qd] + [shifted(qd, "y", i, NY) for i in range(1, NY)])
+    own = lax.all_to_all(jnp.broadcast_to(qd[None], (NY, *qd.shape)), "y", 0, 0, tiled=True)
+    keys = (kv, *(shifted(kv, "x", i, NX) for i in range(1, NX)))
+    own, *keys = lax.optimization_barrier((own, *keys))
     queries = (own, shifted(own, "c", 1, NC))
-    keys = tuple(shifted(kv, "x", i, NX) if i else kv for i in SHIFTS)
-
-    bf16, f32 = jnp.bfloat16, jnp.float32
-    shape, anywhere, vmem = jax.ShapeDtypeStruct, pl.BlockSpec(memory_space=pl.ANY), pl.BlockSpec(memory_space=pltpu.VMEM)
-    square, line = shape((NPAIR, BLK, BLK), bf16), shape((NPAIR, 1, BLK), f32)
+
+    square, line = pltpu.HBM((NPAIR, BLK, BLK), bf16), shape((NPAIR, 1, BLK), f32)
     qd_scratch, kv_scratch = pltpu.VMEM((NQ, QD_ROWS, HD), bf16), pltpu.VMEM((NK, 2 * BLK, HD), bf16)
-    dma = pltpu.SemaphoreType.DMA
     probs, tops, stats = over_pairs(
-        probs_kernel, pairs, meta, (*queries, *keys),
+        probs_kernel, 28, pairs, meta, (*queries, *keys),
         [anywhere] * 6,
         [anywhere, vmem, vmem],
         [square, line, shape((NQ, 2, BLK), f32)],
@@ -342,47 +385,52 @@
         jnp.broadcast_to(stats[None], (NQ, NQ, 2, BLK)), ("y", "c"), 0, 0, tiled=True
     )
     dscore, dquery = over_pairs(
-        dscore_kernel, pairs, meta, (*queries, *keys, probs, tops, stats),
+        dscore_kernel, 32, pairs, meta, (*queries, *keys, in_hbm(probs), tops, stats),
         [anywhere] * 7 + [vmem] * 2,
-        [anywhere, vmem],
-        [square, shape((NQ, BLK, HD), bf16)],
+        [anywhere, anywhere],
+        [square, pltpu.HBM((NQ, BLK, HD), bf16)],
         [
             qd_scratch, kv_scratch, pltpu.VMEM((NK, HD, BLK), bf16), pltpu.VMEM((NQ, HD, BLK), f32),
             pltpu.VMEM((2, UNROLL, BLK, BLK), bf16), pltpu.VMEM((2, UNROLL, BLK, BLK), bf16),
-            dma((2,)), dma((NK,)), dma((2,)), dma((2,)),
+            pltpu.VMEM((NQ, BLK, HD), bf16), dma((2,)), dma((NK,)), dma((2,)), dma((2,)), dma((NQ,)),
         ],
     )
     dquery = lax.all_to_all(dquery, ("y", "c"), 0, 0, tiled=True)
 
-    def key_grads(late):
+    def key_grads(late, pairs):
         return over_pairs(
-            functools.partial(key_kernel, late), pairs, meta, (*queries, probs, dscore, tops, stats_all),
+            functools.partial(key_kernel, late), 40, pairs, meta, (*queries, in_hbm(probs), in_hbm(dscore), tops, stats_all),
             [anywhere] * 4 + [vmem] * 2,
-            vmem,
-            shape((2, 2, BLK, HD), bf16),
+            [anywhere] * 2,
+            [pltpu.HBM((2, BLK, HD), bf16)] * 2,
             [
                 qd_scratch, pltpu.VMEM((NQ, 1, BLK), f32), pltpu.VMEM((2, 2, BLK, HD), f32),
+                pltpu.VMEM((2, 2, BLK, HD), bf16),
                 pltpu.VMEM((DEPTH, UNROLL, BLK, BLK), bf16), pltpu.VMEM((DEPTH, UNROLL, BLK, BLK), bf16),
-                dma((2,)), dma((DEPTH, UNROLL)), dma((DEPTH, UNROLL)),
+                dma((2,)), dma((DEPTH, UNROLL)), dma((DEPTH, UNROLL)), dma((2,)),
             ],
         )
 
-    sent_first, sent_last = key_grads(False), key_grads(True)
-    arrived = [shifted(sent_first[i], "x", -SHIFTS[2 + i], NX) for i in range(2)]
-    arrived.append(shifted(sent_last[1], "x", -SHIFTS[1], NX))
-
-    part = whole(2, BLK, HD)
+    second, third = key_grads(False, pairs)
+    second, third, pairs = lax.optimization_barrier((second, third, pairs))
+    kept, first = key_grads(True, pairs)
+    arrived = [shifted(grad, "x", -i - 1, NX) for i, grad in enumerate((first, second, third))]
+
     grads = pl.pallas_call(
         finish_kernel,
         grid_spec=pltpu.PrefetchScalarGridSpec(
             num_scalar_prefetch=1,
             grid=(1,),
-            in_specs=[whole(NQ, BLK, HD), whole(NQ, NQ, 2, BLK), whole(1, 2, BLK, HD), part, part, part],
-            out_specs=whole(HEADS, 3 * ROWS, HD),
+            in_specs=[anywhere] * 6,
+            out_specs=vmem,
+            scratch_shapes=[
+                pltpu.VMEM((NQ, BLK, HD), bf16), pltpu.VMEM((NQ, NQ, 2, BLK), f32),
+                pltpu.VMEM((NK, 2, BLK, HD), bf16), dma((6,)),
+            ],
         ),
         out_shape=shape((HEADS, 3 * ROWS, HD), bf16),
-        compiler_params=params(),
-    )(meta, dquery, stats_all, sent_last, *arrived)
+        compiler_params=params(12),
+    )(meta, dquery, stats_all, in_hbm(kept), in_hbm(arrived[0]), *arrived[1:])
     grads = lax.all_to_all(grads, "h", 0, 0, tiled=True)
 
     def tokens(i):

time: 196 us -> 188 us (0.959)
  the two profiles are of different devices: /device:TPU:16 before, /device:TPU:24 now
where the time goes in v3:
time: 188 us; the launch traced here: 187 us
  blocking collectives  79.1 us (42%)
  starting transfers between devices  38.2 us (20%)
  Pallas kernels  36.3 us (19%)
  waiting for transfers between devices  17.6 us (9%)
  local copies, waits for them, and re-layouts  10.8 us (6%)
  other arithmetic  3.33 us (2%)
    all_to_all x1, blocking collectives, on_device(): packed = lax.all_to_all(packed, 'h', 0, 0, tiled=True)  49.9 us
    pallas_call x4, Pallas kernels, over_pairs(): pl.pallas_call(kernel, grid_spec=pltpu.PrefetchScalarGridSpec(num_scalar_...  33.4 us
    all_to_all x1, blocking collectives, on_device(): grads = lax.all_to_all(grads, 'h', 0, 0, tiled=True)  29.1 us
    ppermute x7, starting transfers between devices, shifted(): lax.ppermute(array, axis, [(i, (i + by) % size) for i in range(size)])  21.1 us
    ppermute x7, waiting for transfers between devices, shifted(): lax.ppermute(array, axis, [(i, (i + by) % size) for i in range(size)])  17.6 us
    all_to_all x1, starting transfers between devices, on_device(): dquery = lax.all_to_all(dquery, ('y', 'c'), 0, 0, tiled=True)  6.27 us
    all_to_all x1, starting transfers between devices, on_device(): lax.all_to_all(jnp.broadcast_to(stats[None], (NQ, NQ, 2, BLK)), ('y', 'c'...  6.24 us
    all_to_all x1, starting transfers between devices, on_device(): lax.all_to_all(jnp.broadcast_to(qd[None], (NY, *qd.shape)), 'y', 0, 0, ti...  4.68 us
  transfers between devices with their start and end apart: 10, of which 5 were waited for; matrix products, arithmetic and copies ran while one was open for 3% of the time, Pallas kernels for 13%

profile of v3, /device:TPU:24, one launch (start us, length us, event | category | flops | bytes accessed | tf_op | source)
XLA Modules:
  0.0 186.9 jit_solution(859466443803588311)
XLA Ops:
  0.6 0.0 copy-start
  0.6 0.0 copy-start.1
  0.7 0.9 copy-done.1
  1.6 0.0 copy-start.2
  1.6 0.9 copy-done.2
  2.5 0.0 copy-start.3
  2.5 0.9 copy-done.3
  3.4 0.9 copy-done.4
  4.3 0.9 copy-done.5
  5.2 0.3 shard_map.103
  5.4 49.9 %all_to_all.25 = bf16[16,144,128]{2,1,0:T(8,128)(2,1)S(1)} all-to-all(bf16[16,144,128]{2,1,0:T(8,128)(2,1)S(1)} %shard_map.103), channel_id=1, replica_groups=mesh['x'=4,'y'=4,'c'=2,'h'=16] {'h'}, dimensions={0} | all-to-all | bytes 1179648 | tf_op jit(solution)/shard_map/all_to_all | solution.py:358
  55.4 0.1 reshape.227
  55.5 0.1 concatenate.6
  55.6 1.1 broadcast_in_dim.14
  56.8 4.7 %all-to-all-start.1 = ((bf16[4,1040,128]{2,1,0:T(8,128)(2,1)}), bf16[4,1040,128]{2,1,0:T(8,128)(2,1)S(1)}, u32[]{:S(2)}, u32[]{:S(2)}) async-start(bf16[4,1040,128]{2,1,0:T(8,128)(2,1)} %broadcast_in_dim.14), calls=%async_computation.1 | async-start | bytes 2129920 | tf_op jit(solution)/shard_map/all_to_all | solution.py:370
  61.5 0.0 copy-done
  61.5 0.6 gather_fusion
  62.2 3.4 %collective-permute-start = (bf16[1024,128]{1,0:T(8,128)(2,1)S(1)}, bf16[1024,128]{1,0:T(8,128)(2,1)S(1)}, u32[]{:S(2)}, u32[]{:S(2)}) collective-permute-start(bf16[1024,128]{1,0:T(8,128)(2,1)S(1)} %pad_maximum_fusion.kv0), channel_id=1, source_target_pairs={{0,128},{128,256},{256,384},{384,0},{1,129},{129,257},{257,385},{3... | collective-permute-start | bytes 786440 | tf_op jit(solution)/shard_map/ppermute | solution.py:340
  65.6 4.6 %collective-permute-start.1 = (bf16[1024,128]{1,0:T(8,128)(2,1)S(1)}, bf16[1024,128]{1,0:T(8,128)(2,1)S(1)}, u32[]{:S(2)}, u32[]{:S(2)}) collective-permute-start(bf16[1024,128]{1,0:T(8,128)(2,1)S(1)} %pad_maximum_fusion.kv0), channel_id=1, source_target_pairs={{0,256},{128,384},{256,0},{384,128},{1,257},{129,385},{257,1},{385... | collective-permute-start | bytes 786440 | tf_op jit(solution)/shard_map/ppermute | solution.py:340
  70.2 3.3 %collective-permute-start.2 = (bf16[1024,128]{1,0:T(8,128)(2,1)S(1)}, bf16[1024,128]{1,0:T(8,128)(2,1)S(1)}, u32[]{:S(2)}, u32[]{:S(2)}) collective-permute-start(bf16[1024,128]{1,0:T(8,128)(2,1)S(1)} %pad_maximum_fusion.kv0), channel_id=1, source_target_pairs={{0,384},{128,0},{256,128},{384,256},{1,385},{129,1},{257,129},{385... | collective-permute-start | bytes 786440 | tf_op jit(solution)/shard_map/ppermute | solution.py:340
  73.6 0.0 collective-permute-done.kv1
  73.6 2.8 %collective-permute-done.1.kv2 = bf16[1024,128]{1,0:T(8,128)(2,1)S(1)} collective-permute-done((bf16[1024,128]{1,0:T(8,128)(2,1)S(1)}, bf16[1024,128]{1,0:T(8,128)(2,1)S(1)}, u32[]{:S(2)}, u32[]{:S(2)}) %collective-permute-start.1) | collective-permute-done | bytes 262176 | tf_op jit(solution)/shard_map/ppermute | solution.py:340
  76.4 2.5 %collective-permute-done.2.kv3 = bf16[1024,128]{1,0:T(8,128)(2,1)S(1)} collective-permute-done((bf16[1024,128]{1,0:T(8,128)(2,1)S(1)}, bf16[1024,128]{1,0:T(8,128)(2,1)S(1)}, u32[]{:S(2)}, u32[]{:S(2)}) %collective-permute-start.2) | collective-permute-done | bytes 262176 | tf_op jit(solution)/shard_map/ppermute | solution.py:340
  78.9 0.0 all-to-all-done.1.own
  78.9 1.9 %collective-permute-start.3 = (bf16[4,1040,128]{2,1,0:T(8,128)(2,1)S(1)}, bf16[4,1040,128]{2,1,0:T(8,128)(2,1)S(1)}, u32[]{:S(2)}, u32[]{:S(2)}) collective-permute-start(bf16[4,1040,128]{2,1,0:T(8,128)(2,1)S(1)} %all-to-all-done.1.own), channel_id=1, source_target_pairs={{0,16},{16,0},{1,17},{17,1},{2,18},{18,2},{3,19},{19,3},{4,20},{20... | collective-permute-start | bytes 3194888 | tf_op jit(solution)/shard_map/ppermute | solution.py:340
  80.8 0.0 copy-done.8
  80.8 0.1 copy.17
  80.9 0.6 gather_fusion.2
  81.6 0.6 gather_fusion.1
  82.1 0.0 copy-done.6
  82.1 0.6 gather_fusion.3
  82.8 0.1 iota_compare_fusion.1
  82.9 0.2 and_reduce_fusion
  83.1 0.1 and.87
  83.2 0.7 convert_reduce_fusion.1
  84.5 0.6 fusion.1
  85.1 1.4 pad_add_fusion.meta
  86.5 0.1 convert_reduce_fusion
  86.6 0.2 select_reduce_fusion.pairs
  86.8 0.0 collective-permute-done.3.other
  86.8 8.4 %shard_map.104 = (bf16[32,512,512]{2,1,0:T(8,128)(2,1)}, f32[32,1,512]{2,1,0:T(1,128)S(1)}, f32[8,2,512]{2,1,0:T(2,128)S(1)}) custom-call(s32[32]{0:T(128)S(1)} %select_reduce_fusion.pairs, s32[4]{0:T(128)S(1)} %pad_add_fusion.meta, bf16[4,1040,128]{2,1,0:T(8,128)(2,1)S(1)} %all-to-all-done.1.own, bf16[4,1040,128]{2,1,0:T(8,128)(2,1)S(1)} %collective-permute-done.3.other, ...), custom_call_target="tpu_custom_call" | custom-call | tf_op jit(solution)/shard_map/pallas_call | solution.py:308
  95.2 0.8 broadcast_in_dim.15
  96.0 6.2 %all-to-all-start.3 = ((f32[8,8,2,512]{3,2,1,0:T(2,128)}), f32[8,8,2,512]{3,2,1,0:T(2,128)S(1)}, u32[]{:S(2)}, u32[]{:S(2)}) async-start(f32[8,8,2,512]{3,2,1,0:T(2,128)} %broadcast_in_dim.15), calls=%async_computation.3 | async-start | bytes 524288 | tf_op jit(solution)/shard_map/all_to_all | solution.py:384
  102.2 10.8 %shard_map.105 = (bf16[32,512,512]{2,1,0:T(8,128)(2,1)}, bf16[8,512,128]{2,1,0:T(8,128)(2,1)}) custom-call(s32[32]{0:T(128)S(1)} %select_reduce_fusion.pairs, s32[4]{0:T(128)S(1)} %pad_add_fusion.meta, bf16[4,1040,128]{2,1,0:T(8,128)(2,1)S(1)} %all-to-all-done.1.own, bf16[4,1040,128]{2,1,0:T(8,128)(2,1)S(1)} %collective-permute-done.3.other, ...), custom_call_target="tpu_custom_call" | custom-call | tf_op jit(solution)/shard_map/pallas_call | solution.py:308
  113.0 0.0 all-to-all-done.3.stats_all.stats_in
  113.0 6.3 %all-to-all-start.2 = ((bf16[8,512,128]{2,1,0:T(8,128)(2,1)}), bf16[8,512,128]{2,1,0:T(8,128)(2,1)S(1)}, u32[]{:S(2)}, u32[]{:S(2)}) async-start(bf16[8,512,128]{2,1,0:T(8,128)(2,1)} %get-tuple-element.28), calls=%async_computation.2 | async-start | bytes 2097152 | tf_op jit(solution)/shard_map/all_to_all | solution.py:398
  119.3 7.4 %shard_map.106 = (bf16[2,512,128]{2,1,0:T(8,128)(2,1)}, bf16[2,512,128]{2,1,0:T(8,128)(2,1)}) custom-call(s32[32]{0:T(128)S(1)} %select_reduce_fusion.pairs, s32[4]{0:T(128)S(1)} %pad_add_fusion.meta, bf16[4,1040,128]{2,1,0:T(8,128)(2,1)S(1)} %all-to-all-done.1.own, bf16[4,1040,128]{2,1,0:T(8,128)(2,1)S(1)} %collective-permute-done.3.other, ...), custom_call_target="tpu_custom_call" | custom-call | tf_op jit(solution)/shard_map/pallas_call | solution.py:308
  126.8 0.0 copy-start.10
  126.8 0.0 copy-start.9
  126.8 6.8 %shard_map.107 = (bf16[2,512,128]{2,1,0:T(8,128)(2,1)}, bf16[2,512,128]{2,1,0:T(8,128)(2,1)}) custom-call(s32[32]{0:T(128)S(1)} %select_reduce_fusion.pairs, s32[4]{0:T(128)S(1)} %pad_add_fusion.meta, bf16[4,1040,128]{2,1,0:T(8,128)(2,1)S(1)} %all-to-all-done.1.own, bf16[4,1040,128]{2,1,0:T(8,128)(2,1)S(1)} %collective-permute-done.3.other, ...), custom_call_target="tpu_custom_call" | custom-call | tf_op jit(solution)/shard_map/pallas_call | solution.py:308
  133.6 1.9 %collective-permute-start.4 = (bf16[2,512,128]{2,1,0:T(8,128)(2,1)}, bf16[2,512,128]{2,1,0:T(8,128)(2,1)S(1)}, u32[]{:S(2)}, u32[]{:S(2)}) collective-permute-start(bf16[2,512,128]{2,1,0:T(8,128)(2,1)} %get-tuple-element.34), channel_id=1, source_target_pairs={{0,384},{128,0},{256,128},{384,256},{1,385},{129,1},{257,129},{385... | collective-permute-start | bytes 786440 | tf_op jit(solution)/shard_map/ppermute | solution.py:340
  135.5 0.0 copy-done.10
  135.5 1.9 %collective-permute-start.5 = (bf16[2,512,128]{2,1,0:T(8,128)(2,1)S(1)}, bf16[2,512,128]{2,1,0:T(8,128)(2,1)S(1)}, u32[]{:S(2)}, u32[]{:S(2)}) collective-permute-start(bf16[2,512,128]{2,1,0:T(8,128)(2,1)S(1)} %copy-done.10), channel_id=1, source_target_pairs={{0,256},{128,384},{256,0},{384,128},{1,257},{129,385},{257,1},{385... | collective-permute-start | bytes 786440 | tf_op jit(solution)/shard_map/ppermute | solution.py:340
  137.4 0.0 copy-done.9
  137.4 3.9 %collective-permute-start.6 = (bf16[2,512,128]{2,1,0:T(8,128)(2,1)S(1)}, bf16[2,512,128]{2,1,0:T(8,128)(2,1)S(1)}, u32[]{:S(2)}, u32[]{:S(2)}) collective-permute-start(bf16[2,512,128]{2,1,0:T(8,128)(2,1)S(1)} %copy-done.9), channel_id=1, source_target_pairs={{0,128},{128,256},{256,384},{384,0},{1,129},{129,257},{257,385},{3... | collective-permute-start | bytes 786440 | tf_op jit(solution)/shard_map/ppermute | solution.py:340
  141.4 3.2 %collective-permute-done.4.first = bf16[2,512,128]{2,1,0:T(8,128)(2,1)S(1)} collective-permute-done((bf16[2,512,128]{2,1,0:T(8,128)(2,1)}, bf16[2,512,128]{2,1,0:T(8,128)(2,1)S(1)}, u32[]{:S(2)}, u32[]{:S(2)}) %collective-permute-start.4) | collective-permute-done | bytes 262176 | tf_op jit(solution)/shard_map/ppermute | solution.py:340
  144.6 3.3 %collective-permute-done.5.second = bf16[2,512,128]{2,1,0:T(8,128)(2,1)S(1)} collective-permute-done((bf16[2,512,128]{2,1,0:T(8,128)(2,1)S(1)}, bf16[2,512,128]{2,1,0:T(8,128)(2,1)S(1)}, u32[]{:S(2)}, u32[]{:S(2)}) %collective-permute-start.5) | collective-permute-done | bytes 262176 | tf_op jit(solution)/shard_map/ppermute | solution.py:340
  147.9 5.7 %collective-permute-done.6.third = bf16[2,512,128]{2,1,0:T(8,128)(2,1)S(1)} collective-permute-done((bf16[2,512,128]{2,1,0:T(8,128)(2,1)S(1)}, bf16[2,512,128]{2,1,0:T(8,128)(2,1)S(1)}, u32[]{:S(2)}, u32[]{:S(2)}) %collective-permute-start.6) | collective-permute-done | bytes 262176 | tf_op jit(solution)/shard_map/ppermute | solution.py:340
  153.7 0.0 all-to-all-done.2.dquery_in
  153.7 0.0 copy-done.7
  153.7 2.6 %shard_map.108 = bf16[16,96,128]{2,1,0:T(8,128)(2,1)S(1)} custom-call(s32[4]{0:T(128)S(1)} %pad_add_fusion.meta, bf16[8,512,128]{2,1,0:T(8,128)(2,1)S(1)} %all-to-all-done.2.dquery_in, f32[8,8,2,512]{3,2,1,0:T(2,128)S(1)} %all-to-all-done.3.stats_all.stats_in, bf16[2,512,128]{2,1,0:T(8,128)(2,1)} %get-tuple-element.33.own_in, ...), custom_call_target="tpu_custom_call" | custom-call | tf_op jit(solution)/shard_map/pallas_call | solution.py:419
  156.3 29.1 %all_to_all.26 = bf16[16,96,128]{2,1,0:T(8,128)(2,1)S(1)} all-to-all(bf16[16,96,128]{2,1,0:T(8,128)(2,1)S(1)} %shard_map.108), channel_id=1, replica_groups=mesh['x'=4,'y'=4,'c'=2,'h'=16] {'h'}, dimensions={0} | all-to-all | bytes 786432 | tf_op jit(solution)/shard_map/all_to_all | solution.py:434
  185.5 0.7 copy.28
  186.2 0.7 copy_bitcast_fusion
  (18 shorter events, 0.2 us)
Async XLA Ops:
  0.6 60.9 %copy-start = (s32[32]{0:T(128)S(1)}, s32[32]{0:T(128)}, u32[]{:S(2)}) copy-start(s32[32]{0:T(128)} %param.15) | copy-start | bytes 388
  0.6 0.9 copy-start.1
  1.6 0.9 copy-start.2
  2.5 0.9 copy-start.3
  3.4 0.9 copy-start.4
  4.3 0.9 copy-start.5
  56.8 22.1 %all-to-all-start.1 = ((bf16[4,1040,128]{2,1,0:T(8,128)(2,1)}), bf16[4,1040,128]{2,1,0:T(8,128)(2,1)S(1)}, u32[]{:S(2)}, u32[]{:S(2)}) async-start(bf16[4,1040,128]{2,1,0:T(8,128)(2,1)} %broadcast_in_dim.14), calls=%async_computation.1 | async-start | bytes 2129920 | tf_op jit(solution)/shard_map/all_to_all | solution.py:370
  61.4 19.4 %copy-start.8 = (s32[32,16]{0,1:T(8,128)S(1)}, s32[32,16]{0,1:T(8,128)}, u32[]{:S(2)}) copy-start(s32[32,16]{0,1:T(8,128)} %param.13) | copy-start | bytes 6148
  61.5 20.7 %copy-start.6 = (s32[32]{0:T(128)S(1)}, s32[32]{0:T(128)}, u32[]{:S(2)}) copy-start(s32[32]{0:T(128)} %param.14) | copy-start | bytes 388
  62.2 11.5 %collective-permute-start = (bf16[1024,128]{1,0:T(8,128)(2,1)S(1)}, bf16[1024,128]{1,0:T(8,128)(2,1)S(1)}, u32[]{:S(2)}, u32[]{:S(2)}) collective-permute-start(bf16[1024,128]{1,0:T(8,128)(2,1)S(1)} %pad_maximum_fusion.kv0), channel_id=1, source_target_pairs={{0,128},{128,256},{256,384},{384,0},{1,129},{129,257},{257,385},{3... | collective-permute-start | bytes 786440 | tf_op jit(solution)/shard_map/ppermute | solution.py:340
  65.6 10.8 %collective-permute-start.1 = (bf16[1024,128]{1,0:T(8,128)(2,1)S(1)}, bf16[1024,128]{1,0:T(8,128)(2,1)S(1)}, u32[]{:S(2)}, u32[]{:S(2)}) collective-permute-start(bf16[1024,128]{1,0:T(8,128)(2,1)S(1)} %pad_maximum_fusion.kv0), channel_id=1, source_target_pairs={{0,256},{128,384},{256,0},{384,128},{1,257},{129,385},{257,1},{385... | collective-permute-start | bytes 786440 | tf_op jit(solution)/shard_map/ppermute | solution.py:340
  70.2 8.7 %collective-permute-start.2 = (bf16[1024,128]{1,0:T(8,128)(2,1)S(1)}, bf16[1024,128]{1,0:T(8,128)(2,1)S(1)}, u32[]{:S(2)}, u32[]{:S(2)}) collective-permute-start(bf16[1024,128]{1,0:T(8,128)(2,1)S(1)} %pad_maximum_fusion.kv0), channel_id=1, source_target_pairs={{0,384},{128,0},{256,128},{384,256},{1,385},{129,1},{257,129},{385... | collective-permute-start | bytes 786440 | tf_op jit(solution)/shard_map/ppermute | solution.py:340
  78.9 7.9 %collective-permute-start.3 = (bf16[4,1040,128]{2,1,0:T(8,128)(2,1)S(1)}, bf16[4,1040,128]{2,1,0:T(8,128)(2,1)S(1)}, u32[]{:S(2)}, u32[]{:S(2)}) collective-permute-start(bf16[4,1040,128]{2,1,0:T(8,128)(2,1)S(1)} %all-to-all-done.1.own), channel_id=1, source_target_pairs={{0,16},{16,0},{1,17},{17,1},{2,18},{18,2},{3,19},{19,3},{4,20},{20... | collective-permute-start | bytes 3194888 | tf_op jit(solution)/shard_map/ppermute | solution.py:340
  96.0 17.1 %all-to-all-start.3 = ((f32[8,8,2,512]{3,2,1,0:T(2,128)}), f32[8,8,2,512]{3,2,1,0:T(2,128)S(1)}, u32[]{:S(2)}, u32[]{:S(2)}) async-start(f32[8,8,2,512]{3,2,1,0:T(2,128)} %broadcast_in_dim.15), calls=%async_computation.3 | async-start | bytes 524288 | tf_op jit(solution)/shard_map/all_to_all | solution.py:384
  113.0 40.6 %all-to-all-start.2 = ((bf16[8,512,128]{2,1,0:T(8,128)(2,1)}), bf16[8,512,128]{2,1,0:T(8,128)(2,1)S(1)}, u32[]{:S(2)}, u32[]{:S(2)}) async-start(bf16[8,512,128]{2,1,0:T(8,128)(2,1)} %get-tuple-element.28), calls=%async_computation.2 | async-start | bytes 2097152 | tf_op jit(solution)/shard_map/all_to_all | solution.py:398
  126.8 8.7 %copy-start.10 = (bf16[2,512,128]{2,1,0:T(8,128)(2,1)S(1)}, bf16[2,512,128]{2,1,0:T(8,128)(2,1)}, u32[]{:S(2)}) copy-start(bf16[2,512,128]{2,1,0:T(8,128)(2,1)} %get-tuple-element.35) | copy-start | bytes 786436
  126.8 10.6 %copy-start.9 = (bf16[2,512,128]{2,1,0:T(8,128)(2,1)S(1)}, bf16[2,512,128]{2,1,0:T(8,128)(2,1)}, u32[]{:S(2)}) copy-start(bf16[2,512,128]{2,1,0:T(8,128)(2,1)} %get-tuple-element.36) | copy-start | bytes 786436
  133.6 11.0 %collective-permute-start.4 = (bf16[2,512,128]{2,1,0:T(8,128)(2,1)}, bf16[2,512,128]{2,1,0:T(8,128)(2,1)S(1)}, u32[]{:S(2)}, u32[]{:S(2)}) collective-permute-start(bf16[2,512,128]{2,1,0:T(8,128)(2,1)} %get-tuple-element.34), channel_id=1, source_target_pairs={{0,384},{128,0},{256,128},{384,256},{1,385},{129,1},{257,129},{385... | collective-permute-start | bytes 786440 | tf_op jit(solution)/shard_map/ppermute | solution.py:340
  135.5 12.4 %collective-permute-start.5 = (bf16[2,512,128]{2,1,0:T(8,128)(2,1)S(1)}, bf16[2,512,128]{2,1,0:T(8,128)(2,1)S(1)}, u32[]{:S(2)}, u32[]{:S(2)}) collective-permute-start(bf16[2,512,128]{2,1,0:T(8,128)(2,1)S(1)} %copy-done.10), channel_id=1, source_target_pairs={{0,256},{128,384},{256,0},{384,128},{1,257},{129,385},{257,1},{385... | collective-permute-start | bytes 786440 | tf_op jit(solution)/shard_map/ppermute | solution.py:340
  137.4 16.3 %collective-permute-start.6 = (bf16[2,512,128]{2,1,0:T(8,128)(2,1)S(1)}, bf16[2,512,128]{2,1,0:T(8,128)(2,1)S(1)}, u32[]{:S(2)}, u32[]{:S(2)}) collective-permute-start(bf16[2,512,128]{2,1,0:T(8,128)(2,1)S(1)} %copy-done.9), channel_id=1, source_target_pairs={{0,128},{128,256},{256,384},{384,0},{1,129},{129,257},{257,385},{3... | collective-permute-start | bytes 786440 | tf_op jit(solution)/shard_map/ppermute | solution.py:340
  144.6 9.1 %copy-start.7 = (bf16[2,512,128]{2,1,0:T(8,128)(2,1)}, bf16[2,512,128]{2,1,0:T(8,128)(2,1)S(1)}, u32[]{:S(2)}) copy-start(bf16[2,512,128]{2,1,0:T(8,128)(2,1)S(1)} %collective-permute-done.4.first) | copy-start | bytes 786436

commit v4 on v3

--- a/solution.py
+++ b/solution.py
@@ -19,7 +19,6 @@
 PACKED = 4 * ROWS + 16
 QD_ROWS = 2 * BLK + 16
 UNROLL = 4
-DEPTH = 3
 SCALE = 1.0 / math.sqrt(HD)
 SCALE2 = SCALE * math.log2(math.e)
 LOW = -1e30
@@ -51,7 +50,7 @@
 
 
 def probs_kernel(
-    pairs, meta, own, other, kv0, kv1, kv2, kv3, probs, tops, stats, qd, kv, held, sems, key_sems, out_sems
+    pairs, meta, own, other, kv0, kv1, kv2, kv3, probs, tops, copies, qd, kv, stats, held, sems, key_sems, out_sems, copy_sems
 ):
     fetches = fetch_queries(own, other, qd, sems) + fetch_keys((kv0, kv1, kv2, kv3), kv, key_sems)
     for fetch in fetches:
@@ -71,7 +70,7 @@
     def visit(step, first):
         @pl.when(step >= 2)
         def _():
-            store(step).wait()
+            store(step - 2).wait()
 
         found = []
         for u in range(UNROLL):
@@ -104,6 +103,11 @@
         return 0
 
     lax.fori_loop(1, steps, body, 0)
+    sent = [pltpu.make_async_copy(stats, copies.at[i], copy_sems.at[i]) for i in range(NQ)]
+    for copy in sent:
+        copy.start()
+    for copy in sent:
+        copy.wait()
     store(steps - 1).wait()
 
     @pl.when(steps >= 2)
@@ -112,16 +116,15 @@
 
 
 def dscore_kernel(
-    pairs, meta, own, other, kv0, kv1, kv2, kv3, probs, tops, stats, dscore, dquery,
-    qd, kv, keys_t, total, read, held, dquery_held, sems, key_sems, in_sems, out_sems, dquery_sems,
+    pairs, meta, own, other, kv0, kv1, kv2, kv3, probs_in, stats_in, tops, dscore, dquery,
+    qd, kv, keys_t, total, stats, probs, held, dquery_held, sems, key_sems, in_sems, out_sems, dquery_sems,
 ):
     count = meta[0]
     steps = (count + UNROLL - 1) // UNROLL
 
     def load(step):
-        return pltpu.make_async_copy(
-            probs.at[pl.ds(step * UNROLL, UNROLL)], read.at[step & 1], in_sems.at[step & 1]
-        )
+        span = pl.ds(step * UNROLL, UNROLL)
+        return pltpu.make_async_copy(probs_in.at[span], probs.at[span], in_sems.at[step])
 
     def store(step):
         return pltpu.make_async_copy(
@@ -130,9 +133,15 @@
 
     key_fetches = fetch_keys((kv0, kv1, kv2, kv3), kv, key_sems)
     fetches = fetch_queries(own, other, qd, sems)
+    fetches.append(pltpu.make_async_copy(stats_in.at[0], stats, sems.at[2]))
     for fetch in key_fetches + fetches:
         fetch.start()
-    load(0).start()
+
+    def start(step, _):
+        load(step).start()
+        return 0
+
+    lax.fori_loop(0, steps, start, 0)
     total[...] = jnp.zeros_like(total)
     for i, fetch in enumerate(key_fetches):
         fetch.wait()
@@ -143,14 +152,11 @@
     def body(step, _):
         load(step).wait()
 
-        @pl.when(step + 1 < steps)
-        def _():
-            load(step + 1).start()
-
         @pl.when(step >= 2)
         def _():
-            store(step).wait()
-
+            store(step - 2).wait()
+
+        found = []
         for u in range(UNROLL):
             t = step * UNROLL + u
             code = pairs[t]
@@ -160,9 +166,11 @@
             row_dot = jnp.concatenate([row_dot[i : i + 1] for i in range(4)], axis=1)
             weight = jnp.where(t < count, jnp.exp2(tops[t] - stats[place, 0:1, :]), 0.0)
             dprob = dot(kv[key, BLK:, :], qd[query, BLK : 2 * BLK, :], (1, 1))
-            low = (read[step & 1, u].astype(jnp.float32) * (dprob - row_dot)).astype(jnp.bfloat16)
+            low = (probs[t].astype(jnp.float32) * (dprob - row_dot)).astype(jnp.bfloat16)
             held[step & 1, u] = low
-            total[place] += dot(keys_t[key], low, (1, 0)) * weight
+            found.append((place, dot(keys_t[key], low, (1, 0)) * weight))
+        for place, part in found:
+            total[place] += part
         store(step).start()
         return 0
 
@@ -186,68 +194,69 @@
     return top + jnp.log2(jnp.sum(sums * jnp.exp2(tops - top[None]), axis=0))
 
 
-def key_kernel(
-    late, pairs, meta, own, other, probs, dscore, tops, stats_all, out0, out1,
-    qd, norms, total, held, p_read, d_read, sems, p_sems, d_sems, out_sems,
-):
-    begin, end = (0, meta[3]) if late else (meta[3], meta[0])
-    steps = (end - begin + UNROLL - 1) // UNROLL
+def key_kernel(pairs, meta, own, other, probs_in, dscore_in, tops, stats_all, *rest):
+    *outs, qd, norms, total, kept, probs, dscore, sems, probs_sems, dscore_sems = rest
+    count = meta[0]
+    steps = (count + UNROLL - 1) // UNROLL
 
     def loads(step):
-        slot = lax.rem(step, DEPTH)
-        copies = []
-        for u in range(UNROLL):
-            t = jnp.minimum(begin + step * UNROLL + u, end - 1)
-            copies.append(pltpu.make_async_copy(probs.at[t], p_read.at[slot, u], p_sems.at[slot, u]))
-            copies.append(pltpu.make_async_copy(dscore.at[t], d_read.at[slot, u], d_sems.at[slot, u]))
-        return copies
-
-    def prefetch(step):
-        @pl.when(step < steps)
-        def _():
-            for copy in loads(step):
-                copy.start()
+        span = pl.ds(step * UNROLL, UNROLL)
+        return (
+            pltpu.make_async_copy(dscore_in.at[span], dscore.at[span], dscore_sems.at[step]),
+            pltpu.make_async_copy(probs_in.at[span], probs.at[span], probs_sems.at[step]),
+        )
+
+    def start(step, _):
+        for copy in loads(step):
+            copy.start()
+        return 0
 
     fetches = fetch_queries(own, other, qd, sems)
     for fetch in fetches:
         fetch.start()
-    for step in range(DEPTH - 1):
-        prefetch(step)
+    lax.fori_loop(0, steps, start, 0)
     total[...] = jnp.zeros_like(total)
     norms[:, 0, :] = log_norms(stats_all[...])
     for fetch in fetches:
         fetch.wait()
 
     def body(step, _):
-        slot = lax.rem(step, DEPTH)
         for copy in loads(step):
             copy.wait()
-        prefetch(step + DEPTH - 1)
         found = []
         for u in range(UNROLL):
-            t = begin + step * UNROLL + u
-            code = pairs[jnp.minimum(t, end - 1)]
+            t = step * UNROLL + u
+            code = pairs[t]
             place, key, query = query_place(code, meta), code // NQ, query_slot(code, meta)
-            weight = jnp.where(t < end, jnp.exp2(tops[jnp.minimum(t, end - 1)] - norms[place]), 0.0)
+            weight = jnp.where(t < count, jnp.exp2(tops[t] - norms[place]), 0.0)
             weight = jnp.transpose(jnp.broadcast_to(weight, (HD, BLK)))
             queries = (qd[query, :BLK, :].astype(jnp.float32) * (weight * SCALE)).astype(jnp.bfloat16)
             grads = (qd[query, BLK : 2 * BLK, :].astype(jnp.float32) * weight).astype(jnp.bfloat16)
-            found.append((key & 1, dot(d_read[slot, u], queries, (1, 0)), dot(p_read[slot, u], grads, (1, 0))))
+            found.append((key, dot(dscore[t], queries, (1, 0)), dot(probs[t], grads, (1, 0))))
         for key, key_part, value_part in found:
             total[key, 0] += key_part
             total[key, 1] += value_part
         return 0
 
     lax.fori_loop(0, steps, body, 0)
-    sent = [pltpu.make_async_copy(held.at[i], out, out_sems.at[i]) for i, out in enumerate((out0, out1))]
-    for i in range(2):
-        held[i] = total[i].astype(jnp.bfloat16)
-        sent[i].start()
-    for copy in sent:
-        copy.wait()
-
-
-def pack_kernel(query, key, value, output, grad, out):
+    kept[...] = total[0].astype(jnp.bfloat16)
+    sent = pltpu.make_async_copy(kept, outs[0], sems.at[2])
+    sent.start()
+    for i, out in enumerate(outs[1:]):
+        out[...] = total[i + 1].astype(jnp.bfloat16)
+    sent.wait()
+
+
+def pack_kernel(query_in, key_in, value_in, output_in, grad_in, out, held, sems):
+    fetches = [
+        pltpu.make_async_copy(source, held.at[i], sems.at[i])
+        for i, source in enumerate((query_in, key_in, value_in, output_in, grad_in))
+    ]
+    for fetch in fetches:
+        fetch.start()
+    for fetch in fetches:
+        fetch.wait()
+    query, key, value, output, grad = (held.at[i] for i in range(5))
     lane = lax.broadcasted_iota(jnp.int32, (ROWS, HD), 1)
     row_dot = jnp.zeros((ROWS, HD), jnp.float32)
     for h in range(HEADS):
@@ -333,7 +342,7 @@
     count = jnp.sum(named.astype(jnp.int32))
     wanted = jnp.minimum(code, count - 1)
     pairs = jnp.sum(jnp.where(named[None, :] & (rank[None, :] == wanted[:, None]), code[None, :], 0), axis=1)
-    return pairs.astype(jnp.int32), count, jnp.sum(named[: 2 * NQ].astype(jnp.int32))
+    return pairs.astype(jnp.int32), count
 
 
 def shifted(array, axis, by, size):
@@ -350,12 +359,16 @@
 
     packed = pl.pallas_call(
         pack_kernel,
-        in_specs=[vmem] * 5,
+        in_specs=[anywhere] * 5,
         out_specs=vmem,
         out_shape=shape((HEADS, PACKED, HD), bf16),
+        scratch_shapes=[pltpu.VMEM((5, ROWS, HEADS * HD), bf16), dma((5,))],
         compiler_params=params(8),
-    )(query_data, key_data, value_data, output_data, output_grad)
+    )(*(in_hbm(array) for array in (query_data, key_data, value_data, output_data, output_grad)))
     packed = lax.all_to_all(packed, "h", 0, 0, tiled=True)
+    pairs, count = pair_list(key_lists, key_counts, block_order, x, y, c)
+    meta = jnp.stack([count, y, c]).astype(jnp.int32)
+    packed, pairs, meta = lax.optimization_barrier((packed, pairs, meta))
 
     def rows(i):
         return packed[:, i * ROWS : (i + 1) * ROWS, :].reshape(BLK, HD)
@@ -363,9 +376,6 @@
     pieces = jnp.transpose(packed[:, 4 * ROWS : 4 * ROWS + 3, :ROWS], (1, 0, 2)).reshape(12, HD)
     qd = jnp.concatenate([rows(0), rows(1), pieces, jnp.zeros((4, HD), bf16)], axis=0)
     kv = jnp.concatenate([rows(2), rows(3)], axis=0)
-
-    pairs, count, early = pair_list(key_lists, key_counts, block_order, x, y, c)
-    meta = jnp.stack([count, y, c, early]).astype(jnp.int32)
 
     own = lax.all_to_all(jnp.broadcast_to(qd[None], (NY, *qd.shape)), "y", 0, 0, tiled=True)
     keys = (kv, *(shifted(kv, "x", i, NX) for i in range(1, NX)))
@@ -377,44 +387,36 @@
     probs, tops, stats = over_pairs(
         probs_kernel, 28, pairs, meta, (*queries, *keys),
         [anywhere] * 6,
-        [anywhere, vmem, vmem],
-        [square, line, shape((NQ, 2, BLK), f32)],
-        [qd_scratch, kv_scratch, pltpu.VMEM((2, UNROLL, BLK, BLK), bf16), dma((2,)), dma((NK,)), dma((2,))],
+        [anywhere, vmem, anywhere],
+        [square, line, pltpu.HBM((NQ, NQ, 2, BLK), f32)],
+        [qd_scratch, kv_scratch, pltpu.VMEM((NQ, 2, BLK), f32), pltpu.VMEM((2, UNROLL, BLK, BLK), bf16), dma((2,)), dma((NK,)), dma((2,)), dma((NQ,))],
     )
-    stats_all = lax.all_to_all(
-        jnp.broadcast_to(stats[None], (NQ, NQ, 2, BLK)), ("y", "c"), 0, 0, tiled=True
-    )
+    stats_all = lax.all_to_all(stats, ("y", "c"), 0, 0, tiled=True)
+    tiles, two_steps = pltpu.VMEM((NPAIR, BLK, BLK), bf16), pltpu.VMEM((2, UNROLL, BLK, BLK), bf16)
+    step_dma = dma((NPAIR // UNROLL,))
     dscore, dquery = over_pairs(
-        dscore_kernel, 32, pairs, meta, (*queries, *keys, in_hbm(probs), tops, stats),
-        [anywhere] * 7 + [vmem] * 2,
+        dscore_kernel, 44, pairs, meta, (*queries, *keys, in_hbm(probs), in_hbm(stats), tops),
+        [anywhere] * 8 + [vmem],
         [anywhere, anywhere],
         [square, pltpu.HBM((NQ, BLK, HD), bf16)],
         [
             qd_scratch, kv_scratch, pltpu.VMEM((NK, HD, BLK), bf16), pltpu.VMEM((NQ, HD, BLK), f32),
-            pltpu.VMEM((2, UNROLL, BLK, BLK), bf16), pltpu.VMEM((2, UNROLL, BLK, BLK), bf16),
-            pltpu.VMEM((NQ, BLK, HD), bf16), dma((2,)), dma((NK,)), dma((2,)), dma((2,)), dma((NQ,)),
+            pltpu.VMEM((NQ, 2, BLK), f32), tiles, two_steps, pltpu.VMEM((NQ, BLK, HD), bf16), dma((3,)), dma((NK,)), step_dma, dma((2,)), dma((NQ,)),
         ],
     )
     dquery = lax.all_to_all(dquery, ("y", "c"), 0, 0, tiled=True)
 
-    def key_grads(late, pairs):
-        return over_pairs(
-            functools.partial(key_kernel, late), 40, pairs, meta, (*queries, in_hbm(probs), in_hbm(dscore), tops, stats_all),
-            [anywhere] * 4 + [vmem] * 2,
-            [anywhere] * 2,
-            [pltpu.HBM((2, BLK, HD), bf16)] * 2,
-            [
-                qd_scratch, pltpu.VMEM((NQ, 1, BLK), f32), pltpu.VMEM((2, 2, BLK, HD), f32),
-                pltpu.VMEM((2, 2, BLK, HD), bf16),
-                pltpu.VMEM((DEPTH, UNROLL, BLK, BLK), bf16), pltpu.VMEM((DEPTH, UNROLL, BLK, BLK), bf16),
-                dma((2,)), dma((DEPTH, UNROLL)), dma((DEPTH, UNROLL)), dma((2,)),
-            ],
-        )
-
-    second, third = key_grads(False, pairs)
-    second, third, pairs = lax.optimization_barrier((second, third, pairs))
-    kept, first = key_grads(True, pairs)
-    arrived = [shifted(grad, "x", -i - 1, NX) for i, grad in enumerate((first, second, third))]
+    kept, *sent = over_pairs(
+        key_kernel, 50, pairs, meta, (*queries, in_hbm(probs), in_hbm(dscore), tops, stats_all),
+        [anywhere] * 4 + [vmem] * 2,
+        [anywhere] + [vmem] * (NK - 1),
+        [pltpu.HBM((2, BLK, HD), bf16)] + [shape((2, BLK, HD), bf16)] * (NK - 1),
+        [
+            qd_scratch, pltpu.VMEM((NQ, 1, BLK), f32), pltpu.VMEM((NK, 2, BLK, HD), f32),
+            pltpu.VMEM((2, BLK, HD), bf16), tiles, tiles, dma((3,)), step_dma, step_dma,
+        ],
+    )
+    arrived = [shifted(grad, "x", -i - 1, NX) for i, grad in enumerate(sent)]
 
     grads = pl.pallas_call(
         finish_kernel,
@@ -430,7 +432,7 @@
         ),
         out_shape=shape((HEADS, 3 * ROWS, HD), bf16),
         compiler_params=params(12),
-    )(meta, dquery, stats_all, in_hbm(kept), in_hbm(arrived[0]), *arrived[1:])
+    )(meta, dquery, stats_all, in_hbm(kept), *arrived)
     grads = lax.all_to_all(grads, "h", 0, 0, tiled=True)
 
     def tokens(i):

time: 188 us -> 174 us (0.926); the launches traced: 187 us -> 171 us
  blocking collectives: 79.1 us -> 35 us
  waiting for transfers between devices: 17.6 us -> 44.8 us
  starting transfers between devices: 38.2 us -> 58 us
  Pallas kernels: 36.3 us -> 23.9 us
  local copies, waits for them, and re-layouts: 10.8 us -> 5.44 us
    all_to_all x1 -> x0, blocking collectives: 49.9 us -> none  [on_device(): packed = lax.all_to_all(packed, 'h', 0, 0, tiled=True)]
    all_to_all x1 -> x2, waiting for transfers between devices: 0.01 us -> 25.4 us  [the longest x1 25.4 us: on_device(): packed = lax.all_to_all(packed, 'h', 0, 0, tiled=True)]
    all_to_all x1 -> x2, starting transfers between devices: 6.24 us -> 21.6 us  [the longest x1 15.2 us: on_device(): packed = lax.all_to_all(packed, 'h', 0, 0, tiled=True)]
    pallas_call x4 -> x3, Pallas kernels: 33.4 us -> 19.1 us  [over_pairs(): pl.pallas_call(kernel, grid_spec=pltpu.PrefetchScalarGridSpec(num_scalar_...]
    all_to_all x1, blocking collectives: 29.1 us -> 35 us  [on_device(): grads = lax.all_to_all(grads, 'h', 0, 0, tiled=True)]
    unnamed x24 -> x8, local copies, waits for them, and re-layouts: 4.65 us -> 0.12 us
    ppermute x7, starting transfers between devices: 21.1 us -> 25.4 us  [shifted(): lax.ppermute(array, axis, [(i, (i + by) % size) for i in range(size)])]
    pallas_call x1, Pallas kernels: 0.25 us -> 2.28 us  [on_device(): pl.pallas_call(pack_kernel, in_specs=[anywhere] * 5, out_specs=vmem, out_...]
  transfers between devices with their start and end apart: 10 -> 11, of which waited for: 5 -> 6; matrix products, arithmetic and copies ran while one was open for 3% -> 3% of each run, Pallas kernels for 13% -> 8%
where the time goes in v4:
time: 174 us; the launch traced here: 171 us
  starting transfers between devices  58 us (33%)
  waiting for transfers between devices  44.8 us (26%)
  blocking collectives  35 us (20%)
  Pallas kernels  23.9 us (14%)
  local copies, waits for them, and re-layouts  5.44 us (3%)
  other arithmetic  2.03 us (1%)
    all_to_all x1, blocking collectives, on_device(): grads = lax.all_to_all(grads, 'h', 0, 0, tiled=True)  35 us
    all_to_all x1, waiting for transfers between devices, on_device(): packed = lax.all_to_all(packed, 'h', 0, 0, tiled=True)  25.4 us
    ppermute x7, starting transfers between devices, shifted(): lax.ppermute(array, axis, [(i, (i + by) % size) for i in range(size)])  25.4 us
    ppermute x7, waiting for transfers between devices, shifted(): lax.ppermute(array, axis, [(i, (i + by) % size) for i in range(size)])  19.3 us
    pallas_call x3, Pallas kernels, over_pairs(): pl.pallas_call(kernel, grid_spec=pltpu.PrefetchScalarGridSpec(num_scalar_...  19.1 us
    all_to_all x1, starting transfers between devices, on_device(): packed = lax.all_to_all(packed, 'h', 0, 0, tiled=True)  15.2 us
    all_to_all x1, starting transfers between devices, on_device(): stats_all = lax.all_to_all(stats, ('y', 'c'), 0, 0, tiled=True)  6.4 us
    all_to_all x1, starting transfers between devices, on_device(): dquery = lax.all_to_all(dquery, ('y', 'c'), 0, 0, tiled=True)  6.29 us
  transfers between devices with their start and end apart: 11, of which 6 were waited for; matrix products, arithmetic and copies ran while one was open for 3% of the time, Pallas kernels for 8%

profile of v4, /device:TPU:24, one launch (start us, length us, event | category | flops | bytes accessed | tf_op | source)
XLA Modules:
  0.0 170.6 jit_solution(2033774317483061454)
XLA Ops:
  0.6 0.0 copy-start
  0.6 0.0 copy-start.2
  0.7 2.3 %shard_map.103 = bf16[16,144,128]{2,1,0:T(8,128)(2,1)} custom-call(bf16[32,2048]{1,0:T(8,128)(2,1)} %query_in.1, bf16[32,2048]{1,0:T(8,128)(2,1)} %key_in.1, bf16[32,2048]{1,0:T(8,128)(2,1)} %value_in.1, bf16[32,2048]{1,0:T(8,128)(2,1)} %output_in.1, bf16[32,2048]{1,0:T(8,128)(2,1)} %grad_in.1), custom_call_target="tpu_custom_call" | custom-call | tf_op jit(solution)/shard_map/pallas_call | solution.py:360
  2.9 0.0 copy-start.1
  3.0 15.2 %all-to-all-start = ((bf16[16,144,128]{2,1,0:T(8,128)(2,1)}), bf16[16,144,128]{2,1,0:T(8,128)(2,1)S(1)}, u32[]{:S(2)}, u32[]{:S(2)}) async-start(bf16[16,144,128]{2,1,0:T(8,128)(2,1)} %shard_map.103), calls=%async_computation | async-start | bytes 1179648 | tf_op jit(solution)/shard_map/all_to_all | solution.py:368
  18.2 0.0 copy-done.2
  18.2 0.1 copy.17
  18.3 0.0 copy-done
  18.3 0.6 gather_fusion
  19.0 0.6 gather_fusion.1
  19.5 0.0 copy-done.1
  19.5 0.6 gather_fusion.3
  20.2 0.6 gather_fusion.2
  20.9 0.1 iota_compare_fusion.1
  20.9 0.2 and_reduce_fusion
  21.1 0.1 and.87
  21.2 0.6 convert_reduce_fusion.1
  22.5 0.7 pad_add_fusion.meta
  23.3 0.1 convert_reduce_fusion
  23.4 0.2 select_reduce_fusion.pairs
  23.6 25.4 %all-to-all-done = bf16[16,144,128]{2,1,0:T(8,128)(2,1)S(1)} async-done(((bf16[16,144,128]{2,1,0:T(8,128)(2,1)}), bf16[16,144,128]{2,1,0:T(8,128)(2,1)S(1)}, u32[]{:S(2)}, u32[]{:S(2)}) %all-to-all-start) | async-done | bytes 589856 | tf_op jit(solution)/shard_map/all_to_all | solution.py:368
  49.1 0.1 reshape.225
  49.1 0.1 concatenate.6
  49.2 1.1 broadcast_in_dim.12
  50.4 4.7 %all-to-all-start.1 = ((bf16[4,1040,128]{2,1,0:T(8,128)(2,1)}), bf16[4,1040,128]{2,1,0:T(8,128)(2,1)S(1)}, u32[]{:S(2)}, u32[]{:S(2)}) async-start(bf16[4,1040,128]{2,1,0:T(8,128)(2,1)} %broadcast_in_dim.12), calls=%async_computation.1 | async-start | bytes 2129920 | tf_op jit(solution)/shard_map/all_to_all | solution.py:380
  55.1 3.4 %collective-permute-start = (bf16[1024,128]{1,0:T(8,128)(2,1)S(1)}, bf16[1024,128]{1,0:T(8,128)(2,1)S(1)}, u32[]{:S(2)}, u32[]{:S(2)}) collective-permute-start(bf16[1024,128]{1,0:T(8,128)(2,1)S(1)} %pad_maximum_fusion.kv0), channel_id=1, source_target_pairs={{0,128},{128,256},{256,384},{384,0},{1,129},{129,257},{257,385},{3... | collective-permute-start | bytes 786440 | tf_op jit(solution)/shard_map/ppermute | solution.py:349
  58.5 4.6 %collective-permute-start.1 = (bf16[1024,128]{1,0:T(8,128)(2,1)S(1)}, bf16[1024,128]{1,0:T(8,128)(2,1)S(1)}, u32[]{:S(2)}, u32[]{:S(2)}) collective-permute-start(bf16[1024,128]{1,0:T(8,128)(2,1)S(1)} %pad_maximum_fusion.kv0), channel_id=1, source_target_pairs={{0,256},{128,384},{256,0},{384,128},{1,257},{129,385},{257,1},{385... | collective-permute-start | bytes 786440 | tf_op jit(solution)/shard_map/ppermute | solution.py:349
  63.1 3.3 %collective-permute-start.2 = (bf16[1024,128]{1,0:T(8,128)(2,1)S(1)}, bf16[1024,128]{1,0:T(8,128)(2,1)S(1)}, u32[]{:S(2)}, u32[]{:S(2)}) collective-permute-start(bf16[1024,128]{1,0:T(8,128)(2,1)S(1)} %pad_maximum_fusion.kv0), channel_id=1, source_target_pairs={{0,384},{128,0},{256,128},{384,256},{1,385},{129,1},{257,129},{385... | collective-permute-start | bytes 786440 | tf_op jit(solution)/shard_map/ppermute | solution.py:349
  66.5 0.0 collective-permute-done.kv1
  66.5 1.9 %collective-permute-done.1.kv2 = bf16[1024,128]{1,0:T(8,128)(2,1)S(1)} collective-permute-done((bf16[1024,128]{1,0:T(8,128)(2,1)S(1)}, bf16[1024,128]{1,0:T(8,128)(2,1)S(1)}, u32[]{:S(2)}, u32[]{:S(2)}) %collective-permute-start.1) | collective-permute-done | bytes 262176 | tf_op jit(solution)/shard_map/ppermute | solution.py:349
  68.3 3.0 %collective-permute-done.2.kv3 = bf16[1024,128]{1,0:T(8,128)(2,1)S(1)} collective-permute-done((bf16[1024,128]{1,0:T(8,128)(2,1)S(1)}, bf16[1024,128]{1,0:T(8,128)(2,1)S(1)}, u32[]{:S(2)}, u32[]{:S(2)}) %collective-permute-start.2) | collective-permute-done | bytes 262176 | tf_op jit(solution)/shard_map/ppermute | solution.py:349
  71.4 0.0 all-to-all-done.1.own
  71.4 1.9 %collective-permute-start.3 = (bf16[4,1040,128]{2,1,0:T(8,128)(2,1)S(1)}, bf16[4,1040,128]{2,1,0:T(8,128)(2,1)S(1)}, u32[]{:S(2)}, u32[]{:S(2)}) collective-permute-start(bf16[4,1040,128]{2,1,0:T(8,128)(2,1)S(1)} %all-to-all-done.1.own), channel_id=1, source_target_pairs={{0,16},{16,0},{1,17},{17,1},{2,18},{18,2},{3,19},{19,3},{4,20},{20... | collective-permute-start | bytes 3194888 | tf_op jit(solution)/shard_map/ppermute | solution.py:349
  73.3 2.6 %collective-permute-done.3.other = bf16[4,1040,128]{2,1,0:T(8,128)(2,1)S(1)} collective-permute-done((bf16[4,1040,128]{2,1,0:T(8,128)(2,1)S(1)}, bf16[4,1040,128]{2,1,0:T(8,128)(2,1)S(1)}, u32[]{:S(2)}, u32[]{:S(2)}) %collective-permute-start.3) | collective-permute-done | bytes 1064992 | tf_op jit(solution)/shard_map/ppermute | solution.py:349
  76.0 5.4 %shard_map.104 = (bf16[32,512,512]{2,1,0:T(8,128)(2,1)}, f32[32,1,512]{2,1,0:T(1,128)S(1)}, f32[8,8,2,512]{3,2,1,0:T(2,128)}) custom-call(s32[32]{0:T(128)S(1)} %select_reduce_fusion.pairs, s32[3]{0:T(128)S(1)} %pad_add_fusion.meta, bf16[4,1040,128]{2,1,0:T(8,128)(2,1)S(1)} %all-to-all-done.1.own, bf16[4,1040,128]{2,1,0:T(8,128)(2,1)S(1)} %collective-permute-done.3.other, ...), custom_call_target="tpu_custom_call" | custom-call | tf_op jit(solution)/shard_map/pallas_call | solution.py:317
  81.3 6.4 %all-to-all-start.3 = ((f32[8,8,2,512]{3,2,1,0:T(2,128)}), f32[8,8,2,512]{3,2,1,0:T(2,128)S(1)}, u32[]{:S(2)}, u32[]{:S(2)}) async-start(f32[8,8,2,512]{3,2,1,0:T(2,128)} %get-tuple-element.29.stats_in), calls=%async_computation.3 | async-start | bytes 524288 | tf_op jit(solution)/shard_map/all_to_all | solution.py:394
  87.7 7.1 %shard_map.105 = (bf16[32,512,512]{2,1,0:T(8,128)(2,1)}, bf16[8,512,128]{2,1,0:T(8,128)(2,1)}) custom-call(s32[32]{0:T(128)S(1)} %select_reduce_fusion.pairs, s32[3]{0:T(128)S(1)} %pad_add_fusion.meta, bf16[4,1040,128]{2,1,0:T(8,128)(2,1)S(1)} %all-to-all-done.1.own, bf16[4,1040,128]{2,1,0:T(8,128)(2,1)S(1)} %collective-permute-done.3.other, ...), custom_call_target="tpu_custom_call" | custom-call | tf_op jit(solution)/shard_map/pallas_call | solution.py:317
  94.8 0.0 all-to-all-done.3.stats_all.stats_in
  94.8 6.3 %all-to-all-start.2 = ((bf16[8,512,128]{2,1,0:T(8,128)(2,1)}), bf16[8,512,128]{2,1,0:T(8,128)(2,1)S(1)}, u32[]{:S(2)}, u32[]{:S(2)}) async-start(bf16[8,512,128]{2,1,0:T(8,128)(2,1)} %get-tuple-element.31), calls=%async_computation.2 | async-start | bytes 2097152 | tf_op jit(solution)/shard_map/all_to_all | solution.py:407
  101.1 6.6 %shard_map.106 = (bf16[2,512,128]{2,1,0:T(8,128)(2,1)}, bf16[2,512,128]{2,1,0:T(8,128)(2,1)S(1)}, bf16[2,512,128]{2,1,0:T(8,128)(2,1)S(1)}, bf16[2,512,128]{2,1,0:T(8,128)(2,1)S(1)}) custom-call(s32[32]{0:T(128)S(1)} %select_reduce_fusion.pairs, s32[3]{0:T(128)S(1)} %pad_add_fusion.meta, bf16[4,1040,128]{2,1,0:T(8,128)(2,1)S(1)} %all-to-all-done.1.own, ...), custom_call_target="tpu_custom_call" | custom-call | tf_op jit(solution)/shard_map/pallas_call | solution.py:317
  107.7 6.3 %collective-permute-start.4 = (bf16[2,512,128]{2,1,0:T(8,128)(2,1)S(1)}, bf16[2,512,128]{2,1,0:T(8,128)(2,1)S(1)}, u32[]{:S(2)}, u32[]{:S(2)}) collective-permute-start(bf16[2,512,128]{2,1,0:T(8,128)(2,1)S(1)} %get-tuple-element.34), channel_id=1, source_target_pairs={{0,384},{128,0},{256,128},{384,256},{1,385},{129,1},{257,129},{385... | collective-permute-start | bytes 786440 | tf_op jit(solution)/shard_map/ppermute | solution.py:349
  114.1 3.9 %collective-permute-start.5 = (bf16[2,512,128]{2,1,0:T(8,128)(2,1)S(1)}, bf16[2,512,128]{2,1,0:T(8,128)(2,1)S(1)}, u32[]{:S(2)}, u32[]{:S(2)}) collective-permute-start(bf16[2,512,128]{2,1,0:T(8,128)(2,1)S(1)} %get-tuple-element.35), channel_id=1, source_target_pairs={{0,256},{128,384},{256,0},{384,128},{1,257},{129,385},{257,1},{385... | collective-permute-start | bytes 786440 | tf_op jit(solution)/shard_map/ppermute | solution.py:349
  117.9 1.9 %collective-permute-start.6 = (bf16[2,512,128]{2,1,0:T(8,128)(2,1)S(1)}, bf16[2,512,128]{2,1,0:T(8,128)(2,1)S(1)}, u32[]{:S(2)}, u32[]{:S(2)}) collective-permute-start(bf16[2,512,128]{2,1,0:T(8,128)(2,1)S(1)} %get-tuple-element.36), channel_id=1, source_target_pairs={{0,128},{128,256},{256,384},{384,0},{1,129},{129,257},{257,385},{3... | collective-permute-start | bytes 786440 | tf_op jit(solution)/shard_map/ppermute | solution.py:349
  119.9 0.0 collective-permute-done.4.first
  119.9 5.1 %collective-permute-done.5.second = bf16[2,512,128]{2,1,0:T(8,128)(2,1)S(1)} collective-permute-done((bf16[2,512,128]{2,1,0:T(8,128)(2,1)S(1)}, bf16[2,512,128]{2,1,0:T(8,128)(2,1)S(1)}, u32[]{:S(2)}, u32[]{:S(2)}) %collective-permute-start.5) | collective-permute-done | bytes 262176 | tf_op jit(solution)/shard_map/ppermute | solution.py:349
  124.9 6.7 %collective-permute-done.6.third = bf16[2,512,128]{2,1,0:T(8,128)(2,1)S(1)} collective-permute-done((bf16[2,512,128]{2,1,0:T(8,128)(2,1)S(1)}, bf16[2,512,128]{2,1,0:T(8,128)(2,1)S(1)}, u32[]{:S(2)}, u32[]{:S(2)}) %collective-permute-start.6) | collective-permute-done | bytes 262176 | tf_op jit(solution)/shard_map/ppermute | solution.py:349
  131.6 0.0 all-to-all-done.2.dquery_in
  131.6 2.5 %shard_map.107 = bf16[16,96,128]{2,1,0:T(8,128)(2,1)S(1)} custom-call(s32[3]{0:T(128)S(1)} %pad_add_fusion.meta, bf16[8,512,128]{2,1,0:T(8,128)(2,1)S(1)} %all-to-all-done.2.dquery_in, f32[8,8,2,512]{3,2,1,0:T(2,128)S(1)} %all-to-all-done.3.stats_all.stats_in, bf16[2,512,128]{2,1,0:T(8,128)(2,1)} %get-tuple-element.33.own_in, ...), custom_call_target="tpu_custom_call" | custom-call | tf_op jit(solution)/shard_map/pallas_call | solution.py:421
  134.2 35.0 %all_to_all.25 = bf16[16,96,128]{2,1,0:T(8,128)(2,1)S(1)} all-to-all(bf16[16,96,128]{2,1,0:T(8,128)(2,1)S(1)} %shard_map.107), channel_id=1, replica_groups=mesh['x'=4,'y'=4,'c'=2,'h'=16] {'h'}, dimensions={0} | all-to-all | bytes 786432 | tf_op jit(solution)/shard_map/all_to_all | solution.py:436
  169.2 0.7 copy.28
  169.9 0.7 copy_bitcast_fusion
  (13 shorter events, 0.2 us)
Async XLA Ops:
  0.6 17.7 %copy-start = (s32[32]{0:T(128)S(1)}, s32[32]{0:T(128)}, u32[]{:S(2)}) copy-start(s32[32]{0:T(128)} %param.15) | copy-start | bytes 388
  0.6 17.5 %copy-start.2 = (s32[32,16]{0,1:T(8,128)S(1)}, s32[32,16]{0,1:T(8,128)}, u32[]{:S(2)}) copy-start(s32[32,16]{0,1:T(8,128)} %param.13) | copy-start | bytes 6148
  2.9 16.6 %copy-start.1 = (s32[32]{0:T(128)S(1)}, s32[32]{0:T(128)}, u32[]{:S(2)}) copy-start(s32[32]{0:T(128)} %param.14) | copy-start | bytes 388
  3.0 46.0 %all-to-all-start = ((bf16[16,144,128]{2,1,0:T(8,128)(2,1)}), bf16[16,144,128]{2,1,0:T(8,128)(2,1)S(1)}, u32[]{:S(2)}, u32[]{:S(2)}) async-start(bf16[16,144,128]{2,1,0:T(8,128)(2,1)} %shard_map.103), calls=%async_computation | async-start | bytes 1179648 | tf_op jit(solution)/shard_map/all_to_all | solution.py:368
  50.4 21.0 %all-to-all-start.1 = ((bf16[4,1040,128]{2,1,0:T(8,128)(2,1)}), bf16[4,1040,128]{2,1,0:T(8,128)(2,1)S(1)}, u32[]{:S(2)}, u32[]{:S(2)}) async-start(bf16[4,1040,128]{2,1,0:T(8,128)(2,1)} %broadcast_in_dim.12), calls=%async_computation.1 | async-start | bytes 2129920 | tf_op jit(solution)/shard_map/all_to_all | solution.py:380
  55.1 11.4 %collective-permute-start = (bf16[1024,128]{1,0:T(8,128)(2,1)S(1)}, bf16[1024,128]{1,0:T(8,128)(2,1)S(1)}, u32[]{:S(2)}, u32[]{:S(2)}) collective-permute-start(bf16[1024,128]{1,0:T(8,128)(2,1)S(1)} %pad_maximum_fusion.kv0), channel_id=1, source_target_pairs={{0,128},{128,256},{256,384},{384,0},{1,129},{129,257},{257,385},{3... | collective-permute-start | bytes 786440 | tf_op jit(solution)/shard_map/ppermute | solution.py:349
  58.5 9.9 %collective-permute-start.1 = (bf16[1024,128]{1,0:T(8,128)(2,1)S(1)}, bf16[1024,128]{1,0:T(8,128)(2,1)S(1)}, u32[]{:S(2)}, u32[]{:S(2)}) collective-permute-start(bf16[1024,128]{1,0:T(8,128)(2,1)S(1)} %pad_maximum_fusion.kv0), channel_id=1, source_target_pairs={{0,256},{128,384},{256,0},{384,128},{1,257},{129,385},{257,1},{385... | collective-permute-start | bytes 786440 | tf_op jit(solution)/shard_map/ppermute | solution.py:349
  63.1 8.3 %collective-permute-start.2 = (bf16[1024,128]{1,0:T(8,128)(2,1)S(1)}, bf16[1024,128]{1,0:T(8,128)(2,1)S(1)}, u32[]{:S(2)}, u32[]{:S(2)}) collective-permute-start(bf16[1024,128]{1,0:T(8,128)(2,1)S(1)} %pad_maximum_fusion.kv0), channel_id=1, source_target_pairs={{0,384},{128,0},{256,128},{384,256},{1,385},{129,1},{257,129},{385... | collective-permute-start | bytes 786440 | tf_op jit(solution)/shard_map/ppermute | solution.py:349
  71.4 4.6 %collective-permute-start.3 = (bf16[4,1040,128]{2,1,0:T(8,128)(2,1)S(1)}, bf16[4,1040,128]{2,1,0:T(8,128)(2,1)S(1)}, u32[]{:S(2)}, u32[]{:S(2)}) collective-permute-start(bf16[4,1040,128]{2,1,0:T(8,128)(2,1)S(1)} %all-to-all-done.1.own), channel_id=1, source_target_pairs={{0,16},{16,0},{1,17},{17,1},{2,18},{18,2},{3,19},{19,3},{4,20},{20... | collective-permute-start | bytes 3194888 | tf_op jit(solution)/shard_map/ppermute | solution.py:349
  81.3 13.5 %all-to-all-start.3 = ((f32[8,8,2,512]{3,2,1,0:T(2,128)}), f32[8,8,2,512]{3,2,1,0:T(2,128)S(1)}, u32[]{:S(2)}, u32[]{:S(2)}) async-start(f32[8,8,2,512]{3,2,1,0:T(2,128)} %get-tuple-element.29.stats_in), calls=%async_computation.3 | async-start | bytes 524288 | tf_op jit(solution)/shard_map/all_to_all | solution.py:394
  94.8 36.8 %all-to-all-start.2 = ((bf16[8,512,128]{2,1,0:T(8,128)(2,1)}), bf16[8,512,128]{2,1,0:T(8,128)(2,1)S(1)}, u32[]{:S(2)}, u32[]{:S(2)}) async-start(bf16[8,512,128]{2,1,0:T(8,128)(2,1)} %get-tuple-element.31), calls=%async_computation.2 | async-start | bytes 2097152 | tf_op jit(solution)/shard_map/all_to_all | solution.py:407
  107.7 12.1 %collective-permute-start.4 = (bf16[2,512,128]{2,1,0:T(8,128)(2,1)S(1)}, bf16[2,512,128]{2,1,0:T(8,128)(2,1)S(1)}, u32[]{:S(2)}, u32[]{:S(2)}) collective-permute-start(bf16[2,512,128]{2,1,0:T(8,128)(2,1)S(1)} %get-tuple-element.34), channel_id=1, source_target_pairs={{0,384},{128,0},{256,128},{384,256},{1,385},{129,1},{257,129},{385... | collective-permute-start | bytes 786440 | tf_op jit(solution)/shard_map/ppermute | solution.py:349
  114.1 10.9 %collective-permute-start.5 = (bf16[2,512,128]{2,1,0:T(8,128)(2,1)S(1)}, bf16[2,512,128]{2,1,0:T(8,128)(2,1)S(1)}, u32[]{:S(2)}, u32[]{:S(2)}) collective-permute-start(bf16[2,512,128]{2,1,0:T(8,128)(2,1)S(1)} %get-tuple-element.35), channel_id=1, source_target_pairs={{0,256},{128,384},{256,0},{384,128},{1,257},{129,385},{257,1},{385... | collective-permute-start | bytes 786440 | tf_op jit(solution)/shard_map/ppermute | solution.py:349
  117.9 13.7 %collective-permute-start.6 = (bf16[2,512,128]{2,1,0:T(8,128)(2,1)S(1)}, bf16[2,512,128]{2,1,0:T(8,128)(2,1)S(1)}, u32[]{:S(2)}, u32[]{:S(2)}) collective-permute-start(bf16[2,512,128]{2,1,0:T(8,128)(2,1)S(1)} %get-tuple-element.36), channel_id=1, source_target_pairs={{0,128},{128,256},{256,384},{384,0},{1,129},{129,257},{257,385},{3... | collective-permute-start | bytes 786440 | tf_op jit(solution)/shard_map/ppermute | solution.py:349

commit v5 on v4

--- a/solution.py
+++ b/solution.py
@@ -16,7 +16,7 @@
 NQ = NY * NC
 NK = NX
 NPAIR = NQ * NK
-PACKED = 4 * ROWS + 16
+PACKED = 4 * ROWS + 8
 QD_ROWS = 2 * BLK + 16
 UNROLL = 4
 SCALE = 1.0 / math.sqrt(HD)
@@ -194,17 +194,19 @@
     return top + jnp.log2(jnp.sum(sums * jnp.exp2(tops - top[None]), axis=0))
 
 
-def key_kernel(pairs, meta, own, other, probs_in, dscore_in, tops, stats_all, *rest):
-    *outs, qd, norms, total, kept, probs, dscore, sems, probs_sems, dscore_sems = rest
-    count = meta[0]
-    steps = (count + UNROLL - 1) // UNROLL
+def key_kernel(late, pairs, meta, own, other, probs_in, dscore_in, tops, stats_all, *rest):
+    *outs, qd, norms, total, probs, dscore, sems, probs_sems, dscore_sems = rest
+    begin, end = (0, meta[3]) if late else (meta[3], meta[0])
+    steps = (end - begin + UNROLL - 1) // UNROLL
 
     def loads(step):
-        span = pl.ds(step * UNROLL, UNROLL)
-        return (
-            pltpu.make_async_copy(dscore_in.at[span], dscore.at[span], dscore_sems.at[step]),
-            pltpu.make_async_copy(probs_in.at[span], probs.at[span], probs_sems.at[step]),
-        )
+        copies = []
+        for u in range(UNROLL):
+            t = jnp.minimum(begin + step * UNROLL + u, end - 1)
+            held = step * UNROLL + u
+            copies.append(pltpu.make_async_copy(dscore_in.at[t], dscore.at[held], dscore_sems.at[held]))
+            copies.append(pltpu.make_async_copy(probs_in.at[t], probs.at[held], probs_sems.at[held]))
+        return copies
 
     def start(step, _):
         for copy in loads(step):
@@ -225,26 +227,24 @@
             copy.wait()
         found = []
         for u in range(UNROLL):
-            t = step * UNROLL + u
+            held = step * UNROLL + u
+            t = jnp.minimum(begin + held, end - 1)
             code = pairs[t]
             place, key, query = query_place(code, meta), code // NQ, query_slot(code, meta)
-            weight = jnp.where(t < count, jnp.exp2(tops[t] - norms[place]), 0.0)
+            weight = jnp.where(begin + held < end, jnp.exp2(tops[t] - norms[place]), 0.0)
             weight = jnp.transpose(jnp.broadcast_to(weight, (HD, BLK)))
             queries = (qd[query, :BLK, :].astype(jnp.float32) * (weight * SCALE)).astype(jnp.bfloat16)
             grads = (qd[query, BLK : 2 * BLK, :].astype(jnp.float32) * weight).astype(jnp.bfloat16)
-            found.append((key, dot(dscore[t], queries, (1, 0)), dot(probs[t], grads, (1, 0))))
-        for key, key_part, value_part in found:
-            total[key, 0] += key_part
-            total[key, 1] += value_part
+            slot = 0 if late else key - 1
+            found.append((slot, dot(dscore[held], queries, (1, 0)), dot(probs[held], grads, (1, 0))))
+        for slot, key_part, value_part in found:
+            total[slot, 0] += key_part
+            total[slot, 1] += value_part
         return 0
 
     lax.fori_loop(0, steps, body, 0)
-    kept[...] = total[0].astype(jnp.bfloat16)
-    sent = pltpu.make_async_copy(kept, outs[0], sems.at[2])
-    sent.start()
-    for i, out in enumerate(outs[1:]):
-        out[...] = total[i + 1].astype(jnp.bfloat16)
-    sent.wait()
+    for i, out in enumerate(outs):
+        out[...] = total[i].astype(jnp.bfloat16)
 
 
 def pack_kernel(query_in, key_in, value_in, output_in, grad_in, out, held, sems):
@@ -269,40 +269,49 @@
     row_dot = jnp.transpose(row_dot)[:HEADS]
     high = row_dot.astype(jnp.bfloat16).astype(jnp.float32)
     middle = (row_dot - high).astype(jnp.bfloat16).astype(jnp.float32)
-    row = lax.broadcasted_iota(jnp.int32, (HEADS, 16, HD), 1)
-    pieces = jnp.zeros((HEADS, 16, HD), jnp.float32)
+    row = lax.broadcasted_iota(jnp.int32, (HEADS, 8, HD), 1)
+    pieces = jnp.zeros((HEADS, 8, HD), jnp.float32)
     for i, piece in enumerate((high, middle, row_dot - high - middle)):
         pieces = jnp.where(row == i, piece[:, None, :], pieces)
     out[:, 4 * ROWS :, :] = pieces.astype(jnp.bfloat16)
 
 
-def finish_kernel(meta, dquery_in, stats_in, own_in, first, second, third, out, dquery, stats_all, parts, sems):
+def finish_queries_kernel(meta, dquery_in, stats_in, out, dquery, stats_all, sems):
+    fetches = [
+        pltpu.make_async_copy(stats_in, stats_all, sems.at[0]),
+        pltpu.make_async_copy(dquery_in, dquery, sems.at[1]),
+    ]
+    for fetch in fetches:
+        fetch.start()
+    for fetch in fetches:
+        fetch.wait()
+    place = meta[1] * NC + meta[2]
+    tops, sums = stats_all[:, place, 0, :], stats_all[:, place, 1, :]
+    top = jnp.max(tops, axis=0, keepdims=True)
+    norm = top + jnp.log2(jnp.sum(sums * jnp.exp2(tops - top), axis=0, keepdims=True))
+    weight = jnp.transpose(jnp.exp2(tops - norm) * SCALE)
+    grad = dquery[0].astype(jnp.float32) * weight[:, 0:1]
+    for i in range(1, NQ):
+        grad += dquery[i].astype(jnp.float32) * weight[:, i : i + 1]
+    out[...] = grad.astype(jnp.bfloat16)
+
+
+def finish_kernel(query_grad, kept, first, second, third, out, parts, query_held, sems):
     fetches = [
         pltpu.make_async_copy(source, parts.at[i], sems.at[i])
-        for i, source in enumerate((own_in, first, second, third))
+        for i, source in enumerate((kept, first, second, third))
     ]
-    fetches.append(pltpu.make_async_copy(stats_in, stats_all, sems.at[4]))
-    fetches.append(pltpu.make_async_copy(dquery_in, dquery, sems.at[5]))
-    for fetch in fetches:
-        fetch.start()
-    for fetch in fetches[:4]:
-        fetch.wait()
+    fetches.append(pltpu.make_async_copy(query_grad, query_held, sems.at[4]))
+    for fetch in fetches:
+        fetch.start()
+    for fetch in fetches:
+        fetch.wait()
+    out[:, 0:ROWS, :] = query_held[...].reshape(HEADS, ROWS, HD)
     for i in range(2):
         grad = (parts[0, i].astype(jnp.float32) + parts[1, i].astype(jnp.float32)) + (
             parts[2, i].astype(jnp.float32) + parts[3, i].astype(jnp.float32)
         )
         out[:, (i + 1) * ROWS : (i + 2) * ROWS, :] = grad.astype(jnp.bfloat16).reshape(HEADS, ROWS, HD)
-    for fetch in fetches[4:]:
-        fetch.wait()
-    place = meta[1] * NC + meta[2]
-    tops, sums = stats_all[:, place, 0, :], stats_all[:, place, 1, :]
-    top = jnp.max(tops, axis=0, keepdims=True)
-    norm = top + jnp.log2(jnp.sum(sums * jnp.exp2(tops - top), axis=0, keepdims=True))
-    weight = jnp.transpose(jnp.exp2(tops - norm) * SCALE)
-    query_grad = dquery[0].astype(jnp.float32) * weight[:, 0:1]
-    for i in range(1, NQ):
-        query_grad += dquery[i].astype(jnp.float32) * weight[:, i : i + 1]
-    out[:, 0:ROWS, :] = query_grad.astype(jnp.bfloat16).reshape(HEADS, ROWS, HD)
 
 
 def in_hbm(array):
@@ -342,7 +351,7 @@
     count = jnp.sum(named.astype(jnp.int32))
     wanted = jnp.minimum(code, count - 1)
     pairs = jnp.sum(jnp.where(named[None, :] & (rank[None, :] == wanted[:, None]), code[None, :], 0), axis=1)
-    return pairs.astype(jnp.int32), count
+    return pairs.astype(jnp.int32), count, jnp.sum(named[:NQ].astype(jnp.int32))
 
 
 def shifted(array, axis, by, size):
@@ -366,8 +375,8 @@
         compiler_params=params(8),
     )(*(in_hbm(array) for array in (query_data, key_data, value_data, output_data, output_grad)))
     packed = lax.all_to_all(packed, "h", 0, 0, tiled=True)
-    pairs, count = pair_list(key_lists, key_counts, block_order, x, y, c)
-    meta = jnp.stack([count, y, c]).astype(jnp.int32)
+    pairs, count, near = pair_list(key_lists, key_counts, block_order, x, y, c)
+    meta = jnp.stack([count, y, c, near]).astype(jnp.int32)
     packed, pairs, meta = lax.optimization_barrier((packed, pairs, meta))
 
     def rows(i):
@@ -406,33 +415,46 @@
     )
     dquery = lax.all_to_all(dquery, ("y", "c"), 0, 0, tiled=True)
 
-    kept, *sent = over_pairs(
-        key_kernel, 50, pairs, meta, (*queries, in_hbm(probs), in_hbm(dscore), tops, stats_all),
-        [anywhere] * 4 + [vmem] * 2,
-        [anywhere] + [vmem] * (NK - 1),
-        [pltpu.HBM((2, BLK, HD), bf16)] + [shape((2, BLK, HD), bf16)] * (NK - 1),
-        [
-            qd_scratch, pltpu.VMEM((NQ, 1, BLK), f32), pltpu.VMEM((NK, 2, BLK, HD), f32),
-            pltpu.VMEM((2, BLK, HD), bf16), tiles, tiles, dma((3,)), step_dma, step_dma,
-        ],
-    )
-    arrived = [shifted(grad, "x", -i - 1, NX) for i, grad in enumerate(sent)]
-
-    grads = pl.pallas_call(
-        finish_kernel,
+
+    def key_grads(late, pairs):
+        slots = 1 if late else NK - 1
+        most = slots * NQ
+        held = pltpu.VMEM((most, BLK, BLK), bf16)
+        return over_pairs(
+            functools.partial(key_kernel, late), 50, pairs, meta,
+            (*queries, in_hbm(probs), in_hbm(dscore), tops, stats_all),
+            [anywhere] * 4 + [vmem] * 2,
+            [vmem] * slots,
+            [shape((2, BLK, HD), bf16)] * slots,
+            [
+                qd_scratch, pltpu.VMEM((NQ, 1, BLK), f32), pltpu.VMEM((slots, 2, BLK, HD), f32), held, held,
+                dma((2,)), dma((most,)), dma((most,)),
+            ],
+        )
+
+    *sent, pairs = lax.optimization_barrier((*key_grads(False, pairs), pairs))
+    arrived = {i: shifted(sent[i - 1], "x", -i, NX) for i in (2, 1, 3)}
+    (kept,) = key_grads(True, pairs)
+    query_grad = pl.pallas_call(
+        finish_queries_kernel,
         grid_spec=pltpu.PrefetchScalarGridSpec(
             num_scalar_prefetch=1,
             grid=(1,),
-            in_specs=[anywhere] * 6,
+            in_specs=[anywhere] * 2,
             out_specs=vmem,
-            scratch_shapes=[
-                pltpu.VMEM((NQ, BLK, HD), bf16), pltpu.VMEM((NQ, NQ, 2, BLK), f32),
-                pltpu.VMEM((NK, 2, BLK, HD), bf16), dma((6,)),
-            ],
+            scratch_shapes=[pltpu.VMEM((NQ, BLK, HD), bf16), pltpu.VMEM((NQ, NQ, 2, BLK), f32), dma((2,))],
         ),
+        out_shape=shape((BLK, HD), bf16),
+        compiler_params=params(12),
+    )(meta, dquery, stats_all)
+    grads = pl.pallas_call(
+        finish_kernel,
+        in_specs=[anywhere] * 5,
+        out_specs=vmem,
         out_shape=shape((HEADS, 3 * ROWS, HD), bf16),
+        scratch_shapes=[pltpu.VMEM((NK, 2, BLK, HD), bf16), pltpu.VMEM((BLK, HD), bf16), dma((5,))],
         compiler_params=params(12),
-    )(meta, dquery, stats_all, in_hbm(kept), *arrived)
+    )(query_grad, kept, arrived[1], arrived[2], arrived[3])
     grads = lax.all_to_all(grads, "h", 0, 0, tiled=True)
 
     def tokens(i):

time: 174 us -> 170 us (0.977); the launches traced: 171 us -> 169 us
  Pallas kernels: 23.9 us -> 34.2 us
  waiting for transfers between devices: 44.8 us -> 36.1 us
  starting transfers between devices: 58 us -> 53.8 us
    pallas_call x3 -> x4, Pallas kernels: 19.1 us -> 29.1 us  [over_pairs(): pl.pallas_call(kernel, grid_spec=pltpu.PrefetchScalarGridSpec(num_scalar_...]
    ppermute x7, waiting for transfers between devices: 19.3 us -> 12.9 us  [shifted(): lax.ppermute(array, axis, [(i, (i + by) % size) for i in range(size)])]
    all_to_all x1, waiting for transfers between devices: 25.4 us -> 23.2 us  [on_device(): packed = lax.all_to_all(packed, 'h', 0, 0, tiled=True)]
  transfers between devices with their start and end apart: 11 -> 11, of which waited for: 6 -> 6; matrix products, arithmetic and copies ran while one was open for 3% -> 4% of each run, Pallas kernels for 8% -> 14%
where the time goes in v5:
time: 170 us; the launch traced here: 169 us
  starting transfers between devices  53.8 us (32%)
  waiting for transfers between devices  36.1 us (21%)
  Pallas kernels  34.2 us (20%)
  blocking collectives  33.3 us (20%)
  local copies, waits for them, and re-layouts  6.14 us (4%)
  other arithmetic  3.4 us (2%)
    all_to_all x1, blocking collectives, on_device(): grads = lax.all_to_all(grads, 'h', 0, 0, tiled=True)  33.3 us
    pallas_call x4, Pallas kernels, over_pairs(): pl.pallas_call(kernel, grid_spec=pltpu.PrefetchScalarGridSpec(num_scalar_...  29.1 us
    ppermute x7, starting transfers between devices, shifted(): lax.ppermute(array, axis, [(i, (i + by) % size) for i in range(size)])  23.8 us
    all_to_all x1, waiting for transfers between devices, on_device(): packed = lax.all_to_all(packed, 'h', 0, 0, tiled=True)  23.2 us
    all_to_all x1, starting transfers between devices, on_device(): packed = lax.all_to_all(packed, 'h', 0, 0, tiled=True)  15.2 us
    ppermute x7, waiting for transfers between devices, shifted(): lax.ppermute(array, axis, [(i, (i + by) % size) for i in range(size)])  12.9 us
    all_to_all x1, starting transfers between devices, on_device(): dquery = lax.all_to_all(dquery, ('y', 'c'), 0, 0, tiled=True)  5.09 us
    all_to_all x1, starting transfers between devices, on_device(): stats_all = lax.all_to_all(stats, ('y', 'c'), 0, 0, tiled=True)  4.97 us
  transfers between devices with their start and end apart: 11, of which 6 were waited for; matrix products, arithmetic and copies ran while one was open for 4% of the time, Pallas kernels for 14%

profile of v5, /device:TPU:24, one launch (start us, length us, event | category | flops | bytes accessed | tf_op | source)
XLA Modules:
  0.0 168.5 jit_solution(15219364771329776400)
XLA Ops:
  0.6 0.0 copy-start
  0.6 0.0 copy-start.4
  0.7 2.3 %shard_map.103 = bf16[16,136,128]{2,1,0:T(8,128)(2,1)} custom-call(bf16[32,2048]{1,0:T(8,128)(2,1)} %query_in.1, bf16[32,2048]{1,0:T(8,128)(2,1)} %key_in.1, bf16[32,2048]{1,0:T(8,128)(2,1)} %value_in.1, bf16[32,2048]{1,0:T(8,128)(2,1)} %output_in.1, bf16[32,2048]{1,0:T(8,128)(2,1)} %grad_in.1), custom_call_target="tpu_custom_call" | custom-call | tf_op jit(solution)/shard_map/pallas_call | solution.py:369
  2.9 0.0 copy-start.3
  2.9 15.2 %all-to-all-start = ((bf16[16,136,128]{2,1,0:T(8,128)(2,1)}), bf16[16,136,128]{2,1,0:T(8,128)(2,1)S(1)}, u32[]{:S(2)}, u32[]{:S(2)}) async-start(bf16[16,136,128]{2,1,0:T(8,128)(2,1)} %shard_map.103), calls=%async_computation | async-start | bytes 1114112 | tf_op jit(solution)/shard_map/all_to_all | solution.py:377
  18.2 0.0 copy-done.4
  18.2 0.1 copy.17
  18.3 0.0 copy-done
  18.3 0.6 gather_fusion
  18.9 0.6 gather_fusion.1
  19.5 0.0 copy-done.3
  19.5 0.6 gather_fusion.3
  20.2 0.6 gather_fusion.2
  20.8 0.1 iota_compare_fusion.1
  20.9 0.2 and_reduce_fusion
  21.1 0.1 and.87
  21.2 0.7 convert_reduce_fusion.1
  22.6 0.6 fusion.8
  23.2 1.4 pad_add_fusion.meta
  24.6 0.1 convert_reduce_fusion
  24.8 0.2 select_reduce_fusion.pairs
  24.9 23.2 %all-to-all-done = bf16[16,136,128]{2,1,0:T(8,128)(2,1)S(1)} async-done(((bf16[16,136,128]{2,1,0:T(8,128)(2,1)}), bf16[16,136,128]{2,1,0:T(8,128)(2,1)S(1)}, u32[]{:S(2)}, u32[]{:S(2)}) %all-to-all-start) | async-done | bytes 557088 | tf_op jit(solution)/shard_map/all_to_all | solution.py:377
  48.2 0.1 reshape.227
  48.3 0.1 concatenate.6
  48.4 1.1 broadcast_in_dim.12
  49.5 4.7 %all-to-all-start.1 = ((bf16[4,1040,128]{2,1,0:T(8,128)(2,1)}), bf16[4,1040,128]{2,1,0:T(8,128)(2,1)S(1)}, u32[]{:S(2)}, u32[]{:S(2)}) async-start(bf16[4,1040,128]{2,1,0:T(8,128)(2,1)} %broadcast_in_dim.12), calls=%async_computation.1 | async-start | bytes 2129920 | tf_op jit(solution)/shard_map/all_to_all | solution.py:389
  54.2 3.4 %collective-permute-start = (bf16[1024,128]{1,0:T(8,128)(2,1)S(1)}, bf16[1024,128]{1,0:T(8,128)(2,1)S(1)}, u32[]{:S(2)}, u32[]{:S(2)}) collective-permute-start(bf16[1024,128]{1,0:T(8,128)(2,1)S(1)} %pad_maximum_fusion.kv0), channel_id=1, source_target_pairs={{0,128},{128,256},{256,384},{384,0},{1,129},{129,257},{257,385},{3... | collective-permute-start | bytes 786440 | tf_op jit(solution)/shard_map/ppermute | solution.py:358
  57.6 4.6 %collective-permute-start.1 = (bf16[1024,128]{1,0:T(8,128)(2,1)S(1)}, bf16[1024,128]{1,0:T(8,128)(2,1)S(1)}, u32[]{:S(2)}, u32[]{:S(2)}) collective-permute-start(bf16[1024,128]{1,0:T(8,128)(2,1)S(1)} %pad_maximum_fusion.kv0), channel_id=1, source_target_pairs={{0,256},{128,384},{256,0},{384,128},{1,257},{129,385},{257,1},{385... | collective-permute-start | bytes 786440 | tf_op jit(solution)/shard_map/ppermute | solution.py:358
  62.2 3.3 %collective-permute-start.2 = (bf16[1024,128]{1,0:T(8,128)(2,1)S(1)}, bf16[1024,128]{1,0:T(8,128)(2,1)S(1)}, u32[]{:S(2)}, u32[]{:S(2)}) collective-permute-start(bf16[1024,128]{1,0:T(8,128)(2,1)S(1)} %pad_maximum_fusion.kv0), channel_id=1, source_target_pairs={{0,384},{128,0},{256,128},{384,256},{1,385},{129,1},{257,129},{385... | collective-permute-start | bytes 786440 | tf_op jit(solution)/shard_map/ppermute | solution.py:358
  65.6 0.0 collective-permute-done.kv1
  65.6 1.9 %collective-permute-done.1.kv2 = bf16[1024,128]{1,0:T(8,128)(2,1)S(1)} collective-permute-done((bf16[1024,128]{1,0:T(8,128)(2,1)S(1)}, bf16[1024,128]{1,0:T(8,128)(2,1)S(1)}, u32[]{:S(2)}, u32[]{:S(2)}) %collective-permute-start.1) | collective-permute-done | bytes 262176 | tf_op jit(solution)/shard_map/ppermute | solution.py:358
  67.5 3.0 %collective-permute-done.2.kv3 = bf16[1024,128]{1,0:T(8,128)(2,1)S(1)} collective-permute-done((bf16[1024,128]{1,0:T(8,128)(2,1)S(1)}, bf16[1024,128]{1,0:T(8,128)(2,1)S(1)}, u32[]{:S(2)}, u32[]{:S(2)}) %collective-permute-start.2) | collective-permute-done | bytes 262176 | tf_op jit(solution)/shard_map/ppermute | solution.py:358
  70.5 0.0 all-to-all-done.1.own
  70.5 1.9 %collective-permute-start.3 = (bf16[4,1040,128]{2,1,0:T(8,128)(2,1)S(1)}, bf16[4,1040,128]{2,1,0:T(8,128)(2,1)S(1)}, u32[]{:S(2)}, u32[]{:S(2)}) collective-permute-start(bf16[4,1040,128]{2,1,0:T(8,128)(2,1)S(1)} %all-to-all-done.1.own), channel_id=1, source_target_pairs={{0,16},{16,0},{1,17},{17,1},{2,18},{18,2},{3,19},{19,3},{4,20},{20... | collective-permute-start | bytes 3194888 | tf_op jit(solution)/shard_map/ppermute | solution.py:358
  72.4 2.6 %collective-permute-done.3.other = bf16[4,1040,128]{2,1,0:T(8,128)(2,1)S(1)} collective-permute-done((bf16[4,1040,128]{2,1,0:T(8,128)(2,1)S(1)}, bf16[4,1040,128]{2,1,0:T(8,128)(2,1)S(1)}, u32[]{:S(2)}, u32[]{:S(2)}) %collective-permute-start.3) | collective-permute-done | bytes 1064992 | tf_op jit(solution)/shard_map/ppermute | solution.py:358
  75.1 7.0 %shard_map.104 = (bf16[32,512,512]{2,1,0:T(8,128)(2,1)}, f32[32,1,512]{2,1,0:T(1,128)S(1)}, f32[8,8,2,512]{3,2,1,0:T(2,128)}) custom-call(s32[32]{0:T(128)S(1)} %select_reduce_fusion.pairs, s32[4]{0:T(128)S(1)} %pad_add_fusion.meta, bf16[4,1040,128]{2,1,0:T(8,128)(2,1)S(1)} %all-to-all-done.1.own, bf16[4,1040,128]{2,1,0:T(8,128)(2,1)S(1)} %collective-permute-done.3.other, ...), custom_call_target="tpu_custom_call" | custom-call | tf_op jit(solution)/shard_map/pallas_call | solution.py:326
  82.1 5.0 %all-to-all-start.3 = ((f32[8,8,2,512]{3,2,1,0:T(2,128)}), f32[8,8,2,512]{3,2,1,0:T(2,128)S(1)}, u32[]{:S(2)}, u32[]{:S(2)}) async-start(f32[8,8,2,512]{3,2,1,0:T(2,128)} %get-tuple-element.32.stats_in), calls=%async_computation.3 | async-start | bytes 524288 | tf_op jit(solution)/shard_map/all_to_all | solution.py:403
  87.0 8.5 %shard_map.105 = (bf16[32,512,512]{2,1,0:T(8,128)(2,1)}, bf16[8,512,128]{2,1,0:T(8,128)(2,1)}) custom-call(s32[32]{0:T(128)S(1)} %select_reduce_fusion.pairs, s32[4]{0:T(128)S(1)} %pad_add_fusion.meta, bf16[4,1040,128]{2,1,0:T(8,128)(2,1)S(1)} %all-to-all-done.1.own, bf16[4,1040,128]{2,1,0:T(8,128)(2,1)S(1)} %collective-permute-done.3.other, ...), custom_call_target="tpu_custom_call" | custom-call | tf_op jit(solution)/shard_map/pallas_call | solution.py:326
  95.6 0.0 all-to-all-done.3.stats_in.stats_all
  95.6 5.1 %all-to-all-start.2 = ((bf16[8,512,128]{2,1,0:T(8,128)(2,1)}), bf16[8,512,128]{2,1,0:T(8,128)(2,1)S(1)}, u32[]{:S(2)}, u32[]{:S(2)}) async-start(bf16[8,512,128]{2,1,0:T(8,128)(2,1)} %get-tuple-element.34), calls=%async_computation.2 | async-start | bytes 2097152 | tf_op jit(solution)/shard_map/all_to_all | solution.py:416
  100.7 8.4 %shard_map.107 = (bf16[2,512,128]{2,1,0:T(8,128)(2,1)}, bf16[2,512,128]{2,1,0:T(8,128)(2,1)}, bf16[2,512,128]{2,1,0:T(8,128)(2,1)}) custom-call(s32[32]{0:T(128)S(1)} %select_reduce_fusion.pairs, s32[4]{0:T(128)S(1)} %pad_add_fusion.meta, bf16[4,1040,128]{2,1,0:T(8,128)(2,1)S(1)} %all-to-all-done.1.own, ...), custom_call_target="tpu_custom_call" | custom-call | tf_op jit(solution)/shard_map/pallas_call | solution.py:326
  109.1 5.8 %collective-permute-start.4 = (bf16[2,512,128]{2,1,0:T(8,128)(2,1)}, bf16[2,512,128]{2,1,0:T(8,128)(2,1)}, u32[]{:S(2)}, u32[]{:S(2)}) collective-permute-start(bf16[2,512,128]{2,1,0:T(8,128)(2,1)} %get-tuple-element.40), channel_id=1, source_target_pairs={{0,384},{128,0},{256,128},{384,256},{1,385},{129,1},{257,129},{385... | collective-permute-start | bytes 786440 | tf_op jit(solution)/shard_map/ppermute | solution.py:358
  115.0 1.9 %collective-permute-start.5 = (bf16[2,512,128]{2,1,0:T(8,128)(2,1)}, bf16[2,512,128]{2,1,0:T(8,128)(2,1)}, u32[]{:S(2)}, u32[]{:S(2)}) collective-permute-start(bf16[2,512,128]{2,1,0:T(8,128)(2,1)} %get-tuple-element.41), channel_id=1, source_target_pairs={{0,256},{128,384},{256,0},{384,128},{1,257},{129,385},{257,1},{385... | collective-permute-start | bytes 786440 | tf_op jit(solution)/shard_map/ppermute | solution.py:358
  116.9 2.8 %collective-permute-start.6 = (bf16[2,512,128]{2,1,0:T(8,128)(2,1)}, bf16[2,512,128]{2,1,0:T(8,128)(2,1)}, u32[]{:S(2)}, u32[]{:S(2)}) collective-permute-start(bf16[2,512,128]{2,1,0:T(8,128)(2,1)} %get-tuple-element.42), channel_id=1, source_target_pairs={{0,128},{128,256},{256,384},{384,0},{1,129},{129,257},{257,385},{3... | collective-permute-start | bytes 786440 | tf_op jit(solution)/shard_map/ppermute | solution.py:358
  119.7 5.2 %shard_map.108.kept = bf16[2,512,128]{2,1,0:T(8,128)(2,1)S(1)} custom-call(s32[32]{0:T(128)S(1)} %select_reduce_fusion.pairs, s32[4]{0:T(128)S(1)} %pad_add_fusion.meta, bf16[4,1040,128]{2,1,0:T(8,128)(2,1)S(1)} %all-to-all-done.1.own, bf16[4,1040,128]{2,1,0:T(8,128)(2,1)S(1)} %collective-permute-done.3.other, ...), custom_call_target="tpu_custom_call" | custom-call | tf_op jit(solution)/shard_map/pallas_call | solution.py:326
  124.9 0.0 copy-start.1
  124.9 0.7 copy-done.1
  125.6 0.0 all-to-all-done.2.dquery_in
  125.6 0.0 copy-start.2
  125.6 1.5 shard_map.106.query_grad
  127.1 0.0 collective-permute-done.4.first
  127.1 0.8 collective-permute-done.5.second
  127.9 4.6 %collective-permute-done.6.third = bf16[2,512,128]{2,1,0:T(8,128)(2,1)} collective-permute-done((bf16[2,512,128]{2,1,0:T(8,128)(2,1)}, bf16[2,512,128]{2,1,0:T(8,128)(2,1)}, u32[]{:S(2)}, u32[]{:S(2)}) %collective-permute-start.6) | collective-permute-done | bytes 262176 | tf_op jit(solution)/shard_map/ppermute | solution.py:358
  132.5 0.0 copy-done.2
  132.5 1.3 shard_map.109
  133.8 33.3 %all_to_all.25 = bf16[16,96,128]{2,1,0:T(8,128)(2,1)S(1)} all-to-all(bf16[16,96,128]{2,1,0:T(8,128)(2,1)S(1)} %shard_map.109), channel_id=1, replica_groups=mesh['x'=4,'y'=4,'c'=2,'h'=16] {'h'}, dimensions={0} | all-to-all | bytes 786432 | tf_op jit(solution)/shard_map/all_to_all | solution.py:458
  167.1 0.7 copy.28
  167.8 0.7 copy_bitcast_fusion
  (13 shorter events, 0.2 us)
Async XLA Ops:
  0.6 17.6 %copy-start = (s32[32]{0:T(128)S(1)}, s32[32]{0:T(128)}, u32[]{:S(2)}) copy-start(s32[32]{0:T(128)} %param.15) | copy-start | bytes 388
  0.6 17.5 %copy-start.4 = (s32[32,16]{0,1:T(8,128)S(1)}, s32[32,16]{0,1:T(8,128)}, u32[]{:S(2)}) copy-start(s32[32,16]{0,1:T(8,128)} %param.13) | copy-start | bytes 6148
  2.9 16.6 %copy-start.3 = (s32[32]{0:T(128)S(1)}, s32[32]{0:T(128)}, u32[]{:S(2)}) copy-start(s32[32]{0:T(128)} %param.14) | copy-start | bytes 388
  2.9 45.2 %all-to-all-start = ((bf16[16,136,128]{2,1,0:T(8,128)(2,1)}), bf16[16,136,128]{2,1,0:T(8,128)(2,1)S(1)}, u32[]{:S(2)}, u32[]{:S(2)}) async-start(bf16[16,136,128]{2,1,0:T(8,128)(2,1)} %shard_map.103), calls=%async_computation | async-start | bytes 1114112 | tf_op jit(solution)/shard_map/all_to_all | solution.py:377
  49.5 21.0 %all-to-all-start.1 = ((bf16[4,1040,128]{2,1,0:T(8,128)(2,1)}), bf16[4,1040,128]{2,1,0:T(8,128)(2,1)S(1)}, u32[]{:S(2)}, u32[]{:S(2)}) async-start(bf16[4,1040,128]{2,1,0:T(8,128)(2,1)} %broadcast_in_dim.12), calls=%async_computation.1 | async-start | bytes 2129920 | tf_op jit(solution)/shard_map/all_to_all | solution.py:389
  54.2 11.4 %collective-permute-start = (bf16[1024,128]{1,0:T(8,128)(2,1)S(1)}, bf16[1024,128]{1,0:T(8,128)(2,1)S(1)}, u32[]{:S(2)}, u32[]{:S(2)}) collective-permute-start(bf16[1024,128]{1,0:T(8,128)(2,1)S(1)} %pad_maximum_fusion.kv0), channel_id=1, source_target_pairs={{0,128},{128,256},{256,384},{384,0},{1,129},{129,257},{257,385},{3... | collective-permute-start | bytes 786440 | tf_op jit(solution)/shard_map/ppermute | solution.py:358
  57.6 9.9 %collective-permute-start.1 = (bf16[1024,128]{1,0:T(8,128)(2,1)S(1)}, bf16[1024,128]{1,0:T(8,128)(2,1)S(1)}, u32[]{:S(2)}, u32[]{:S(2)}) collective-permute-start(bf16[1024,128]{1,0:T(8,128)(2,1)S(1)} %pad_maximum_fusion.kv0), channel_id=1, source_target_pairs={{0,256},{128,384},{256,0},{384,128},{1,257},{129,385},{257,1},{385... | collective-permute-start | bytes 786440 | tf_op jit(solution)/shard_map/ppermute | solution.py:358
  62.2 8.3 %collective-permute-start.2 = (bf16[1024,128]{1,0:T(8,128)(2,1)S(1)}, bf16[1024,128]{1,0:T(8,128)(2,1)S(1)}, u32[]{:S(2)}, u32[]{:S(2)}) collective-permute-start(bf16[1024,128]{1,0:T(8,128)(2,1)S(1)} %pad_maximum_fusion.kv0), channel_id=1, source_target_pairs={{0,384},{128,0},{256,128},{384,256},{1,385},{129,1},{257,129},{385... | collective-permute-start | bytes 786440 | tf_op jit(solution)/shard_map/ppermute | solution.py:358
  70.5 4.6 %collective-permute-start.3 = (bf16[4,1040,128]{2,1,0:T(8,128)(2,1)S(1)}, bf16[4,1040,128]{2,1,0:T(8,128)(2,1)S(1)}, u32[]{:S(2)}, u32[]{:S(2)}) collective-permute-start(bf16[4,1040,128]{2,1,0:T(8,128)(2,1)S(1)} %all-to-all-done.1.own), channel_id=1, source_target_pairs={{0,16},{16,0},{1,17},{17,1},{2,18},{18,2},{3,19},{19,3},{4,20},{20... | collective-permute-start | bytes 3194888 | tf_op jit(solution)/shard_map/ppermute | solution.py:358
  82.1 13.5 %all-to-all-start.3 = ((f32[8,8,2,512]{3,2,1,0:T(2,128)}), f32[8,8,2,512]{3,2,1,0:T(2,128)S(1)}, u32[]{:S(2)}, u32[]{:S(2)}) async-start(f32[8,8,2,512]{3,2,1,0:T(2,128)} %get-tuple-element.32.stats_in), calls=%async_computation.3 | async-start | bytes 524288 | tf_op jit(solution)/shard_map/all_to_all | solution.py:403
  95.6 30.0 %all-to-all-start.2 = ((bf16[8,512,128]{2,1,0:T(8,128)(2,1)}), bf16[8,512,128]{2,1,0:T(8,128)(2,1)S(1)}, u32[]{:S(2)}, u32[]{:S(2)}) async-start(bf16[8,512,128]{2,1,0:T(8,128)(2,1)} %get-tuple-element.34), calls=%async_computation.2 | async-start | bytes 2097152 | tf_op jit(solution)/shard_map/all_to_all | solution.py:416
  109.1 18.0 %collective-permute-start.4 = (bf16[2,512,128]{2,1,0:T(8,128)(2,1)}, bf16[2,512,128]{2,1,0:T(8,128)(2,1)}, u32[]{:S(2)}, u32[]{:S(2)}) collective-permute-start(bf16[2,512,128]{2,1,0:T(8,128)(2,1)} %get-tuple-element.40), channel_id=1, source_target_pairs={{0,384},{128,0},{256,128},{384,256},{1,385},{129,1},{257,129},{385... | collective-permute-start | bytes 786440 | tf_op jit(solution)/shard_map/ppermute | solution.py:358
  115.0 12.9 %collective-permute-start.5 = (bf16[2,512,128]{2,1,0:T(8,128)(2,1)}, bf16[2,512,128]{2,1,0:T(8,128)(2,1)}, u32[]{:S(2)}, u32[]{:S(2)}) collective-permute-start(bf16[2,512,128]{2,1,0:T(8,128)(2,1)} %get-tuple-element.41), channel_id=1, source_target_pairs={{0,256},{128,384},{256,0},{384,128},{1,257},{129,385},{257,1},{385... | collective-permute-start | bytes 786440 | tf_op jit(solution)/shard_map/ppermute | solution.py:358
  116.9 15.6 %collective-permute-start.6 = (bf16[2,512,128]{2,1,0:T(8,128)(2,1)}, bf16[2,512,128]{2,1,0:T(8,128)(2,1)}, u32[]{:S(2)}, u32[]{:S(2)}) collective-permute-start(bf16[2,512,128]{2,1,0:T(8,128)(2,1)} %get-tuple-element.42), channel_id=1, source_target_pairs={{0,128},{128,256},{256,384},{384,0},{1,129},{129,257},{257,385},{3... | collective-permute-start | bytes 786440 | tf_op jit(solution)/shard_map/ppermute | solution.py:358
  124.9 0.7 copy-start.1
  125.6 6.9 %copy-start.2 = (bf16[2,512,128]{2,1,0:T(8,128)(2,1)S(1)}, bf16[2,512,128]{2,1,0:T(8,128)(2,1)}, u32[]{:S(2)}) copy-start(bf16[2,512,128]{2,1,0:T(8,128)(2,1)} %copy-done.1) | copy-start | bytes 786436

commit v6 on v5

--- a/solution.py
+++ b/solution.py
@@ -62,15 +62,19 @@
     count = meta[0]
     steps = (count + UNROLL - 1) // UNROLL
 
-    def store(step):
+    def store(step, u):
         return pltpu.make_async_copy(
-            held.at[step & 1], probs.at[pl.ds(step * UNROLL, UNROLL)], out_sems.at[step & 1]
+            held.at[step & 1, u], probs.at[step * UNROLL + u], out_sems.at[step & 1, u]
         )
+
+    def wait_stores(step):
+        for u in range(UNROLL):
+            store(step, u).wait()
 
     def visit(step, first):
         @pl.when(step >= 2)
         def _():
-            store(step - 2).wait()
+            wait_stores(step - 2)
 
         found = []
         for u in range(UNROLL):
@@ -87,6 +91,7 @@
             values = jnp.exp2(scores * SCALE2 - top)
             total = jnp.sum(values, axis=0, keepdims=True)
             held[step & 1, u] = values.astype(jnp.bfloat16)
+            store(step, u).start()
             tops[t] = top
             top = jnp.where(t < count, top, LOW)
             total = jnp.where(t < count, total, 0.0)
@@ -94,7 +99,6 @@
             new_top = jnp.maximum(old_top, top)
             stats[place, 0:1, :] = new_top
             stats[place, 1:2, :] = old_total * jnp.exp2(old_top - new_top) + total * jnp.exp2(top - new_top)
-        store(step).start()
 
     visit(0, True)
 
@@ -108,11 +112,11 @@
         copy.start()
     for copy in sent:
         copy.wait()
-    store(steps - 1).wait()
+    wait_stores(steps - 1)
 
     @pl.when(steps >= 2)
     def _():
-        store(steps - 2).wait()
+        wait_stores(steps - 2)
 
 
 def dscore_kernel(
@@ -126,10 +130,14 @@
         span = pl.ds(step * UNROLL, UNROLL)
         return pltpu.make_async_copy(probs_in.at[span], probs.at[span], in_sems.at[step])
 
-    def store(step):
+    def store(step, u):
         return pltpu.make_async_copy(
-            held.at[step & 1], dscore.at[pl.ds(step * UNROLL, UNROLL)], out_sems.at[step & 1]
+            held.at[step & 1, u], dscore.at[step * UNROLL + u], out_sems.at[step & 1, u]
         )
+
+    def wait_stores(step):
+        for u in range(UNROLL):
+            store(step, u).wait()
 
     key_fetches = fetch_keys((kv0, kv1, kv2, kv3), kv, key_sems)
     fetches = fetch_queries(own, other, qd, sems)
@@ -154,7 +162,7 @@
 
         @pl.when(step >= 2)
         def _():
-            store(step - 2).wait()
+            wait_stores(step - 2)
 
         found = []
         for u in range(UNROLL):
@@ -168,24 +176,24 @@
             dprob = dot(kv[key, BLK:, :], qd[query, BLK : 2 * BLK, :], (1, 1))
             low = (probs[t].astype(jnp.float32) * (dprob - row_dot)).astype(jnp.bfloat16)
             held[step & 1, u] = low
+            store(step, u).start()
             found.append((place, dot(keys_t[key], low, (1, 0)) * weight))
         for place, part in found:
             total[place] += part
-        store(step).start()
         return 0
 
     lax.fori_loop(0, steps, body, 0)
     sent = [pltpu.make_async_copy(dquery_held.at[i], dquery.at[i], dquery_sems.at[i]) for i in range(NQ)]
     for i in range(NQ):
-        dquery_held[i] = jnp.transpose(total[i]).astype(jnp.bfloat16)
+        dquery_held[i] = total[i].astype(jnp.bfloat16)
         sent[i].start()
     for copy in sent:
         copy.wait()
-    store(steps - 1).wait()
+    wait_stores(steps - 1)
 
     @pl.when(steps >= 2)
     def _():
-        store(steps - 2).wait()
+        wait_stores(steps - 2)
 
 
 def log_norms(stats_all):
@@ -213,10 +221,11 @@
             copy.start()
         return 0
 
+    lax.fori_loop(0, jnp.minimum(steps, 1), start, 0)
     fetches = fetch_queries(own, other, qd, sems)
     for fetch in fetches:
         fetch.start()
-    lax.fori_loop(0, steps, start, 0)
+    lax.fori_loop(1, steps, start, 0)
     total[...] = jnp.zeros_like(total)
     norms[:, 0, :] = log_norms(stats_all[...])
     for fetch in fetches:
@@ -289,11 +298,11 @@
     tops, sums = stats_all[:, place, 0, :], stats_all[:, place, 1, :]
     top = jnp.max(tops, axis=0, keepdims=True)
     norm = top + jnp.log2(jnp.sum(sums * jnp.exp2(tops - top), axis=0, keepdims=True))
-    weight = jnp.transpose(jnp.exp2(tops - norm) * SCALE)
-    grad = dquery[0].astype(jnp.float32) * weight[:, 0:1]
+    weight = jnp.exp2(tops - norm) * SCALE
+    grad = dquery[0].astype(jnp.float32) * weight[0:1]
     for i in range(1, NQ):
-        grad += dquery[i].astype(jnp.float32) * weight[:, i : i + 1]
-    out[...] = grad.astype(jnp.bfloat16)
+        grad += dquery[i].astype(jnp.float32) * weight[i : i + 1]
+    out[...] = jnp.transpose(grad).astype(jnp.bfloat16)
 
 
 def finish_kernel(query_grad, kept, first, second, third, out, parts, query_held, sems):
@@ -398,7 +407,7 @@
         [anywhere] * 6,
         [anywhere, vmem, anywhere],
         [square, line, pltpu.HBM((NQ, NQ, 2, BLK), f32)],
-        [qd_scratch, kv_scratch, pltpu.VMEM((NQ, 2, BLK), f32), pltpu.VMEM((2, UNROLL, BLK, BLK), bf16), dma((2,)), dma((NK,)), dma((2,)), dma((NQ,))],
+        [qd_scratch, kv_scratch, pltpu.VMEM((NQ, 2, BLK), f32), pltpu.VMEM((2, UNROLL, BLK, BLK), bf16), dma((2,)), dma((NK,)), dma((2, UNROLL)), dma((NQ,))],
     )
     stats_all = lax.all_to_all(stats, ("y", "c"), 0, 0, tiled=True)
     tiles, two_steps = pltpu.VMEM((NPAIR, BLK, BLK), bf16), pltpu.VMEM((2, UNROLL, BLK, BLK), bf16)
@@ -407,10 +416,10 @@
         dscore_kernel, 44, pairs, meta, (*queries, *keys, in_hbm(probs), in_hbm(stats), tops),
         [anywhere] * 8 + [vmem],
         [anywhere, anywhere],
-        [square, pltpu.HBM((NQ, BLK, HD), bf16)],
+        [square, pltpu.HBM((NQ, HD, BLK), bf16)],
         [
             qd_scratch, kv_scratch, pltpu.VMEM((NK, HD, BLK), bf16), pltpu.VMEM((NQ, HD, BLK), f32),
-            pltpu.VMEM((NQ, 2, BLK), f32), tiles, two_steps, pltpu.VMEM((NQ, BLK, HD), bf16), dma((3,)), dma((NK,)), step_dma, dma((2,)), dma((NQ,)),
+            pltpu.VMEM((NQ, 2, BLK), f32), tiles, two_steps, pltpu.VMEM((NQ, HD, BLK), bf16), dma((3,)), dma((NK,)), step_dma, dma((2, UNROLL)), dma((NQ,)),
         ],
     )
     dquery = lax.all_to_all(dquery, ("y", "c"), 0, 0, tiled=True)
@@ -442,7 +451,7 @@
             grid=(1,),
             in_specs=[anywhere] * 2,
             out_specs=vmem,
-            scratch_shapes=[pltpu.VMEM((NQ, BLK, HD), bf16), pltpu.VMEM((NQ, NQ, 2, BLK), f32), dma((2,))],
+            scratch_shapes=[pltpu.VMEM((NQ, HD, BLK), bf16), pltpu.VMEM((NQ, NQ, 2, BLK), f32), dma((2,))],
         ),
         out_shape=shape((BLK, HD), bf16),
         compiler_params=params(12),

time: 170 us -> 172 us (1.012)
  Pallas kernels: 34.2 us -> 26.6 us
  starting transfers between devices: 53.8 us -> 61.1 us
    pallas_call x4, Pallas kernels: 29.1 us -> 22 us  [over_pairs(): pl.pallas_call(kernel, grid_spec=pltpu.PrefetchScalarGridSpec(num_scalar_...]
    all_to_all x1, starting transfers between devices: 4.97 us -> 9.39 us  [on_device(): stats_all = lax.all_to_all(stats, ('y', 'c'), 0, 0, tiled=True)]
    all_to_all x1, starting transfers between devices: 5.09 us -> 9.28 us  [on_device(): dquery = lax.all_to_all(dquery, ('y', 'c'), 0, 0, tiled=True)]
  transfers between devices with their start and end apart: 11 -> 11, of which waited for: 6 -> 5; matrix products, arithmetic and copies ran while one was open for 4% -> 4% of each run, Pallas kernels for 14% -> 11%
where the time goes in v6:
time: 172 us; the launch traced here: 169 us
  starting transfers between devices  61.1 us (36%)
  waiting for transfers between devices  35.9 us (21%)
  blocking collectives  34.4 us (20%)
  Pallas kernels  26.6 us (15%)
  local copies, waits for them, and re-layouts  6.14 us (4%)
  other arithmetic  3.4 us (2%)
    all_to_all x1, blocking collectives, on_device(): grads = lax.all_to_all(grads, 'h', 0, 0, tiled=True)  34.4 us
    all_to_all x1, waiting for transfers between devices, on_device(): packed = lax.all_to_all(packed, 'h', 0, 0, tiled=True)  23.2 us
    ppermute x7, starting transfers between devices, shifted(): lax.ppermute(array, axis, [(i, (i + by) % size) for i in range(size)])  22.5 us
    pallas_call x4, Pallas kernels, over_pairs(): pl.pallas_call(kernel, grid_spec=pltpu.PrefetchScalarGridSpec(num_scalar_...  22 us
    all_to_all x1, starting transfers between devices, on_device(): packed = lax.all_to_all(packed, 'h', 0, 0, tiled=True)  15.2 us
    ppermute x7, waiting for transfers between devices, shifted(): lax.ppermute(array, axis, [(i, (i + by) % size) for i in range(size)])  12.7 us
    all_to_all x1, starting transfers between devices, on_device(): stats_all = lax.all_to_all(stats, ('y', 'c'), 0, 0, tiled=True)  9.39 us
    all_to_all x1, starting transfers between devices, on_device(): dquery = lax.all_to_all(dquery, ('y', 'c'), 0, 0, tiled=True)  9.28 us
  transfers between devices with their start and end apart: 11, of which 5 were waited for; matrix products, arithmetic and copies ran while one was open for 4% of the time, Pallas kernels for 11%

profile of v6, /device:TPU:24, one launch (start us, length us, event | category | flops | bytes accessed | tf_op | source)
XLA Modules:
  0.0 169.1 jit_solution(7414443850807351677)
XLA Ops:
  0.6 0.0 copy-start
  0.6 0.0 copy-start.4
  0.7 2.3 %shard_map.103 = bf16[16,136,128]{2,1,0:T(8,128)(2,1)} custom-call(bf16[32,2048]{1,0:T(8,128)(2,1)} %query_in.1, bf16[32,2048]{1,0:T(8,128)(2,1)} %key_in.1, bf16[32,2048]{1,0:T(8,128)(2,1)} %value_in.1, bf16[32,2048]{1,0:T(8,128)(2,1)} %output_in.1, bf16[32,2048]{1,0:T(8,128)(2,1)} %grad_in.1), custom_call_target="tpu_custom_call" | custom-call | tf_op jit(solution)/shard_map/pallas_call | solution.py:378
  2.9 0.0 copy-start.3
  2.9 15.2 %all-to-all-start = ((bf16[16,136,128]{2,1,0:T(8,128)(2,1)}), bf16[16,136,128]{2,1,0:T(8,128)(2,1)S(1)}, u32[]{:S(2)}, u32[]{:S(2)}) async-start(bf16[16,136,128]{2,1,0:T(8,128)(2,1)} %shard_map.103), calls=%async_computation | async-start | bytes 1114112 | tf_op jit(solution)/shard_map/all_to_all | solution.py:386
  18.2 0.0 copy-done.4
  18.2 0.1 copy.17
  18.3 0.0 copy-done
  18.3 0.6 gather_fusion
  18.9 0.6 gather_fusion.1
  19.5 0.0 copy-done.3
  19.5 0.6 gather_fusion.3
  20.2 0.6 gather_fusion.2
  20.8 0.1 iota_compare_fusion.1
  20.9 0.2 and_reduce_fusion
  21.1 0.1 and.87
  21.2 0.7 convert_reduce_fusion.1
  22.6 0.6 fusion.8
  23.2 1.4 pad_add_fusion.meta
  24.6 0.1 convert_reduce_fusion
  24.8 0.2 select_reduce_fusion.pairs
  24.9 23.2 %all-to-all-done = bf16[16,136,128]{2,1,0:T(8,128)(2,1)S(1)} async-done(((bf16[16,136,128]{2,1,0:T(8,128)(2,1)}), bf16[16,136,128]{2,1,0:T(8,128)(2,1)S(1)}, u32[]{:S(2)}, u32[]{:S(2)}) %all-to-all-start) | async-done | bytes 557088 | tf_op jit(solution)/shard_map/all_to_all | solution.py:386
  48.2 0.1 reshape.227
  48.3 0.1 concatenate.6
  48.4 1.1 broadcast_in_dim.12
  49.5 4.7 %all-to-all-start.1 = ((bf16[4,1040,128]{2,1,0:T(8,128)(2,1)}), bf16[4,1040,128]{2,1,0:T(8,128)(2,1)S(1)}, u32[]{:S(2)}, u32[]{:S(2)}) async-start(bf16[4,1040,128]{2,1,0:T(8,128)(2,1)} %broadcast_in_dim.12), calls=%async_computation.1 | async-start | bytes 2129920 | tf_op jit(solution)/shard_map/all_to_all | solution.py:398
  54.2 3.4 %collective-permute-start = (bf16[1024,128]{1,0:T(8,128)(2,1)S(1)}, bf16[1024,128]{1,0:T(8,128)(2,1)S(1)}, u32[]{:S(2)}, u32[]{:S(2)}) collective-permute-start(bf16[1024,128]{1,0:T(8,128)(2,1)S(1)} %pad_maximum_fusion.kv0), channel_id=1, source_target_pairs={{0,128},{128,256},{256,384},{384,0},{1,129},{129,257},{257,385},{3... | collective-permute-start | bytes 786440 | tf_op jit(solution)/shard_map/ppermute | solution.py:367
  57.6 4.6 %collective-permute-start.1 = (bf16[1024,128]{1,0:T(8,128)(2,1)S(1)}, bf16[1024,128]{1,0:T(8,128)(2,1)S(1)}, u32[]{:S(2)}, u32[]{:S(2)}) collective-permute-start(bf16[1024,128]{1,0:T(8,128)(2,1)S(1)} %pad_maximum_fusion.kv0), channel_id=1, source_target_pairs={{0,256},{128,384},{256,0},{384,128},{1,257},{129,385},{257,1},{385... | collective-permute-start | bytes 786440 | tf_op jit(solution)/shard_map/ppermute | solution.py:367
  62.2 3.3 %collective-permute-start.2 = (bf16[1024,128]{1,0:T(8,128)(2,1)S(1)}, bf16[1024,128]{1,0:T(8,128)(2,1)S(1)}, u32[]{:S(2)}, u32[]{:S(2)}) collective-permute-start(bf16[1024,128]{1,0:T(8,128)(2,1)S(1)} %pad_maximum_fusion.kv0), channel_id=1, source_target_pairs={{0,384},{128,0},{256,128},{384,256},{1,385},{129,1},{257,129},{385... | collective-permute-start | bytes 786440 | tf_op jit(solution)/shard_map/ppermute | solution.py:367
  65.6 0.0 collective-permute-done.kv1
  65.6 1.9 %collective-permute-done.1.kv2 = bf16[1024,128]{1,0:T(8,128)(2,1)S(1)} collective-permute-done((bf16[1024,128]{1,0:T(8,128)(2,1)S(1)}, bf16[1024,128]{1,0:T(8,128)(2,1)S(1)}, u32[]{:S(2)}, u32[]{:S(2)}) %collective-permute-start.1) | collective-permute-done | bytes 262176 | tf_op jit(solution)/shard_map/ppermute | solution.py:367
  67.5 3.0 %collective-permute-done.2.kv3 = bf16[1024,128]{1,0:T(8,128)(2,1)S(1)} collective-permute-done((bf16[1024,128]{1,0:T(8,128)(2,1)S(1)}, bf16[1024,128]{1,0:T(8,128)(2,1)S(1)}, u32[]{:S(2)}, u32[]{:S(2)}) %collective-permute-start.2) | collective-permute-done | bytes 262176 | tf_op jit(solution)/shard_map/ppermute | solution.py:367
  70.5 0.0 all-to-all-done.1.own
  70.5 1.9 %collective-permute-start.3 = (bf16[4,1040,128]{2,1,0:T(8,128)(2,1)S(1)}, bf16[4,1040,128]{2,1,0:T(8,128)(2,1)S(1)}, u32[]{:S(2)}, u32[]{:S(2)}) collective-permute-start(bf16[4,1040,128]{2,1,0:T(8,128)(2,1)S(1)} %all-to-all-done.1.own), channel_id=1, source_target_pairs={{0,16},{16,0},{1,17},{17,1},{2,18},{18,2},{3,19},{19,3},{4,20},{20... | collective-permute-start | bytes 3194888 | tf_op jit(solution)/shard_map/ppermute | solution.py:367
  72.4 2.6 %collective-permute-done.3.other = bf16[4,1040,128]{2,1,0:T(8,128)(2,1)S(1)} collective-permute-done((bf16[4,1040,128]{2,1,0:T(8,128)(2,1)S(1)}, bf16[4,1040,128]{2,1,0:T(8,128)(2,1)S(1)}, u32[]{:S(2)}, u32[]{:S(2)}) %collective-permute-start.3) | collective-permute-done | bytes 1064992 | tf_op jit(solution)/shard_map/ppermute | solution.py:367
  75.1 5.1 %shard_map.104 = (bf16[32,512,512]{2,1,0:T(8,128)(2,1)}, f32[32,1,512]{2,1,0:T(1,128)S(1)}, f32[8,8,2,512]{3,2,1,0:T(2,128)}) custom-call(s32[32]{0:T(128)S(1)} %select_reduce_fusion.pairs, s32[4]{0:T(128)S(1)} %pad_add_fusion.meta, bf16[4,1040,128]{2,1,0:T(8,128)(2,1)S(1)} %all-to-all-done.1.own, bf16[4,1040,128]{2,1,0:T(8,128)(2,1)S(1)} %collective-permute-done.3.other, ...), custom_call_target="tpu_custom_call" | custom-call | tf_op jit(solution)/shard_map/pallas_call | solution.py:335
  80.2 9.4 %all-to-all-start.3 = ((f32[8,8,2,512]{3,2,1,0:T(2,128)}), f32[8,8,2,512]{3,2,1,0:T(2,128)S(1)}, u32[]{:S(2)}, u32[]{:S(2)}) async-start(f32[8,8,2,512]{3,2,1,0:T(2,128)} %get-tuple-element.32.stats_in), calls=%async_computation.3 | async-start | bytes 524288 | tf_op jit(solution)/shard_map/all_to_all | solution.py:412
  89.6 6.6 %shard_map.105 = (bf16[32,512,512]{2,1,0:T(8,128)(2,1)}, bf16[8,128,512]{2,1,0:T(8,128)(2,1)}) custom-call(s32[32]{0:T(128)S(1)} %select_reduce_fusion.pairs, s32[4]{0:T(128)S(1)} %pad_add_fusion.meta, bf16[4,1040,128]{2,1,0:T(8,128)(2,1)S(1)} %all-to-all-done.1.own, bf16[4,1040,128]{2,1,0:T(8,128)(2,1)S(1)} %collective-permute-done.3.other, ...), custom_call_target="tpu_custom_call" | custom-call | tf_op jit(solution)/shard_map/pallas_call | solution.py:335
  96.2 0.0 all-to-all-done.3.stats_in.stats_all
  96.2 9.3 %all-to-all-start.2 = ((bf16[8,128,512]{2,1,0:T(8,128)(2,1)}), bf16[8,128,512]{2,1,0:T(8,128)(2,1)S(1)}, u32[]{:S(2)}, u32[]{:S(2)}) async-start(bf16[8,128,512]{2,1,0:T(8,128)(2,1)} %get-tuple-element.34), calls=%async_computation.2 | async-start | bytes 2097152 | tf_op jit(solution)/shard_map/all_to_all | solution.py:425
  105.5 6.0 %shard_map.107 = (bf16[2,512,128]{2,1,0:T(8,128)(2,1)}, bf16[2,512,128]{2,1,0:T(8,128)(2,1)}, bf16[2,512,128]{2,1,0:T(8,128)(2,1)}) custom-call(s32[32]{0:T(128)S(1)} %select_reduce_fusion.pairs, s32[4]{0:T(128)S(1)} %pad_add_fusion.meta, bf16[4,1040,128]{2,1,0:T(8,128)(2,1)S(1)} %all-to-all-done.1.own, ...), custom_call_target="tpu_custom_call" | custom-call | tf_op jit(solution)/shard_map/pallas_call | solution.py:335
  111.5 1.9 %collective-permute-start.4 = (bf16[2,512,128]{2,1,0:T(8,128)(2,1)}, bf16[2,512,128]{2,1,0:T(8,128)(2,1)}, u32[]{:S(2)}, u32[]{:S(2)}) collective-permute-start(bf16[2,512,128]{2,1,0:T(8,128)(2,1)} %get-tuple-element.40), channel_id=1, source_target_pairs={{0,384},{128,0},{256,128},{384,256},{1,385},{129,1},{257,129},{385... | collective-permute-start | bytes 786440 | tf_op jit(solution)/shard_map/ppermute | solution.py:367
  113.4 5.4 %collective-permute-start.5 = (bf16[2,512,128]{2,1,0:T(8,128)(2,1)}, bf16[2,512,128]{2,1,0:T(8,128)(2,1)}, u32[]{:S(2)}, u32[]{:S(2)}) collective-permute-start(bf16[2,512,128]{2,1,0:T(8,128)(2,1)} %get-tuple-element.41), channel_id=1, source_target_pairs={{0,256},{128,384},{256,0},{384,128},{1,257},{129,385},{257,1},{385... | collective-permute-start | bytes 786440 | tf_op jit(solution)/shard_map/ppermute | solution.py:367
  118.8 1.9 %collective-permute-start.6 = (bf16[2,512,128]{2,1,0:T(8,128)(2,1)}, bf16[2,512,128]{2,1,0:T(8,128)(2,1)}, u32[]{:S(2)}, u32[]{:S(2)}) collective-permute-start(bf16[2,512,128]{2,1,0:T(8,128)(2,1)} %get-tuple-element.42), channel_id=1, source_target_pairs={{0,128},{128,256},{256,384},{384,0},{1,129},{129,257},{257,385},{3... | collective-permute-start | bytes 786440 | tf_op jit(solution)/shard_map/ppermute | solution.py:367
  120.8 4.3 %shard_map.108.kept = bf16[2,512,128]{2,1,0:T(8,128)(2,1)S(1)} custom-call(s32[32]{0:T(128)S(1)} %select_reduce_fusion.pairs, s32[4]{0:T(128)S(1)} %pad_add_fusion.meta, bf16[4,1040,128]{2,1,0:T(8,128)(2,1)S(1)} %all-to-all-done.1.own, bf16[4,1040,128]{2,1,0:T(8,128)(2,1)S(1)} %collective-permute-done.3.other, ...), custom_call_target="tpu_custom_call" | custom-call | tf_op jit(solution)/shard_map/pallas_call | solution.py:335
  125.1 0.0 copy-start.1
  125.1 0.7 copy-done.1
  125.8 0.0 all-to-all-done.2.dquery_in
  125.8 0.0 copy-start.2
  125.8 1.0 shard_map.106.query_grad
  126.8 0.0 collective-permute-done.4.first
  126.8 0.0 collective-permute-done.5.second
  126.8 5.2 %collective-permute-done.6.third = bf16[2,512,128]{2,1,0:T(8,128)(2,1)} collective-permute-done((bf16[2,512,128]{2,1,0:T(8,128)(2,1)}, bf16[2,512,128]{2,1,0:T(8,128)(2,1)}, u32[]{:S(2)}, u32[]{:S(2)}) %collective-permute-start.6) | collective-permute-done | bytes 262176 | tf_op jit(solution)/shard_map/ppermute | solution.py:367
  132.0 0.0 copy-done.2
  132.0 1.3 shard_map.109
  133.3 34.4 %all_to_all.25 = bf16[16,96,128]{2,1,0:T(8,128)(2,1)S(1)} all-to-all(bf16[16,96,128]{2,1,0:T(8,128)(2,1)S(1)} %shard_map.109), channel_id=1, replica_groups=mesh['x'=4,'y'=4,'c'=2,'h'=16] {'h'}, dimensions={0} | all-to-all | bytes 786432 | tf_op jit(solution)/shard_map/all_to_all | solution.py:467
  167.7 0.7 copy.28
  168.4 0.7 copy_bitcast_fusion
  (13 shorter events, 0.2 us)
Async XLA Ops:
  0.6 17.6 %copy-start = (s32[32]{0:T(128)S(1)}, s32[32]{0:T(128)}, u32[]{:S(2)}) copy-start(s32[32]{0:T(128)} %param.15) | copy-start | bytes 388
  0.6 17.5 %copy-start.4 = (s32[32,16]{0,1:T(8,128)S(1)}, s32[32,16]{0,1:T(8,128)}, u32[]{:S(2)}) copy-start(s32[32,16]{0,1:T(8,128)} %param.13) | copy-start | bytes 6148
  2.9 16.6 %copy-start.3 = (s32[32]{0:T(128)S(1)}, s32[32]{0:T(128)}, u32[]{:S(2)}) copy-start(s32[32]{0:T(128)} %param.14) | copy-start | bytes 388
  2.9 45.2 %all-to-all-start = ((bf16[16,136,128]{2,1,0:T(8,128)(2,1)}), bf16[16,136,128]{2,1,0:T(8,128)(2,1)S(1)}, u32[]{:S(2)}, u32[]{:S(2)}) async-start(bf16[16,136,128]{2,1,0:T(8,128)(2,1)} %shard_map.103), calls=%async_computation | async-start | bytes 1114112 | tf_op jit(solution)/shard_map/all_to_all | solution.py:386
  49.5 21.0 %all-to-all-start.1 = ((bf16[4,1040,128]{2,1,0:T(8,128)(2,1)}), bf16[4,1040,128]{2,1,0:T(8,128)(2,1)S(1)}, u32[]{:S(2)}, u32[]{:S(2)}) async-start(bf16[4,1040,128]{2,1,0:T(8,128)(2,1)} %broadcast_in_dim.12), calls=%async_computation.1 | async-start | bytes 2129920 | tf_op jit(solution)/shard_map/all_to_all | solution.py:398
  54.2 11.4 %collective-permute-start = (bf16[1024,128]{1,0:T(8,128)(2,1)S(1)}, bf16[1024,128]{1,0:T(8,128)(2,1)S(1)}, u32[]{:S(2)}, u32[]{:S(2)}) collective-permute-start(bf16[1024,128]{1,0:T(8,128)(2,1)S(1)} %pad_maximum_fusion.kv0), channel_id=1, source_target_pairs={{0,128},{128,256},{256,384},{384,0},{1,129},{129,257},{257,385},{3... | collective-permute-start | bytes 786440 | tf_op jit(solution)/shard_map/ppermute | solution.py:367
  57.6 9.9 %collective-permute-start.1 = (bf16[1024,128]{1,0:T(8,128)(2,1)S(1)}, bf16[1024,128]{1,0:T(8,128)(2,1)S(1)}, u32[]{:S(2)}, u32[]{:S(2)}) collective-permute-start(bf16[1024,128]{1,0:T(8,128)(2,1)S(1)} %pad_maximum_fusion.kv0), channel_id=1, source_target_pairs={{0,256},{128,384},{256,0},{384,128},{1,257},{129,385},{257,1},{385... | collective-permute-start | bytes 786440 | tf_op jit(solution)/shard_map/ppermute | solution.py:367
  62.2 8.3 %collective-permute-start.2 = (bf16[1024,128]{1,0:T(8,128)(2,1)S(1)}, bf16[1024,128]{1,0:T(8,128)(2,1)S(1)}, u32[]{:S(2)}, u32[]{:S(2)}) collective-permute-start(bf16[1024,128]{1,0:T(8,128)(2,1)S(1)} %pad_maximum_fusion.kv0), channel_id=1, source_target_pairs={{0,384},{128,0},{256,128},{384,256},{1,385},{129,1},{257,129},{385... | collective-permute-start | bytes 786440 | tf_op jit(solution)/shard_map/ppermute | solution.py:367
  70.5 4.6 %collective-permute-start.3 = (bf16[4,1040,128]{2,1,0:T(8,128)(2,1)S(1)}, bf16[4,1040,128]{2,1,0:T(8,128)(2,1)S(1)}, u32[]{:S(2)}, u32[]{:S(2)}) collective-permute-start(bf16[4,1040,128]{2,1,0:T(8,128)(2,1)S(1)} %all-to-all-done.1.own), channel_id=1, source_target_pairs={{0,16},{16,0},{1,17},{17,1},{2,18},{18,2},{3,19},{19,3},{4,20},{20... | collective-permute-start | bytes 3194888 | tf_op jit(solution)/shard_map/ppermute | solution.py:367
  80.2 16.1 %all-to-all-start.3 = ((f32[8,8,2,512]{3,2,1,0:T(2,128)}), f32[8,8,2,512]{3,2,1,0:T(2,128)S(1)}, u32[]{:S(2)}, u32[]{:S(2)}) async-start(f32[8,8,2,512]{3,2,1,0:T(2,128)} %get-tuple-element.32.stats_in), calls=%async_computation.3 | async-start | bytes 524288 | tf_op jit(solution)/shard_map/all_to_all | solution.py:412
  96.2 29.6 %all-to-all-start.2 = ((bf16[8,128,512]{2,1,0:T(8,128)(2,1)}), bf16[8,128,512]{2,1,0:T(8,128)(2,1)S(1)}, u32[]{:S(2)}, u32[]{:S(2)}) async-start(bf16[8,128,512]{2,1,0:T(8,128)(2,1)} %get-tuple-element.34), calls=%async_computation.2 | async-start | bytes 2097152 | tf_op jit(solution)/shard_map/all_to_all | solution.py:425
  111.5 15.3 %collective-permute-start.4 = (bf16[2,512,128]{2,1,0:T(8,128)(2,1)}, bf16[2,512,128]{2,1,0:T(8,128)(2,1)}, u32[]{:S(2)}, u32[]{:S(2)}) collective-permute-start(bf16[2,512,128]{2,1,0:T(8,128)(2,1)} %get-tuple-element.40), channel_id=1, source_target_pairs={{0,384},{128,0},{256,128},{384,256},{1,385},{129,1},{257,129},{385... | collective-permute-start | bytes 786440 | tf_op jit(solution)/shard_map/ppermute | solution.py:367
  113.4 13.3 %collective-permute-start.5 = (bf16[2,512,128]{2,1,0:T(8,128)(2,1)}, bf16[2,512,128]{2,1,0:T(8,128)(2,1)}, u32[]{:S(2)}, u32[]{:S(2)}) collective-permute-start(bf16[2,512,128]{2,1,0:T(8,128)(2,1)} %get-tuple-element.41), channel_id=1, source_target_pairs={{0,256},{128,384},{256,0},{384,128},{1,257},{129,385},{257,1},{385... | collective-permute-start | bytes 786440 | tf_op jit(solution)/shard_map/ppermute | solution.py:367
  118.8 13.1 %collective-permute-start.6 = (bf16[2,512,128]{2,1,0:T(8,128)(2,1)}, bf16[2,512,128]{2,1,0:T(8,128)(2,1)}, u32[]{:S(2)}, u32[]{:S(2)}) collective-permute-start(bf16[2,512,128]{2,1,0:T(8,128)(2,1)} %get-tuple-element.42), channel_id=1, source_target_pairs={{0,128},{128,256},{256,384},{384,0},{1,129},{129,257},{257,385},{3... | collective-permute-start | bytes 786440 | tf_op jit(solution)/shard_map/ppermute | solution.py:367
  125.1 0.7 copy-start.1
  125.8 6.2 %copy-start.2 = (bf16[2,512,128]{2,1,0:T(8,128)(2,1)S(1)}, bf16[2,512,128]{2,1,0:T(8,128)(2,1)}, u32[]{:S(2)}) copy-start(bf16[2,512,128]{2,1,0:T(8,128)(2,1)} %copy-done.1) | copy-start | bytes 786436

commit v7 on v6

--- a/solution.py
+++ b/solution.py
@@ -19,6 +19,8 @@
 PACKED = 4 * ROWS + 8
 QD_ROWS = 2 * BLK + 16
 UNROLL = 4
+CHUNK = 256
+CHUNKS = BLK // CHUNK
 SCALE = 1.0 / math.sqrt(HD)
 SCALE2 = SCALE * math.log2(math.e)
 LOW = -1e30
@@ -49,8 +51,14 @@
     ]
 
 
+def chunk(index):
+    start = index % CHUNKS * CHUNK
+    return index // CHUNKS, start, slice(start, start + CHUNK)
+
+
 def probs_kernel(
-    pairs, meta, own, other, kv0, kv1, kv2, kv3, probs, tops, copies, qd, kv, stats, held, sems, key_sems, out_sems, copy_sems
+    pairs, meta, own, other, kv0, kv1, kv2, kv3, probs, tops, copies,
+    qd, kv, stats, scores, tops_held, held, sems, key_sems, out_sems, copy_sems,
 ):
     fetches = fetch_queries(own, other, qd, sems) + fetch_keys((kv0, kv1, kv2, kv3), kv, key_sems)
     for fetch in fetches:
@@ -71,35 +79,45 @@
         for u in range(UNROLL):
             store(step, u).wait()
 
+    def product(step, index, first):
+        u, start, part = chunk(index)
+        code = pairs[jnp.minimum(step * UNROLL + u, NPAIR - 1)]
+        found = dot(kv[code // NQ, :BLK, :], qd[query_slot(code, meta), part, :], (1, 1))
+        if first and u == 0:
+            key_row = lax.broadcasted_iota(jnp.int32, found.shape, 0)
+            query_row = lax.broadcasted_iota(jnp.int32, found.shape, 1) + start
+            found = jnp.where(key_row <= query_row, found, LOW)
+        tops_held[index % 2][...] = jnp.max(found, axis=0, keepdims=True) * SCALE2
+        scores[index % 2][...] = found
+
+    def normalize(step, index):
+        u, _, part = chunk(index)
+        t = step * UNROLL + u
+        place = query_place(pairs[t], meta)
+        top = tops_held[index % 2][...]
+        values = jnp.exp2(scores[index % 2][...] * SCALE2 - top)
+        total = jnp.sum(values, axis=0, keepdims=True)
+        held[step & 1, u, :, part] = values.astype(jnp.bfloat16)
+        tops[t, :, part] = top
+        top = jnp.where(t < count, top, LOW)
+        total = jnp.where(t < count, total, 0.0)
+        old_top, old_total = stats[place, 0:1, part], stats[place, 1:2, part]
+        new_top = jnp.maximum(old_top, top)
+        stats[place, 0:1, part] = new_top
+        stats[place, 1:2, part] = old_total * jnp.exp2(old_top - new_top) + total * jnp.exp2(top - new_top)
+
     def visit(step, first):
         @pl.when(step >= 2)
         def _():
             wait_stores(step - 2)
 
-        found = []
-        for u in range(UNROLL):
-            code = pairs[step * UNROLL + u]
-            scores = dot(kv[code // NQ, :BLK, :], qd[query_slot(code, meta), :BLK, :], (1, 1))
-            if first and u == 0:
-                key_row = lax.broadcasted_iota(jnp.int32, scores.shape, 0)
-                query_row = lax.broadcasted_iota(jnp.int32, scores.shape, 1)
-                scores = jnp.where(key_row <= query_row, scores, LOW)
-            found.append((scores, jnp.max(scores, axis=0, keepdims=True) * SCALE2))
-        for u, (scores, top) in enumerate(found):
-            t = step * UNROLL + u
-            place = query_place(pairs[t], meta)
-            values = jnp.exp2(scores * SCALE2 - top)
-            total = jnp.sum(values, axis=0, keepdims=True)
-            held[step & 1, u] = values.astype(jnp.bfloat16)
-            store(step, u).start()
-            tops[t] = top
-            top = jnp.where(t < count, top, LOW)
-            total = jnp.where(t < count, total, 0.0)
-            old_top, old_total = stats[place, 0:1, :], stats[place, 1:2, :]
-            new_top = jnp.maximum(old_top, top)
-            stats[place, 0:1, :] = new_top
-            stats[place, 1:2, :] = old_total * jnp.exp2(old_top - new_top) + total * jnp.exp2(top - new_top)
-
+        for index in range(UNROLL * CHUNKS):
+            product(step, index + 1, first)
+            normalize(step, index)
+            if index % CHUNKS == CHUNKS - 1:
+                store(step, index // CHUNKS).start()
+
+    product(0, 0, True)
     visit(0, True)
 
     def body(step, _):
@@ -121,7 +139,7 @@
 
 def dscore_kernel(
     pairs, meta, own, other, kv0, kv1, kv2, kv3, probs_in, stats_in, tops, dscore, dquery,
-    qd, kv, keys_t, total, stats, probs, held, dquery_held, sems, key_sems, in_sems, out_sems, dquery_sems,
+    qd, kv, keys_t, total, stats, dprob, probs, held, dquery_held, sems, key_sems, in_sems, out_sems, dquery_sems,
 ):
     count = meta[0]
     steps = (count + UNROLL - 1) // UNROLL
@@ -157,6 +175,30 @@
     for fetch in fetches:
         fetch.wait()
 
+    def product(step, index):
+        u, start, _ = chunk(index)
+        code = pairs[jnp.minimum(step * UNROLL + u, NPAIR - 1)]
+        grads = qd[query_slot(code, meta), BLK + start : BLK + start + CHUNK, :]
+        dprob[index % 2][...] = dot(kv[code // NQ, BLK:, :], grads, (1, 1))
+
+    def differentiate(step, index):
+        u, start, part = chunk(index)
+        t = step * UNROLL + u
+        pieces = qd[query_slot(pairs[t], meta), 2 * BLK :, :].astype(jnp.float32)
+        row_dot = pieces[0:4] + pieces[4:8] + pieces[8:12]
+        lines = range(start // HD, (start + CHUNK) // HD)
+        row_dot = jnp.concatenate([row_dot[i : i + 1] for i in lines], axis=1)
+        low = probs[t, :, part].astype(jnp.float32) * (dprob[index % 2][...] - row_dot)
+        held[step & 1, u, :, part] = low.astype(jnp.bfloat16)
+
+    def accumulate(step, index):
+        u, _, part = chunk(index)
+        t = step * UNROLL + u
+        code = pairs[t]
+        place = query_place(code, meta)
+        weight = jnp.where(t < count, jnp.exp2(tops[t, :, part] - stats[place, 0:1, part]), 0.0)
+        total[place, :, part] += dot(keys_t[code // NQ], held[step & 1, u, :, part], (1, 0)) * weight
+
     def body(step, _):
         load(step).wait()
 
@@ -164,24 +206,17 @@
         def _():
             wait_stores(step - 2)
 
-        found = []
-        for u in range(UNROLL):
-            t = step * UNROLL + u
-            code = pairs[t]
-            place, key, query = query_place(code, meta), code // NQ, query_slot(code, meta)
-            pieces = qd[query, 2 * BLK :, :].astype(jnp.float32)
-            row_dot = pieces[0:4] + pieces[4:8] + pieces[8:12]
-            row_dot = jnp.concatenate([row_dot[i : i + 1] for i in range(4)], axis=1)
-            weight = jnp.where(t < count, jnp.exp2(tops[t] - stats[place, 0:1, :]), 0.0)
-            dprob = dot(kv[key, BLK:, :], qd[query, BLK : 2 * BLK, :], (1, 1))
-            low = (probs[t].astype(jnp.float32) * (dprob - row_dot)).astype(jnp.bfloat16)
-            held[step & 1, u] = low
-            store(step, u).start()
-            found.append((place, dot(keys_t[key], low, (1, 0)) * weight))
-        for place, part in found:
-            total[place] += part
+        for index in range(UNROLL * CHUNKS):
+            product(step, index + 1)
+            if index > 0:
+                accumulate(step, index - 1)
+            differentiate(step, index)
+            if index % CHUNKS == CHUNKS - 1:
+                store(step, index // CHUNKS).start()
+        accumulate(step, UNROLL * CHUNKS - 1)
         return 0
 
+    product(0, 0)
     lax.fori_loop(0, steps, body, 0)
     sent = [pltpu.make_async_copy(dquery_held.at[i], dquery.at[i], dquery_sems.at[i]) for i in range(NQ)]
     for i in range(NQ):
@@ -407,7 +442,11 @@
         [anywhere] * 6,
         [anywhere, vmem, anywhere],
         [square, line, pltpu.HBM((NQ, NQ, 2, BLK), f32)],
-        [qd_scratch, kv_scratch, pltpu.VMEM((NQ, 2, BLK), f32), pltpu.VMEM((2, UNROLL, BLK, BLK), bf16), dma((2,)), dma((NK,)), dma((2, UNROLL)), dma((NQ,))],
+        [
+            qd_scratch, kv_scratch, pltpu.VMEM((NQ, 2, BLK), f32), [pltpu.VMEM((BLK, CHUNK), f32)] * 2,
+            [pltpu.VMEM((1, CHUNK), f32)] * 2, pltpu.VMEM((2, UNROLL, BLK, BLK), bf16),
+            dma((2,)), dma((NK,)), dma((2, UNROLL)), dma((NQ,)),
+        ],
     )
     stats_all = lax.all_to_all(stats, ("y", "c"), 0, 0, tiled=True)
     tiles, two_steps = pltpu.VMEM((NPAIR, BLK, BLK), bf16), pltpu.VMEM((2, UNROLL, BLK, BLK), bf16)
@@ -419,7 +458,7 @@
         [square, pltpu.HBM((NQ, HD, BLK), bf16)],
         [
             qd_scratch, kv_scratch, pltpu.VMEM((NK, HD, BLK), bf16), pltpu.VMEM((NQ, HD, BLK), f32),
-            pltpu.VMEM((NQ, 2, BLK), f32), tiles, two_steps, pltpu.VMEM((NQ, HD, BLK), bf16), dma((3,)), dma((NK,)), step_dma, dma((2, UNROLL)), dma((NQ,)),
+            pltpu.VMEM((NQ, 2, BLK), f32), [pltpu.VMEM((BLK, CHUNK), f32)] * 2, tiles, two_steps, pltpu.VMEM((NQ, HD, BLK), bf16), dma((3,)), dma((NK,)), step_dma, dma((2, UNROLL)), dma((NQ,)),
         ],
     )
     dquery = lax.all_to_all(dquery, ("y", "c"), 0, 0, tiled=True)

time: 172 us -> 167 us (0.971)
  the two profiles are of different devices: /device:TPU:24 before, /device:TPU:8 now
where the time goes in v7:
time: 167 us; the launch traced here: 166 us
  starting transfers between devices  58.5 us (35%)
  waiting for transfers between devices  38.4 us (23%)
  blocking collectives  33.3 us (20%)
  Pallas kernels  25.1 us (15%)
  local copies, waits for them, and re-layouts  6.14 us (4%)
  other arithmetic  3.4 us (2%)
    all_to_all x1, blocking collectives, on_device(): grads = lax.all_to_all(grads, 'h', 0, 0, tiled=True)  33.3 us
    ppermute x7, starting transfers between devices, shifted(): lax.ppermute(array, axis, [(i, (i + by) % size) for i in range(size)])  27 us
    all_to_all x1, waiting for transfers between devices, on_device(): packed = lax.all_to_all(packed, 'h', 0, 0, tiled=True)  23.2 us
    pallas_call x4, Pallas kernels, over_pairs(): pl.pallas_call(kernel, grid_spec=pltpu.PrefetchScalarGridSpec(num_scalar_...  20.6 us
    all_to_all x1, starting transfers between devices, on_device(): packed = lax.all_to_all(packed, 'h', 0, 0, tiled=True)  15.2 us
    ppermute x7, waiting for transfers between devices, shifted(): lax.ppermute(array, axis, [(i, (i + by) % size) for i in range(size)])  15 us
    all_to_all x1, starting transfers between devices, on_device(): stats_all = lax.all_to_all(stats, ('y', 'c'), 0, 0, tiled=True)  5.87 us
    all_to_all x1, starting transfers between devices, on_device(): dquery = lax.all_to_all(dquery, ('y', 'c'), 0, 0, tiled=True)  5.58 us
  transfers between devices with their start and end apart: 11, of which 8 were waited for; matrix products, arithmetic and copies ran while one was open for 4% of the time, Pallas kernels for 10%

profile of v7, /device:TPU:8, one launch (start us, length us, event | category | flops | bytes accessed | tf_op | source)
XLA Modules:
  0.0 166.4 jit_solution(17304500753076238307)
XLA Ops:
  0.6 0.0 copy-start
  0.6 0.0 copy-start.4
  0.7 2.3 %shard_map.103 = bf16[16,136,128]{2,1,0:T(8,128)(2,1)} custom-call(bf16[32,2048]{1,0:T(8,128)(2,1)} %query_in.1, bf16[32,2048]{1,0:T(8,128)(2,1)} %key_in.1, bf16[32,2048]{1,0:T(8,128)(2,1)} %value_in.1, bf16[32,2048]{1,0:T(8,128)(2,1)} %output_in.1, bf16[32,2048]{1,0:T(8,128)(2,1)} %grad_in.1), custom_call_target="tpu_custom_call" | custom-call | tf_op jit(solution)/shard_map/pallas_call | solution.py:413
  2.9 0.0 copy-start.3
  2.9 15.2 %all-to-all-start = ((bf16[16,136,128]{2,1,0:T(8,128)(2,1)}), bf16[16,136,128]{2,1,0:T(8,128)(2,1)S(1)}, u32[]{:S(2)}, u32[]{:S(2)}) async-start(bf16[16,136,128]{2,1,0:T(8,128)(2,1)} %shard_map.103), calls=%async_computation | async-start | bytes 1114112 | tf_op jit(solution)/shard_map/all_to_all | solution.py:421
  18.2 0.0 copy-done.4
  18.2 0.1 copy.17
  18.3 0.0 copy-done
  18.3 0.6 gather_fusion
  18.9 0.6 gather_fusion.1
  19.5 0.0 copy-done.3
  19.5 0.6 gather_fusion.3
  20.2 0.6 gather_fusion.2
  20.8 0.1 iota_compare_fusion.1
  20.9 0.2 and_reduce_fusion
  21.1 0.1 and.87
  21.2 0.7 convert_reduce_fusion.1
  22.6 0.6 fusion.8
  23.2 1.4 pad_add_fusion.meta
  24.6 0.1 convert_reduce_fusion
  24.8 0.2 select_reduce_fusion.pairs
  24.9 23.2 %all-to-all-done = bf16[16,136,128]{2,1,0:T(8,128)(2,1)S(1)} async-done(((bf16[16,136,128]{2,1,0:T(8,128)(2,1)}), bf16[16,136,128]{2,1,0:T(8,128)(2,1)S(1)}, u32[]{:S(2)}, u32[]{:S(2)}) %all-to-all-start) | async-done | bytes 557088 | tf_op jit(solution)/shard_map/all_to_all | solution.py:421
  48.2 0.1 reshape.227
  48.3 0.1 concatenate.6
  48.4 1.1 broadcast_in_dim.12
  49.5 4.9 %all-to-all-start.1 = ((bf16[4,1040,128]{2,1,0:T(8,128)(2,1)}), bf16[4,1040,128]{2,1,0:T(8,128)(2,1)S(1)}, u32[]{:S(2)}, u32[]{:S(2)}) async-start(bf16[4,1040,128]{2,1,0:T(8,128)(2,1)} %broadcast_in_dim.12), calls=%async_computation.1 | async-start | bytes 2129920 | tf_op jit(solution)/shard_map/all_to_all | solution.py:433
  54.4 3.4 %collective-permute-start = (bf16[1024,128]{1,0:T(8,128)(2,1)S(1)}, bf16[1024,128]{1,0:T(8,128)(2,1)S(1)}, u32[]{:S(2)}, u32[]{:S(2)}) collective-permute-start(bf16[1024,128]{1,0:T(8,128)(2,1)S(1)} %pad_maximum_fusion.kv0), channel_id=1, source_target_pairs={{0,128},{128,256},{256,384},{384,0},{1,129},{129,257},{257,385},{3... | collective-permute-start | bytes 786440 | tf_op jit(solution)/shard_map/ppermute | solution.py:402
  57.8 4.6 %collective-permute-start.1 = (bf16[1024,128]{1,0:T(8,128)(2,1)S(1)}, bf16[1024,128]{1,0:T(8,128)(2,1)S(1)}, u32[]{:S(2)}, u32[]{:S(2)}) collective-permute-start(bf16[1024,128]{1,0:T(8,128)(2,1)S(1)} %pad_maximum_fusion.kv0), channel_id=1, source_target_pairs={{0,256},{128,384},{256,0},{384,128},{1,257},{129,385},{257,1},{385... | collective-permute-start | bytes 786440 | tf_op jit(solution)/shard_map/ppermute | solution.py:402
  62.5 3.3 %collective-permute-start.2 = (bf16[1024,128]{1,0:T(8,128)(2,1)S(1)}, bf16[1024,128]{1,0:T(8,128)(2,1)S(1)}, u32[]{:S(2)}, u32[]{:S(2)}) collective-permute-start(bf16[1024,128]{1,0:T(8,128)(2,1)S(1)} %pad_maximum_fusion.kv0), channel_id=1, source_target_pairs={{0,384},{128,0},{256,128},{384,256},{1,385},{129,1},{257,129},{385... | collective-permute-start | bytes 786440 | tf_op jit(solution)/shard_map/ppermute | solution.py:402
  65.8 0.0 collective-permute-done.kv1
  65.8 1.9 %collective-permute-done.1.kv2 = bf16[1024,128]{1,0:T(8,128)(2,1)S(1)} collective-permute-done((bf16[1024,128]{1,0:T(8,128)(2,1)S(1)}, bf16[1024,128]{1,0:T(8,128)(2,1)S(1)}, u32[]{:S(2)}, u32[]{:S(2)}) %collective-permute-start.1) | collective-permute-done | bytes 262176 | tf_op jit(solution)/shard_map/ppermute | solution.py:402
  67.7 3.0 %collective-permute-done.2.kv3 = bf16[1024,128]{1,0:T(8,128)(2,1)S(1)} collective-permute-done((bf16[1024,128]{1,0:T(8,128)(2,1)S(1)}, bf16[1024,128]{1,0:T(8,128)(2,1)S(1)}, u32[]{:S(2)}, u32[]{:S(2)}) %collective-permute-start.2) | collective-permute-done | bytes 262176 | tf_op jit(solution)/shard_map/ppermute | solution.py:402
  70.7 0.0 all-to-all-done.1.own
  70.7 1.9 %collective-permute-start.3 = (bf16[4,1040,128]{2,1,0:T(8,128)(2,1)S(1)}, bf16[4,1040,128]{2,1,0:T(8,128)(2,1)S(1)}, u32[]{:S(2)}, u32[]{:S(2)}) collective-permute-start(bf16[4,1040,128]{2,1,0:T(8,128)(2,1)S(1)} %all-to-all-done.1.own), channel_id=1, source_target_pairs={{0,16},{16,0},{1,17},{17,1},{2,18},{18,2},{3,19},{19,3},{4,20},{20... | collective-permute-start | bytes 3194888 | tf_op jit(solution)/shard_map/ppermute | solution.py:402
  72.7 2.6 %collective-permute-done.3.other = bf16[4,1040,128]{2,1,0:T(8,128)(2,1)S(1)} collective-permute-done((bf16[4,1040,128]{2,1,0:T(8,128)(2,1)S(1)}, bf16[4,1040,128]{2,1,0:T(8,128)(2,1)S(1)}, u32[]{:S(2)}, u32[]{:S(2)}) %collective-permute-start.3) | collective-permute-done | bytes 1064992 | tf_op jit(solution)/shard_map/ppermute | solution.py:402
  75.3 4.6 %shard_map.104 = (bf16[32,512,512]{2,1,0:T(8,128)(2,1)}, f32[32,1,512]{2,1,0:T(1,128)S(1)}, f32[8,8,2,512]{3,2,1,0:T(2,128)}) custom-call(s32[32]{0:T(128)S(1)} %select_reduce_fusion.pairs, s32[4]{0:T(128)S(1)} %pad_add_fusion.meta, bf16[4,1040,128]{2,1,0:T(8,128)(2,1)S(1)} %all-to-all-done.1.own, bf16[4,1040,128]{2,1,0:T(8,128)(2,1)S(1)} %collective-permute-done.3.other, ...), custom_call_target="tpu_custom_call" | custom-call | tf_op jit(solution)/shard_map/pallas_call | solution.py:370
  79.9 5.9 %all-to-all-start.3 = ((f32[8,8,2,512]{3,2,1,0:T(2,128)}), f32[8,8,2,512]{3,2,1,0:T(2,128)S(1)}, u32[]{:S(2)}, u32[]{:S(2)}) async-start(f32[8,8,2,512]{3,2,1,0:T(2,128)} %get-tuple-element.32.stats_in), calls=%async_computation.3 | async-start | bytes 524288 | tf_op jit(solution)/shard_map/all_to_all | solution.py:451
  85.8 5.9 %shard_map.105 = (bf16[32,512,512]{2,1,0:T(8,128)(2,1)}, bf16[8,128,512]{2,1,0:T(8,128)(2,1)}) custom-call(s32[32]{0:T(128)S(1)} %select_reduce_fusion.pairs, s32[4]{0:T(128)S(1)} %pad_add_fusion.meta, bf16[4,1040,128]{2,1,0:T(8,128)(2,1)S(1)} %all-to-all-done.1.own, bf16[4,1040,128]{2,1,0:T(8,128)(2,1)S(1)} %collective-permute-done.3.other, ...), custom_call_target="tpu_custom_call" | custom-call | tf_op jit(solution)/shard_map/pallas_call | solution.py:370
  91.7 0.1 all-to-all-done.3.stats_in.stats_all
  91.9 5.6 %all-to-all-start.2 = ((bf16[8,128,512]{2,1,0:T(8,128)(2,1)}), bf16[8,128,512]{2,1,0:T(8,128)(2,1)S(1)}, u32[]{:S(2)}, u32[]{:S(2)}) async-start(bf16[8,128,512]{2,1,0:T(8,128)(2,1)} %get-tuple-element.34), calls=%async_computation.2 | async-start | bytes 2097152 | tf_op jit(solution)/shard_map/all_to_all | solution.py:464
  97.4 5.5 %shard_map.107 = (bf16[2,512,128]{2,1,0:T(8,128)(2,1)}, bf16[2,512,128]{2,1,0:T(8,128)(2,1)}, bf16[2,512,128]{2,1,0:T(8,128)(2,1)}) custom-call(s32[32]{0:T(128)S(1)} %select_reduce_fusion.pairs, s32[4]{0:T(128)S(1)} %pad_add_fusion.meta, bf16[4,1040,128]{2,1,0:T(8,128)(2,1)S(1)} %all-to-all-done.1.own, ...), custom_call_target="tpu_custom_call" | custom-call | tf_op jit(solution)/shard_map/pallas_call | solution.py:370
  102.9 9.0 %collective-permute-start.4 = (bf16[2,512,128]{2,1,0:T(8,128)(2,1)}, bf16[2,512,128]{2,1,0:T(8,128)(2,1)}, u32[]{:S(2)}, u32[]{:S(2)}) collective-permute-start(bf16[2,512,128]{2,1,0:T(8,128)(2,1)} %get-tuple-element.40), channel_id=1, source_target_pairs={{0,384},{128,0},{256,128},{384,256},{1,385},{129,1},{257,129},{385... | collective-permute-start | bytes 786440 | tf_op jit(solution)/shard_map/ppermute | solution.py:402
  111.9 1.9 %collective-permute-start.5 = (bf16[2,512,128]{2,1,0:T(8,128)(2,1)}, bf16[2,512,128]{2,1,0:T(8,128)(2,1)}, u32[]{:S(2)}, u32[]{:S(2)}) collective-permute-start(bf16[2,512,128]{2,1,0:T(8,128)(2,1)} %get-tuple-element.41), channel_id=1, source_target_pairs={{0,256},{128,384},{256,0},{384,128},{1,257},{129,385},{257,1},{385... | collective-permute-start | bytes 786440 | tf_op jit(solution)/shard_map/ppermute | solution.py:402
  113.8 2.8 %collective-permute-start.6 = (bf16[2,512,128]{2,1,0:T(8,128)(2,1)}, bf16[2,512,128]{2,1,0:T(8,128)(2,1)}, u32[]{:S(2)}, u32[]{:S(2)}) collective-permute-start(bf16[2,512,128]{2,1,0:T(8,128)(2,1)} %get-tuple-element.42), channel_id=1, source_target_pairs={{0,128},{128,256},{256,384},{384,0},{1,129},{129,257},{257,385},{3... | collective-permute-start | bytes 786440 | tf_op jit(solution)/shard_map/ppermute | solution.py:402
  116.6 4.6 %shard_map.108.kept = bf16[2,512,128]{2,1,0:T(8,128)(2,1)S(1)} custom-call(s32[32]{0:T(128)S(1)} %select_reduce_fusion.pairs, s32[4]{0:T(128)S(1)} %pad_add_fusion.meta, bf16[4,1040,128]{2,1,0:T(8,128)(2,1)S(1)} %all-to-all-done.1.own, bf16[4,1040,128]{2,1,0:T(8,128)(2,1)S(1)} %collective-permute-done.3.other, ...), custom_call_target="tpu_custom_call" | custom-call | tf_op jit(solution)/shard_map/pallas_call | solution.py:370
  121.2 0.0 copy-start.1
  121.2 0.7 copy-done.1
  121.9 0.0 all-to-all-done.2.dquery_in
  121.9 0.0 copy-start.2
  121.9 1.0 shard_map.106.query_grad
  122.9 1.1 collective-permute-done.4.first
  124.0 0.6 collective-permute-done.5.second
  124.6 5.8 %collective-permute-done.6.third = bf16[2,512,128]{2,1,0:T(8,128)(2,1)} collective-permute-done((bf16[2,512,128]{2,1,0:T(8,128)(2,1)}, bf16[2,512,128]{2,1,0:T(8,128)(2,1)}, u32[]{:S(2)}, u32[]{:S(2)}) %collective-permute-start.6) | collective-permute-done | bytes 262176 | tf_op jit(solution)/shard_map/ppermute | solution.py:402
  130.4 0.0 copy-done.2
  130.4 1.3 shard_map.109
  131.7 33.3 %all_to_all.25 = bf16[16,96,128]{2,1,0:T(8,128)(2,1)S(1)} all-to-all(bf16[16,96,128]{2,1,0:T(8,128)(2,1)S(1)} %shard_map.109), channel_id=1, replica_groups=mesh['x'=4,'y'=4,'c'=2,'h'=16] {'h'}, dimensions={0} | all-to-all | bytes 786432 | tf_op jit(solution)/shard_map/all_to_all | solution.py:506
  165.1 0.7 copy.28
  165.7 0.7 copy_bitcast_fusion
  (13 shorter events, 0.2 us)
Async XLA Ops:
  0.6 17.6 %copy-start = (s32[32]{0:T(128)S(1)}, s32[32]{0:T(128)}, u32[]{:S(2)}) copy-start(s32[32]{0:T(128)} %param.15) | copy-start | bytes 388
  0.6 17.5 %copy-start.4 = (s32[32,16]{0,1:T(8,128)S(1)}, s32[32,16]{0,1:T(8,128)}, u32[]{:S(2)}) copy-start(s32[32,16]{0,1:T(8,128)} %param.13) | copy-start | bytes 6148
  2.9 16.6 %copy-start.3 = (s32[32]{0:T(128)S(1)}, s32[32]{0:T(128)}, u32[]{:S(2)}) copy-start(s32[32]{0:T(128)} %param.14) | copy-start | bytes 388
  2.9 45.2 %all-to-all-start = ((bf16[16,136,128]{2,1,0:T(8,128)(2,1)}), bf16[16,136,128]{2,1,0:T(8,128)(2,1)S(1)}, u32[]{:S(2)}, u32[]{:S(2)}) async-start(bf16[16,136,128]{2,1,0:T(8,128)(2,1)} %shard_map.103), calls=%async_computation | async-start | bytes 1114112 | tf_op jit(solution)/shard_map/all_to_all | solution.py:421
  49.5 21.3 %all-to-all-start.1 = ((bf16[4,1040,128]{2,1,0:T(8,128)(2,1)}), bf16[4,1040,128]{2,1,0:T(8,128)(2,1)S(1)}, u32[]{:S(2)}, u32[]{:S(2)}) async-start(bf16[4,1040,128]{2,1,0:T(8,128)(2,1)} %broadcast_in_dim.12), calls=%async_computation.1 | async-start | bytes 2129920 | tf_op jit(solution)/shard_map/all_to_all | solution.py:433
  54.4 11.4 %collective-permute-start = (bf16[1024,128]{1,0:T(8,128)(2,1)S(1)}, bf16[1024,128]{1,0:T(8,128)(2,1)S(1)}, u32[]{:S(2)}, u32[]{:S(2)}) collective-permute-start(bf16[1024,128]{1,0:T(8,128)(2,1)S(1)} %pad_maximum_fusion.kv0), channel_id=1, source_target_pairs={{0,128},{128,256},{256,384},{384,0},{1,129},{129,257},{257,385},{3... | collective-permute-start | bytes 786440 | tf_op jit(solution)/shard_map/ppermute | solution.py:402
  57.8 9.9 %collective-permute-start.1 = (bf16[1024,128]{1,0:T(8,128)(2,1)S(1)}, bf16[1024,128]{1,0:T(8,128)(2,1)S(1)}, u32[]{:S(2)}, u32[]{:S(2)}) collective-permute-start(bf16[1024,128]{1,0:T(8,128)(2,1)S(1)} %pad_maximum_fusion.kv0), channel_id=1, source_target_pairs={{0,256},{128,384},{256,0},{384,128},{1,257},{129,385},{257,1},{385... | collective-permute-start | bytes 786440 | tf_op jit(solution)/shard_map/ppermute | solution.py:402
  62.5 8.3 %collective-permute-start.2 = (bf16[1024,128]{1,0:T(8,128)(2,1)S(1)}, bf16[1024,128]{1,0:T(8,128)(2,1)S(1)}, u32[]{:S(2)}, u32[]{:S(2)}) collective-permute-start(bf16[1024,128]{1,0:T(8,128)(2,1)S(1)} %pad_maximum_fusion.kv0), channel_id=1, source_target_pairs={{0,384},{128,0},{256,128},{384,256},{1,385},{129,1},{257,129},{385... | collective-permute-start | bytes 786440 | tf_op jit(solution)/shard_map/ppermute | solution.py:402
  70.7 4.6 %collective-permute-start.3 = (bf16[4,1040,128]{2,1,0:T(8,128)(2,1)S(1)}, bf16[4,1040,128]{2,1,0:T(8,128)(2,1)S(1)}, u32[]{:S(2)}, u32[]{:S(2)}) collective-permute-start(bf16[4,1040,128]{2,1,0:T(8,128)(2,1)S(1)} %all-to-all-done.1.own), channel_id=1, source_target_pairs={{0,16},{16,0},{1,17},{17,1},{2,18},{18,2},{3,19},{19,3},{4,20},{20... | collective-permute-start | bytes 3194888 | tf_op jit(solution)/shard_map/ppermute | solution.py:402
  79.9 12.0 %all-to-all-start.3 = ((f32[8,8,2,512]{3,2,1,0:T(2,128)}), f32[8,8,2,512]{3,2,1,0:T(2,128)S(1)}, u32[]{:S(2)}, u32[]{:S(2)}) async-start(f32[8,8,2,512]{3,2,1,0:T(2,128)} %get-tuple-element.32.stats_in), calls=%async_computation.3 | async-start | bytes 524288 | tf_op jit(solution)/shard_map/all_to_all | solution.py:451
  91.9 30.1 %all-to-all-start.2 = ((bf16[8,128,512]{2,1,0:T(8,128)(2,1)}), bf16[8,128,512]{2,1,0:T(8,128)(2,1)S(1)}, u32[]{:S(2)}, u32[]{:S(2)}) async-start(bf16[8,128,512]{2,1,0:T(8,128)(2,1)} %get-tuple-element.34), calls=%async_computation.2 | async-start | bytes 2097152 | tf_op jit(solution)/shard_map/all_to_all | solution.py:464
  102.9 21.0 %collective-permute-start.4 = (bf16[2,512,128]{2,1,0:T(8,128)(2,1)}, bf16[2,512,128]{2,1,0:T(8,128)(2,1)}, u32[]{:S(2)}, u32[]{:S(2)}) collective-permute-start(bf16[2,512,128]{2,1,0:T(8,128)(2,1)} %get-tuple-element.40), channel_id=1, source_target_pairs={{0,384},{128,0},{256,128},{384,256},{1,385},{129,1},{257,129},{385... | collective-permute-start | bytes 786440 | tf_op jit(solution)/shard_map/ppermute | solution.py:402
  111.9 12.7 %collective-permute-start.5 = (bf16[2,512,128]{2,1,0:T(8,128)(2,1)}, bf16[2,512,128]{2,1,0:T(8,128)(2,1)}, u32[]{:S(2)}, u32[]{:S(2)}) collective-permute-start(bf16[2,512,128]{2,1,0:T(8,128)(2,1)} %get-tuple-element.41), channel_id=1, source_target_pairs={{0,256},{128,384},{256,0},{384,128},{1,257},{129,385},{257,1},{385... | collective-permute-start | bytes 786440 | tf_op jit(solution)/shard_map/ppermute | solution.py:402
  113.8 16.6 %collective-permute-start.6 = (bf16[2,512,128]{2,1,0:T(8,128)(2,1)}, bf16[2,512,128]{2,1,0:T(8,128)(2,1)}, u32[]{:S(2)}, u32[]{:S(2)}) collective-permute-start(bf16[2,512,128]{2,1,0:T(8,128)(2,1)} %get-tuple-element.42), channel_id=1, source_target_pairs={{0,128},{128,256},{256,384},{384,0},{1,129},{129,257},{257,385},{3... | collective-permute-start | bytes 786440 | tf_op jit(solution)/shard_map/ppermute | solution.py:402
  121.2 0.7 copy-start.1
  121.9 8.5 %copy-start.2 = (bf16[2,512,128]{2,1,0:T(8,128)(2,1)S(1)}, bf16[2,512,128]{2,1,0:T(8,128)(2,1)}, u32[]{:S(2)}) copy-start(bf16[2,512,128]{2,1,0:T(8,128)(2,1)} %copy-done.1) | copy-start | bytes 786436

commit v8 on v7

--- a/solution.py
+++ b/solution.py
@@ -16,7 +16,7 @@
 NQ = NY * NC
 NK = NX
 NPAIR = NQ * NK
-PACKED = 4 * ROWS + 8
+PACKED = 4 * ROWS + 16
 QD_ROWS = 2 * BLK + 16
 UNROLL = 4
 CHUNK = 256
@@ -313,8 +313,8 @@
     row_dot = jnp.transpose(row_dot)[:HEADS]
     high = row_dot.astype(jnp.bfloat16).astype(jnp.float32)
     middle = (row_dot - high).astype(jnp.bfloat16).astype(jnp.float32)
-    row = lax.broadcasted_iota(jnp.int32, (HEADS, 8, HD), 1)
-    pieces = jnp.zeros((HEADS, 8, HD), jnp.float32)
+    row = lax.broadcasted_iota(jnp.int32, (HEADS, 16, HD), 1)
+    pieces = jnp.zeros((HEADS, 16, HD), jnp.float32)
     for i, piece in enumerate((high, middle, row_dot - high - middle)):
         pieces = jnp.where(row == i, piece[:, None, :], pieces)
     out[:, 4 * ROWS :, :] = pieces.astype(jnp.bfloat16)
@@ -356,6 +356,12 @@
             parts[2, i].astype(jnp.float32) + parts[3, i].astype(jnp.float32)
         )
         out[:, (i + 1) * ROWS : (i + 2) * ROWS, :] = grad.astype(jnp.bfloat16).reshape(HEADS, ROWS, HD)
+
+
+def unpack_kernel(grads, *outs):
+    for h in range(HEADS):
+        for i, out in enumerate(outs):
+            out[:, h * HD : (h + 1) * HD] = grads[h, i * ROWS : (i + 1) * ROWS, :]
 
 
 def in_hbm(array):
@@ -505,11 +511,13 @@
     )(query_grad, kept, arrived[1], arrived[2], arrived[3])
     grads = lax.all_to_all(grads, "h", 0, 0, tiled=True)
 
-    def tokens(i):
-        part = grads[:, i * ROWS : (i + 1) * ROWS, :]
-        return jnp.transpose(part, (1, 0, 2)).reshape(ROWS, HEADS * HD)
-
-    return tokens(0), tokens(1), tokens(2)
+    return pl.pallas_call(
+        unpack_kernel,
+        in_specs=[vmem],
+        out_specs=[vmem] * 3,
+        out_shape=[shape((ROWS, HEADS * HD), bf16)] * 3,
+        compiler_params=params(8),
+    )(grads)
 
 
 def solution(mesh):

time: 167 us -> 167 us (level)
  the two profiles are of different devices: /device:TPU:8 before, /device:TPU:24 now
where the time goes in v8:
time: 167 us; the launch traced here: 165 us
  starting transfers between devices  57 us (34%)
  waiting for transfers between devices  37 us (22%)
  blocking collectives  33.9 us (20%)
  Pallas kernels  27.4 us (16%)
  local copies, waits for them, and re-layouts  4.72 us (3%)
  other arithmetic  3.4 us (2%)
    all_to_all x1, blocking collectives, on_device(): grads = lax.all_to_all(grads, 'h', 0, 0, tiled=True)  33.9 us
    ppermute x7, starting transfers between devices, shifted(): lax.ppermute(array, axis, [(i, (i + by) % size) for i in range(size)])  24.7 us
    all_to_all x1, waiting for transfers between devices, on_device(): packed = lax.all_to_all(packed, 'h', 0, 0, tiled=True)  24 us
    pallas_call x4, Pallas kernels, over_pairs(): pl.pallas_call(kernel, grid_spec=pltpu.PrefetchScalarGridSpec(num_scalar_...  22 us
    all_to_all x1, starting transfers between devices, on_device(): packed = lax.all_to_all(packed, 'h', 0, 0, tiled=True)  15.2 us
    ppermute x7, waiting for transfers between devices, shifted(): lax.ppermute(array, axis, [(i, (i + by) % size) for i in range(size)])  12.9 us
    all_to_all x1, starting transfers between devices, on_device(): dquery = lax.all_to_all(dquery, ('y', 'c'), 0, 0, tiled=True)  6.77 us
    all_to_all x1, starting transfers between devices, on_device(): stats_all = lax.all_to_all(stats, ('y', 'c'), 0, 0, tiled=True)  5.6 us
  transfers between devices with their start and end apart: 11, of which 6 were waited for; matrix products, arithmetic and copies ran while one was open for 4% of the time, Pallas kernels for 11%

profile of v8, /device:TPU:24, one launch (start us, length us, event | category | flops | bytes accessed | tf_op | source)
XLA Modules:
  0.0 164.9 jit_solution(14773042139572608707)
XLA Ops:
  0.6 0.0 copy-start
  0.6 0.0 copy-start.4
  0.7 2.3 %shard_map.103 = bf16[16,144,128]{2,1,0:T(8,128)(2,1)} custom-call(bf16[32,2048]{1,0:T(8,128)(2,1)} %query_in.1, bf16[32,2048]{1,0:T(8,128)(2,1)} %key_in.1, bf16[32,2048]{1,0:T(8,128)(2,1)} %value_in.1, bf16[32,2048]{1,0:T(8,128)(2,1)} %output_in.1, bf16[32,2048]{1,0:T(8,128)(2,1)} %grad_in.1), custom_call_target="tpu_custom_call" | custom-call | tf_op jit(solution)/shard_map/pallas_call | solution.py:419
  2.9 0.0 copy-start.3
  2.9 15.2 %all-to-all-start = ((bf16[16,144,128]{2,1,0:T(8,128)(2,1)}), bf16[16,144,128]{2,1,0:T(8,128)(2,1)S(1)}, u32[]{:S(2)}, u32[]{:S(2)}) async-start(bf16[16,144,128]{2,1,0:T(8,128)(2,1)} %shard_map.103), calls=%async_computation | async-start | bytes 1179648 | tf_op jit(solution)/shard_map/all_to_all | solution.py:427
  18.2 0.0 copy-done.4
  18.2 0.1 copy.14
  18.3 0.0 copy-done
  18.3 0.6 gather_fusion
  19.0 0.6 gather_fusion.1
  19.5 0.0 copy-done.3
  19.5 0.6 gather_fusion.3
  20.2 0.6 gather_fusion.2
  20.8 0.1 iota_compare_fusion.1
  20.9 0.2 and_reduce_fusion
  21.1 0.1 and.87
  21.2 0.7 convert_reduce_fusion.1
  22.6 0.6 fusion.8
  23.3 1.4 pad_add_fusion.meta
  24.6 0.1 convert_reduce_fusion
  24.8 0.2 select_reduce_fusion.pairs
  24.9 24.0 %all-to-all-done = bf16[16,144,128]{2,1,0:T(8,128)(2,1)S(1)} async-done(((bf16[16,144,128]{2,1,0:T(8,128)(2,1)}), bf16[16,144,128]{2,1,0:T(8,128)(2,1)S(1)}, u32[]{:S(2)}, u32[]{:S(2)}) %all-to-all-start) | async-done | bytes 589856 | tf_op jit(solution)/shard_map/all_to_all | solution.py:427
  49.1 0.1 reshape.218
  49.1 0.1 concatenate.6
  49.2 1.1 broadcast_in_dim.12
  50.4 4.7 %all-to-all-start.1 = ((bf16[4,1040,128]{2,1,0:T(8,128)(2,1)}), bf16[4,1040,128]{2,1,0:T(8,128)(2,1)S(1)}, u32[]{:S(2)}, u32[]{:S(2)}) async-start(bf16[4,1040,128]{2,1,0:T(8,128)(2,1)} %broadcast_in_dim.12), calls=%async_computation.1 | async-start | bytes 2129920 | tf_op jit(solution)/shard_map/all_to_all | solution.py:439
  55.1 3.4 %collective-permute-start = (bf16[1024,128]{1,0:T(8,128)(2,1)S(1)}, bf16[1024,128]{1,0:T(8,128)(2,1)S(1)}, u32[]{:S(2)}, u32[]{:S(2)}) collective-permute-start(bf16[1024,128]{1,0:T(8,128)(2,1)S(1)} %pad_maximum_fusion.kv0), channel_id=1, source_target_pairs={{0,128},{128,256},{256,384},{384,0},{1,129},{129,257},{257,385},{3... | collective-permute-start | bytes 786440 | tf_op jit(solution)/shard_map/ppermute | solution.py:408
  58.5 4.6 %collective-permute-start.1 = (bf16[1024,128]{1,0:T(8,128)(2,1)S(1)}, bf16[1024,128]{1,0:T(8,128)(2,1)S(1)}, u32[]{:S(2)}, u32[]{:S(2)}) collective-permute-start(bf16[1024,128]{1,0:T(8,128)(2,1)S(1)} %pad_maximum_fusion.kv0), channel_id=1, source_target_pairs={{0,256},{128,384},{256,0},{384,128},{1,257},{129,385},{257,1},{385... | collective-permute-start | bytes 786440 | tf_op jit(solution)/shard_map/ppermute | solution.py:408
  63.1 3.3 %collective-permute-start.2 = (bf16[1024,128]{1,0:T(8,128)(2,1)S(1)}, bf16[1024,128]{1,0:T(8,128)(2,1)S(1)}, u32[]{:S(2)}, u32[]{:S(2)}) collective-permute-start(bf16[1024,128]{1,0:T(8,128)(2,1)S(1)} %pad_maximum_fusion.kv0), channel_id=1, source_target_pairs={{0,384},{128,0},{256,128},{384,256},{1,385},{129,1},{257,129},{385... | collective-permute-start | bytes 786440 | tf_op jit(solution)/shard_map/ppermute | solution.py:408
  66.5 0.0 collective-permute-done.kv1
  66.5 1.9 %collective-permute-done.1.kv2 = bf16[1024,128]{1,0:T(8,128)(2,1)S(1)} collective-permute-done((bf16[1024,128]{1,0:T(8,128)(2,1)S(1)}, bf16[1024,128]{1,0:T(8,128)(2,1)S(1)}, u32[]{:S(2)}, u32[]{:S(2)}) %collective-permute-start.1) | collective-permute-done | bytes 262176 | tf_op jit(solution)/shard_map/ppermute | solution.py:408
  68.3 3.0 %collective-permute-done.2.kv3 = bf16[1024,128]{1,0:T(8,128)(2,1)S(1)} collective-permute-done((bf16[1024,128]{1,0:T(8,128)(2,1)S(1)}, bf16[1024,128]{1,0:T(8,128)(2,1)S(1)}, u32[]{:S(2)}, u32[]{:S(2)}) %collective-permute-start.2) | collective-permute-done | bytes 262176 | tf_op jit(solution)/shard_map/ppermute | solution.py:408
  71.4 0.0 all-to-all-done.1.own
  71.4 1.9 %collective-permute-start.3 = (bf16[4,1040,128]{2,1,0:T(8,128)(2,1)S(1)}, bf16[4,1040,128]{2,1,0:T(8,128)(2,1)S(1)}, u32[]{:S(2)}, u32[]{:S(2)}) collective-permute-start(bf16[4,1040,128]{2,1,0:T(8,128)(2,1)S(1)} %all-to-all-done.1.own), channel_id=1, source_target_pairs={{0,16},{16,0},{1,17},{17,1},{2,18},{18,2},{3,19},{19,3},{4,20},{20... | collective-permute-start | bytes 3194888 | tf_op jit(solution)/shard_map/ppermute | solution.py:408
  73.3 2.6 %collective-permute-done.3.other = bf16[4,1040,128]{2,1,0:T(8,128)(2,1)S(1)} collective-permute-done((bf16[4,1040,128]{2,1,0:T(8,128)(2,1)S(1)}, bf16[4,1040,128]{2,1,0:T(8,128)(2,1)S(1)}, u32[]{:S(2)}, u32[]{:S(2)}) %collective-permute-start.3) | collective-permute-done | bytes 1064992 | tf_op jit(solution)/shard_map/ppermute | solution.py:408
  76.0 4.6 %shard_map.104 = (bf16[32,512,512]{2,1,0:T(8,128)(2,1)}, f32[32,1,512]{2,1,0:T(1,128)S(1)}, f32[8,8,2,512]{3,2,1,0:T(2,128)}) custom-call(s32[32]{0:T(128)S(1)} %select_reduce_fusion.pairs, s32[4]{0:T(128)S(1)} %pad_add_fusion.meta, bf16[4,1040,128]{2,1,0:T(8,128)(2,1)S(1)} %all-to-all-done.1.own, bf16[4,1040,128]{2,1,0:T(8,128)(2,1)S(1)} %collective-permute-done.3.other, ...), custom_call_target="tpu_custom_call" | custom-call | tf_op jit(solution)/shard_map/pallas_call | solution.py:376
  80.5 5.6 %all-to-all-start.3 = ((f32[8,8,2,512]{3,2,1,0:T(2,128)}), f32[8,8,2,512]{3,2,1,0:T(2,128)S(1)}, u32[]{:S(2)}, u32[]{:S(2)}) async-start(f32[8,8,2,512]{3,2,1,0:T(2,128)} %get-tuple-element.32.stats_in), calls=%async_computation.3 | async-start | bytes 524288 | tf_op jit(solution)/shard_map/all_to_all | solution.py:457
  86.1 5.9 %shard_map.105 = (bf16[32,512,512]{2,1,0:T(8,128)(2,1)}, bf16[8,128,512]{2,1,0:T(8,128)(2,1)}) custom-call(s32[32]{0:T(128)S(1)} %select_reduce_fusion.pairs, s32[4]{0:T(128)S(1)} %pad_add_fusion.meta, bf16[4,1040,128]{2,1,0:T(8,128)(2,1)S(1)} %all-to-all-done.1.own, bf16[4,1040,128]{2,1,0:T(8,128)(2,1)S(1)} %collective-permute-done.3.other, ...), custom_call_target="tpu_custom_call" | custom-call | tf_op jit(solution)/shard_map/pallas_call | solution.py:376
  92.1 0.0 all-to-all-done.3.stats_in.stats_all
  92.1 6.8 %all-to-all-start.2 = ((bf16[8,128,512]{2,1,0:T(8,128)(2,1)}), bf16[8,128,512]{2,1,0:T(8,128)(2,1)S(1)}, u32[]{:S(2)}, u32[]{:S(2)}) async-start(bf16[8,128,512]{2,1,0:T(8,128)(2,1)} %get-tuple-element.34), calls=%async_computation.2 | async-start | bytes 2097152 | tf_op jit(solution)/shard_map/all_to_all | solution.py:470
  98.9 5.8 %shard_map.107 = (bf16[2,512,128]{2,1,0:T(8,128)(2,1)}, bf16[2,512,128]{2,1,0:T(8,128)(2,1)}, bf16[2,512,128]{2,1,0:T(8,128)(2,1)}) custom-call(s32[32]{0:T(128)S(1)} %select_reduce_fusion.pairs, s32[4]{0:T(128)S(1)} %pad_add_fusion.meta, bf16[4,1040,128]{2,1,0:T(8,128)(2,1)S(1)} %all-to-all-done.1.own, ...), custom_call_target="tpu_custom_call" | custom-call | tf_op jit(solution)/shard_map/pallas_call | solution.py:376
  104.7 6.7 %collective-permute-start.4 = (bf16[2,512,128]{2,1,0:T(8,128)(2,1)}, bf16[2,512,128]{2,1,0:T(8,128)(2,1)}, u32[]{:S(2)}, u32[]{:S(2)}) collective-permute-start(bf16[2,512,128]{2,1,0:T(8,128)(2,1)} %get-tuple-element.40), channel_id=1, source_target_pairs={{0,384},{128,0},{256,128},{384,256},{1,385},{129,1},{257,129},{385... | collective-permute-start | bytes 786440 | tf_op jit(solution)/shard_map/ppermute | solution.py:408
  111.4 1.9 %collective-permute-start.5 = (bf16[2,512,128]{2,1,0:T(8,128)(2,1)}, bf16[2,512,128]{2,1,0:T(8,128)(2,1)}, u32[]{:S(2)}, u32[]{:S(2)}) collective-permute-start(bf16[2,512,128]{2,1,0:T(8,128)(2,1)} %get-tuple-element.41), channel_id=1, source_target_pairs={{0,256},{128,384},{256,0},{384,128},{1,257},{129,385},{257,1},{385... | collective-permute-start | bytes 786440 | tf_op jit(solution)/shard_map/ppermute | solution.py:408
  113.4 2.8 %collective-permute-start.6 = (bf16[2,512,128]{2,1,0:T(8,128)(2,1)}, bf16[2,512,128]{2,1,0:T(8,128)(2,1)}, u32[]{:S(2)}, u32[]{:S(2)}) collective-permute-start(bf16[2,512,128]{2,1,0:T(8,128)(2,1)} %get-tuple-element.42), channel_id=1, source_target_pairs={{0,128},{128,256},{256,384},{384,0},{1,129},{129,257},{257,385},{3... | collective-permute-start | bytes 786440 | tf_op jit(solution)/shard_map/ppermute | solution.py:408
  116.1 5.7 %shard_map.108.kept = bf16[2,512,128]{2,1,0:T(8,128)(2,1)S(1)} custom-call(s32[32]{0:T(128)S(1)} %select_reduce_fusion.pairs, s32[4]{0:T(128)S(1)} %pad_add_fusion.meta, bf16[4,1040,128]{2,1,0:T(8,128)(2,1)S(1)} %all-to-all-done.1.own, bf16[4,1040,128]{2,1,0:T(8,128)(2,1)S(1)} %collective-permute-done.3.other, ...), custom_call_target="tpu_custom_call" | custom-call | tf_op jit(solution)/shard_map/pallas_call | solution.py:376
  121.8 0.0 copy-start.1
  121.8 0.7 copy-done.1
  122.5 0.0 all-to-all-done.2.dquery_in
  122.5 0.0 copy-start.2
  122.5 1.0 shard_map.106.query_grad
  123.5 0.0 collective-permute-done.4.first
  123.5 0.9 collective-permute-done.5.second
  124.4 4.5 %collective-permute-done.6.third = bf16[2,512,128]{2,1,0:T(8,128)(2,1)} collective-permute-done((bf16[2,512,128]{2,1,0:T(8,128)(2,1)}, bf16[2,512,128]{2,1,0:T(8,128)(2,1)}, u32[]{:S(2)}, u32[]{:S(2)}) %collective-permute-start.6) | collective-permute-done | bytes 262176 | tf_op jit(solution)/shard_map/ppermute | solution.py:408
  128.8 0.0 copy-done.2
  128.8 1.3 shard_map.109
  130.2 33.9 %all_to_all.25.grads = bf16[16,96,128]{2,1,0:T(8,128)(2,1)S(1)} all-to-all(bf16[16,96,128]{2,1,0:T(8,128)(2,1)S(1)} %shard_map.109), channel_id=1, replica_groups=mesh['x'=4,'y'=4,'c'=2,'h'=16] {'h'}, dimensions={0} | all-to-all | bytes 786432 | tf_op jit(solution)/shard_map/all_to_all | solution.py:512
  164.1 0.8 shard_map.110
  (12 shorter events, 0.1 us)
Async XLA Ops:
  0.6 17.7 %copy-start = (s32[32]{0:T(128)S(1)}, s32[32]{0:T(128)}, u32[]{:S(2)}) copy-start(s32[32]{0:T(128)} %param.15) | copy-start | bytes 388
  0.6 17.5 %copy-start.4 = (s32[32,16]{0,1:T(8,128)S(1)}, s32[32,16]{0,1:T(8,128)}, u32[]{:S(2)}) copy-start(s32[32,16]{0,1:T(8,128)} %param.13) | copy-start | bytes 6148
  2.9 16.6 %copy-start.3 = (s32[32]{0:T(128)S(1)}, s32[32]{0:T(128)}, u32[]{:S(2)}) copy-start(s32[32]{0:T(128)} %param.14) | copy-start | bytes 388
  2.9 46.0 %all-to-all-start = ((bf16[16,144,128]{2,1,0:T(8,128)(2,1)}), bf16[16,144,128]{2,1,0:T(8,128)(2,1)S(1)}, u32[]{:S(2)}, u32[]{:S(2)}) async-start(bf16[16,144,128]{2,1,0:T(8,128)(2,1)} %shard_map.103), calls=%async_computation | async-start | bytes 1179648 | tf_op jit(solution)/shard_map/all_to_all | solution.py:427
  50.4 21.0 %all-to-all-start.1 = ((bf16[4,1040,128]{2,1,0:T(8,128)(2,1)}), bf16[4,1040,128]{2,1,0:T(8,128)(2,1)S(1)}, u32[]{:S(2)}, u32[]{:S(2)}) async-start(bf16[4,1040,128]{2,1,0:T(8,128)(2,1)} %broadcast_in_dim.12), calls=%async_computation.1 | async-start | bytes 2129920 | tf_op jit(solution)/shard_map/all_to_all | solution.py:439
  55.1 11.4 %collective-permute-start = (bf16[1024,128]{1,0:T(8,128)(2,1)S(1)}, bf16[1024,128]{1,0:T(8,128)(2,1)S(1)}, u32[]{:S(2)}, u32[]{:S(2)}) collective-permute-start(bf16[1024,128]{1,0:T(8,128)(2,1)S(1)} %pad_maximum_fusion.kv0), channel_id=1, source_target_pairs={{0,128},{128,256},{256,384},{384,0},{1,129},{129,257},{257,385},{3... | collective-permute-start | bytes 786440 | tf_op jit(solution)/shard_map/ppermute | solution.py:408
  58.5 9.9 %collective-permute-start.1 = (bf16[1024,128]{1,0:T(8,128)(2,1)S(1)}, bf16[1024,128]{1,0:T(8,128)(2,1)S(1)}, u32[]{:S(2)}, u32[]{:S(2)}) collective-permute-start(bf16[1024,128]{1,0:T(8,128)(2,1)S(1)} %pad_maximum_fusion.kv0), channel_id=1, source_target_pairs={{0,256},{128,384},{256,0},{384,128},{1,257},{129,385},{257,1},{385... | collective-permute-start | bytes 786440 | tf_op jit(solution)/shard_map/ppermute | solution.py:408
  63.1 8.3 %collective-permute-start.2 = (bf16[1024,128]{1,0:T(8,128)(2,1)S(1)}, bf16[1024,128]{1,0:T(8,128)(2,1)S(1)}, u32[]{:S(2)}, u32[]{:S(2)}) collective-permute-start(bf16[1024,128]{1,0:T(8,128)(2,1)S(1)} %pad_maximum_fusion.kv0), channel_id=1, source_target_pairs={{0,384},{128,0},{256,128},{384,256},{1,385},{129,1},{257,129},{385... | collective-permute-start | bytes 786440 | tf_op jit(solution)/shard_map/ppermute | solution.py:408
  71.4 4.6 %collective-permute-start.3 = (bf16[4,1040,128]{2,1,0:T(8,128)(2,1)S(1)}, bf16[4,1040,128]{2,1,0:T(8,128)(2,1)S(1)}, u32[]{:S(2)}, u32[]{:S(2)}) collective-permute-start(bf16[4,1040,128]{2,1,0:T(8,128)(2,1)S(1)} %all-to-all-done.1.own), channel_id=1, source_target_pairs={{0,16},{16,0},{1,17},{17,1},{2,18},{18,2},{3,19},{19,3},{4,20},{20... | collective-permute-start | bytes 3194888 | tf_op jit(solution)/shard_map/ppermute | solution.py:408
  80.5 11.6 %all-to-all-start.3 = ((f32[8,8,2,512]{3,2,1,0:T(2,128)}), f32[8,8,2,512]{3,2,1,0:T(2,128)S(1)}, u32[]{:S(2)}, u32[]{:S(2)}) async-start(f32[8,8,2,512]{3,2,1,0:T(2,128)} %get-tuple-element.32.stats_in), calls=%async_computation.3 | async-start | bytes 524288 | tf_op jit(solution)/shard_map/all_to_all | solution.py:457
  92.1 30.4 %all-to-all-start.2 = ((bf16[8,128,512]{2,1,0:T(8,128)(2,1)}), bf16[8,128,512]{2,1,0:T(8,128)(2,1)S(1)}, u32[]{:S(2)}, u32[]{:S(2)}) async-start(bf16[8,128,512]{2,1,0:T(8,128)(2,1)} %get-tuple-element.34), calls=%async_computation.2 | async-start | bytes 2097152 | tf_op jit(solution)/shard_map/all_to_all | solution.py:470
  104.7 18.8 %collective-permute-start.4 = (bf16[2,512,128]{2,1,0:T(8,128)(2,1)}, bf16[2,512,128]{2,1,0:T(8,128)(2,1)}, u32[]{:S(2)}, u32[]{:S(2)}) collective-permute-start(bf16[2,512,128]{2,1,0:T(8,128)(2,1)} %get-tuple-element.40), channel_id=1, source_target_pairs={{0,384},{128,0},{256,128},{384,256},{1,385},{129,1},{257,129},{385... | collective-permute-start | bytes 786440 | tf_op jit(solution)/shard_map/ppermute | solution.py:408
  111.4 12.9 %collective-permute-start.5 = (bf16[2,512,128]{2,1,0:T(8,128)(2,1)}, bf16[2,512,128]{2,1,0:T(8,128)(2,1)}, u32[]{:S(2)}, u32[]{:S(2)}) collective-permute-start(bf16[2,512,128]{2,1,0:T(8,128)(2,1)} %get-tuple-element.41), channel_id=1, source_target_pairs={{0,256},{128,384},{256,0},{384,128},{1,257},{129,385},{257,1},{385... | collective-permute-start | bytes 786440 | tf_op jit(solution)/shard_map/ppermute | solution.py:408
  113.4 15.5 %collective-permute-start.6 = (bf16[2,512,128]{2,1,0:T(8,128)(2,1)}, bf16[2,512,128]{2,1,0:T(8,128)(2,1)}, u32[]{:S(2)}, u32[]{:S(2)}) collective-permute-start(bf16[2,512,128]{2,1,0:T(8,128)(2,1)} %get-tuple-element.42), channel_id=1, source_target_pairs={{0,128},{128,256},{256,384},{384,0},{1,129},{129,257},{257,385},{3... | collective-permute-start | bytes 786440 | tf_op jit(solution)/shard_map/ppermute | solution.py:408
  121.8 0.7 copy-start.1
  122.5 6.3 %copy-start.2 = (bf16[2,512,128]{2,1,0:T(8,128)(2,1)S(1)}, bf16[2,512,128]{2,1,0:T(8,128)(2,1)}, u32[]{:S(2)}) copy-start(bf16[2,512,128]{2,1,0:T(8,128)(2,1)} %copy-done.1) | copy-start | bytes 786436

commit v9 on v8

--- a/solution.py
+++ b/solution.py
@@ -44,11 +44,10 @@
     return [pltpu.make_async_copy(block, kv.at[i], sems.at[i]) for i, block in enumerate(blocks)]
 
 
-def fetch_queries(own, other, qd, sems):
-    return [
-        pltpu.make_async_copy(own, qd.at[pl.ds(0, NY)], sems.at[0]),
-        pltpu.make_async_copy(other, qd.at[pl.ds(NY, NY)], sems.at[1]),
-    ]
+def query_rows(own, other, code, meta, rows):
+    slot = query_slot(code, meta)
+    here = slot & (NY - 1)
+    return jnp.where(slot < NY, own[here, rows, :], other[here, rows, :])
 
 
 def chunk(index):
@@ -58,9 +57,9 @@
 
 def probs_kernel(
     pairs, meta, own, other, kv0, kv1, kv2, kv3, probs, tops, copies,
-    qd, kv, stats, scores, tops_held, held, sems, key_sems, out_sems, copy_sems,
+    kv, stats, scores, tops_held, held, key_sems, out_sems, copy_sems,
 ):
-    fetches = fetch_queries(own, other, qd, sems) + fetch_keys((kv0, kv1, kv2, kv3), kv, key_sems)
+    fetches = fetch_keys((kv0, kv1, kv2, kv3), kv, key_sems)
     for fetch in fetches:
         fetch.start()
     stats[:, 0, :] = jnp.full((NQ, BLK), LOW, jnp.float32)
@@ -82,7 +81,7 @@
     def product(step, index, first):
         u, start, part = chunk(index)
         code = pairs[jnp.minimum(step * UNROLL + u, NPAIR - 1)]
-        found = dot(kv[code // NQ, :BLK, :], qd[query_slot(code, meta), part, :], (1, 1))
+        found = dot(kv[code // NQ, :BLK, :], query_rows(own, other, code, meta, part), (1, 1))
         if first and u == 0:
             key_row = lax.broadcasted_iota(jnp.int32, found.shape, 0)
             query_row = lax.broadcasted_iota(jnp.int32, found.shape, 1) + start
@@ -139,7 +138,7 @@
 
 def dscore_kernel(
     pairs, meta, own, other, kv0, kv1, kv2, kv3, probs_in, stats_in, tops, dscore, dquery,
-    qd, kv, keys_t, total, stats, dprob, probs, held, dquery_held, sems, key_sems, in_sems, out_sems, dquery_sems,
+    kv, keys_t, total, stats, dprob, probs, held, dquery_held, sems, key_sems, in_sems, out_sems, dquery_sems,
 ):
     count = meta[0]
     steps = (count + UNROLL - 1) // UNROLL
@@ -158,8 +157,7 @@
             store(step, u).wait()
 
     key_fetches = fetch_keys((kv0, kv1, kv2, kv3), kv, key_sems)
-    fetches = fetch_queries(own, other, qd, sems)
-    fetches.append(pltpu.make_async_copy(stats_in.at[0], stats, sems.at[2]))
+    fetches = [pltpu.make_async_copy(stats_in.at[0], stats, sems.at[0])]
     for fetch in key_fetches + fetches:
         fetch.start()
 
@@ -178,13 +176,13 @@
     def product(step, index):
         u, start, _ = chunk(index)
         code = pairs[jnp.minimum(step * UNROLL + u, NPAIR - 1)]
-        grads = qd[query_slot(code, meta), BLK + start : BLK + start + CHUNK, :]
+        grads = query_rows(own, other, code, meta, slice(BLK + start, BLK + start + CHUNK))
         dprob[index % 2][...] = dot(kv[code // NQ, BLK:, :], grads, (1, 1))
 
     def differentiate(step, index):
         u, start, part = chunk(index)
         t = step * UNROLL + u
-        pieces = qd[query_slot(pairs[t], meta), 2 * BLK :, :].astype(jnp.float32)
+        pieces = query_rows(own, other, pairs[t], meta, slice(2 * BLK, QD_ROWS)).astype(jnp.float32)
         row_dot = pieces[0:4] + pieces[4:8] + pieces[8:12]
         lines = range(start // HD, (start + CHUNK) // HD)
         row_dot = jnp.concatenate([row_dot[i : i + 1] for i in lines], axis=1)
@@ -238,7 +236,7 @@
 
 
 def key_kernel(late, pairs, meta, own, other, probs_in, dscore_in, tops, stats_all, *rest):
-    *outs, qd, norms, total, probs, dscore, sems, probs_sems, dscore_sems = rest
+    *outs, norms, total, probs, dscore, probs_sems, dscore_sems = rest
     begin, end = (0, meta[3]) if late else (meta[3], meta[0])
     steps = (end - begin + UNROLL - 1) // UNROLL
 
@@ -256,15 +254,9 @@
             copy.start()
         return 0
 
-    lax.fori_loop(0, jnp.minimum(steps, 1), start, 0)
-    fetches = fetch_queries(own, other, qd, sems)
-    for fetch in fetches:
-        fetch.start()
-    lax.fori_loop(1, steps, start, 0)
+    lax.fori_loop(0, steps, start, 0)
     total[...] = jnp.zeros_like(total)
     norms[:, 0, :] = log_norms(stats_all[...])
-    for fetch in fetches:
-        fetch.wait()
 
     def body(step, _):
         for copy in loads(step):
@@ -274,11 +266,11 @@
             held = step * UNROLL + u
             t = jnp.minimum(begin + held, end - 1)
             code = pairs[t]
-            place, key, query = query_place(code, meta), code // NQ, query_slot(code, meta)
+            place, key = query_place(code, meta), code // NQ
             weight = jnp.where(begin + held < end, jnp.exp2(tops[t] - norms[place]), 0.0)
             weight = jnp.transpose(jnp.broadcast_to(weight, (HD, BLK)))
-            queries = (qd[query, :BLK, :].astype(jnp.float32) * (weight * SCALE)).astype(jnp.bfloat16)
-            grads = (qd[query, BLK : 2 * BLK, :].astype(jnp.float32) * weight).astype(jnp.bfloat16)
+            queries = (query_rows(own, other, code, meta, slice(0, BLK)).astype(jnp.float32) * (weight * SCALE)).astype(jnp.bfloat16)
+            grads = (query_rows(own, other, code, meta, slice(BLK, 2 * BLK)).astype(jnp.float32) * weight).astype(jnp.bfloat16)
             slot = 0 if late else key - 1
             found.append((slot, dot(dscore[held], queries, (1, 0)), dot(probs[held], grads, (1, 0))))
         for slot, key_part, value_part in found:
@@ -442,16 +434,16 @@
     queries = (own, shifted(own, "c", 1, NC))
 
     square, line = pltpu.HBM((NPAIR, BLK, BLK), bf16), shape((NPAIR, 1, BLK), f32)
-    qd_scratch, kv_scratch = pltpu.VMEM((NQ, QD_ROWS, HD), bf16), pltpu.VMEM((NK, 2 * BLK, HD), bf16)
+    kv_scratch = pltpu.VMEM((NK, 2 * BLK, HD), bf16)
     probs, tops, stats = over_pairs(
         probs_kernel, 28, pairs, meta, (*queries, *keys),
-        [anywhere] * 6,
+        [vmem] * 2 + [anywhere] * 4,
         [anywhere, vmem, anywhere],
         [square, line, pltpu.HBM((NQ, NQ, 2, BLK), f32)],
         [
-            qd_scratch, kv_scratch, pltpu.VMEM((NQ, 2, BLK), f32), [pltpu.VMEM((BLK, CHUNK), f32)] * 2,
+            kv_scratch, pltpu.VMEM((NQ, 2, BLK), f32), [pltpu.VMEM((BLK, CHUNK), f32)] * 2,
             [pltpu.VMEM((1, CHUNK), f32)] * 2, pltpu.VMEM((2, UNROLL, BLK, BLK), bf16),
-            dma((2,)), dma((NK,)), dma((2, UNROLL)), dma((NQ,)),
+            dma((NK,)), dma((2, UNROLL)), dma((NQ,)),
         ],
     )
     stats_all = lax.all_to_all(stats, ("y", "c"), 0, 0, tiled=True)
@@ -459,12 +451,12 @@
     step_dma = dma((NPAIR // UNROLL,))
     dscore, dquery = over_pairs(
         dscore_kernel, 44, pairs, meta, (*queries, *keys, in_hbm(probs), in_hbm(stats), tops),
-        [anywhere] * 8 + [vmem],
+        [vmem] * 2 + [anywhere] * 6 + [vmem],
         [anywhere, anywhere],
         [square, pltpu.HBM((NQ, HD, BLK), bf16)],
         [
-            qd_scratch, kv_scratch, pltpu.VMEM((NK, HD, BLK), bf16), pltpu.VMEM((NQ, HD, BLK), f32),
-            pltpu.VMEM((NQ, 2, BLK), f32), [pltpu.VMEM((BLK, CHUNK), f32)] * 2, tiles, two_steps, pltpu.VMEM((NQ, HD, BLK), bf16), dma((3,)), dma((NK,)), step_dma, dma((2, UNROLL)), dma((NQ,)),
+            kv_scratch, pltpu.VMEM((NK, HD, BLK), bf16), pltpu.VMEM((NQ, HD, BLK), f32),
+            pltpu.VMEM((NQ, 2, BLK), f32), [pltpu.VMEM((BLK, CHUNK), f32)] * 2, tiles, two_steps, pltpu.VMEM((NQ, HD, BLK), bf16), dma((1,)), dma((NK,)), step_dma, dma((2, UNROLL)), dma((NQ,)),
         ],
     )
     dquery = lax.all_to_all(dquery, ("y", "c"), 0, 0, tiled=True)
@@ -477,12 +469,12 @@
         return over_pairs(
             functools.partial(key_kernel, late), 50, pairs, meta,
             (*queries, in_hbm(probs), in_hbm(dscore), tops, stats_all),
-            [anywhere] * 4 + [vmem] * 2,
+            [vmem] * 2 + [anywhere] * 2 + [vmem] * 2,
             [vmem] * slots,
             [shape((2, BLK, HD), bf16)] * slots,
             [
-                qd_scratch, pltpu.VMEM((NQ, 1, BLK), f32), pltpu.VMEM((slots, 2, BLK, HD), f32), held, held,
-                dma((2,)), dma((most,)), dma((most,)),
+                pltpu.VMEM((NQ, 1, BLK), f32), pltpu.VMEM((slots, 2, BLK, HD), f32), held, held,
+                dma((most,)), dma((most,)),
             ],
         )
 

time: 167 us -> 168 us (level)
  starting transfers between devices: 57 us -> 54 us
  waiting for transfers between devices: 37 us -> 39.4 us
  Pallas kernels: 27.4 us -> 29.5 us
    ppermute x7, waiting for transfers between devices: 12.9 us -> 15.4 us  [shifted(): lax.ppermute(array, axis, [(i, (i + by) % size) for i in range(size)])]
    all_to_all x1, starting transfers between devices: 6.77 us -> 4.53 us  [on_device(): dquery = lax.all_to_all(dquery, ('y', 'c'), 0, 0, tiled=True)]
    pallas_call x4, Pallas kernels: 22 us -> 24.2 us  [over_pairs(): pl.pallas_call(kernel, grid_spec=pltpu.PrefetchScalarGridSpec(num_scalar_...]
  transfers between devices with their start and end apart: 11 -> 11, of which waited for: 6 -> 7; matrix products, arithmetic and copies ran while one was open for 4% -> 4% of each run, Pallas kernels for 11% -> 12%
where the time goes in v9:
time: 168 us; the launch traced here: 167 us
  starting transfers between devices  54 us (32%)
  waiting for transfers between devices  39.4 us (23%)
  blocking collectives  34 us (20%)
  Pallas kernels  29.5 us (18%)
  local copies, waits for them, and re-layouts  4.72 us (3%)
  other arithmetic  3.4 us (2%)
    all_to_all x1, blocking collectives, on_device(): grads = lax.all_to_all(grads, 'h', 0, 0, tiled=True)  34 us
    ppermute x7, starting transfers between devices, shifted(): lax.ppermute(array, axis, [(i, (i + by) % size) for i in range(size)])  25 us
    pallas_call x4, Pallas kernels, over_pairs(): pl.pallas_call(kernel, grid_spec=pltpu.PrefetchScalarGridSpec(num_scalar_...  24.2 us
    all_to_all x1, waiting for transfers between devices, on_device(): packed = lax.all_to_all(packed, 'h', 0, 0, tiled=True)  24 us
    ppermute x7, waiting for transfers between devices, shifted(): lax.ppermute(array, axis, [(i, (i + by) % size) for i in range(size)])  15.4 us
    all_to_all x1, starting transfers between devices, on_device(): packed = lax.all_to_all(packed, 'h', 0, 0, tiled=True)  15.2 us
    all_to_all x1, starting transfers between devices, on_device(): lax.all_to_all(jnp.broadcast_to(qd[None], (NY, *qd.shape)), 'y', 0, 0, ti...  4.68 us
    all_to_all x1, starting transfers between devices, on_device(): stats_all = lax.all_to_all(stats, ('y', 'c'), 0, 0, tiled=True)  4.56 us
  transfers between devices with their start and end apart: 11, of which 7 were waited for; matrix products, arithmetic and copies ran while one was open for 4% of the time, Pallas kernels for 12%

profile of v9, /device:TPU:24, one launch (start us, length us, event | category | flops | bytes accessed | tf_op | source)
XLA Modules:
  0.0 166.6 jit_solution(10775140951019850735)
XLA Ops:
  0.6 0.0 copy-start
  0.6 0.0 copy-start.4
  0.7 2.3 %shard_map.103 = bf16[16,144,128]{2,1,0:T(8,128)(2,1)} custom-call(bf16[32,2048]{1,0:T(8,128)(2,1)} %query_in.1, bf16[32,2048]{1,0:T(8,128)(2,1)} %key_in.1, bf16[32,2048]{1,0:T(8,128)(2,1)} %value_in.1, bf16[32,2048]{1,0:T(8,128)(2,1)} %output_in.1, bf16[32,2048]{1,0:T(8,128)(2,1)} %grad_in.1), custom_call_target="tpu_custom_call" | custom-call | tf_op jit(solution)/shard_map/pallas_call | solution.py:411
  2.9 0.0 copy-start.3
  2.9 15.2 %all-to-all-start = ((bf16[16,144,128]{2,1,0:T(8,128)(2,1)}), bf16[16,144,128]{2,1,0:T(8,128)(2,1)S(1)}, u32[]{:S(2)}, u32[]{:S(2)}) async-start(bf16[16,144,128]{2,1,0:T(8,128)(2,1)} %shard_map.103), calls=%async_computation | async-start | bytes 1179648 | tf_op jit(solution)/shard_map/all_to_all | solution.py:419
  18.2 0.0 copy-done.4
  18.2 0.1 copy.14
  18.3 0.0 copy-done
  18.3 0.6 gather_fusion
  19.0 0.6 gather_fusion.1
  19.5 0.0 copy-done.3
  19.5 0.6 gather_fusion.3
  20.2 0.6 gather_fusion.2
  20.8 0.1 iota_compare_fusion.1
  20.9 0.2 and_reduce_fusion
  21.1 0.1 and.87
  21.2 0.7 convert_reduce_fusion.1
  22.6 0.6 fusion.8
  23.3 1.4 pad_add_fusion.meta
  24.6 0.1 convert_reduce_fusion
  24.8 0.2 select_reduce_fusion.pairs
  24.9 24.0 %all-to-all-done = bf16[16,144,128]{2,1,0:T(8,128)(2,1)S(1)} async-done(((bf16[16,144,128]{2,1,0:T(8,128)(2,1)}), bf16[16,144,128]{2,1,0:T(8,128)(2,1)S(1)}, u32[]{:S(2)}, u32[]{:S(2)}) %all-to-all-start) | async-done | bytes 589856 | tf_op jit(solution)/shard_map/all_to_all | solution.py:419
  49.1 0.1 reshape.218
  49.1 0.1 concatenate.6
  49.2 1.1 broadcast_in_dim.12
  50.4 4.7 %all-to-all-start.1 = ((bf16[4,1040,128]{2,1,0:T(8,128)(2,1)}), bf16[4,1040,128]{2,1,0:T(8,128)(2,1)S(1)}, u32[]{:S(2)}, u32[]{:S(2)}) async-start(bf16[4,1040,128]{2,1,0:T(8,128)(2,1)} %broadcast_in_dim.12), calls=%async_computation.1 | async-start | bytes 2129920 | tf_op jit(solution)/shard_map/all_to_all | solution.py:431
  55.1 3.4 %collective-permute-start = (bf16[1024,128]{1,0:T(8,128)(2,1)S(1)}, bf16[1024,128]{1,0:T(8,128)(2,1)S(1)}, u32[]{:S(2)}, u32[]{:S(2)}) collective-permute-start(bf16[1024,128]{1,0:T(8,128)(2,1)S(1)} %pad_maximum_fusion.kv0), channel_id=1, source_target_pairs={{0,128},{128,256},{256,384},{384,0},{1,129},{129,257},{257,385},{3... | collective-permute-start | bytes 786440 | tf_op jit(solution)/shard_map/ppermute | solution.py:400
  58.5 4.6 %collective-permute-start.1 = (bf16[1024,128]{1,0:T(8,128)(2,1)S(1)}, bf16[1024,128]{1,0:T(8,128)(2,1)S(1)}, u32[]{:S(2)}, u32[]{:S(2)}) collective-permute-start(bf16[1024,128]{1,0:T(8,128)(2,1)S(1)} %pad_maximum_fusion.kv0), channel_id=1, source_target_pairs={{0,256},{128,384},{256,0},{384,128},{1,257},{129,385},{257,1},{385... | collective-permute-start | bytes 786440 | tf_op jit(solution)/shard_map/ppermute | solution.py:400
  63.1 3.3 %collective-permute-start.2 = (bf16[1024,128]{1,0:T(8,128)(2,1)S(1)}, bf16[1024,128]{1,0:T(8,128)(2,1)S(1)}, u32[]{:S(2)}, u32[]{:S(2)}) collective-permute-start(bf16[1024,128]{1,0:T(8,128)(2,1)S(1)} %pad_maximum_fusion.kv0), channel_id=1, source_target_pairs={{0,384},{128,0},{256,128},{384,256},{1,385},{129,1},{257,129},{385... | collective-permute-start | bytes 786440 | tf_op jit(solution)/shard_map/ppermute | solution.py:400
  66.5 0.0 collective-permute-done.kv1
  66.5 1.9 %collective-permute-done.1.kv2 = bf16[1024,128]{1,0:T(8,128)(2,1)S(1)} collective-permute-done((bf16[1024,128]{1,0:T(8,128)(2,1)S(1)}, bf16[1024,128]{1,0:T(8,128)(2,1)S(1)}, u32[]{:S(2)}, u32[]{:S(2)}) %collective-permute-start.1) | collective-permute-done | bytes 262176 | tf_op jit(solution)/shard_map/ppermute | solution.py:400
  68.3 3.0 %collective-permute-done.2.kv3 = bf16[1024,128]{1,0:T(8,128)(2,1)S(1)} collective-permute-done((bf16[1024,128]{1,0:T(8,128)(2,1)S(1)}, bf16[1024,128]{1,0:T(8,128)(2,1)S(1)}, u32[]{:S(2)}, u32[]{:S(2)}) %collective-permute-start.2) | collective-permute-done | bytes 262176 | tf_op jit(solution)/shard_map/ppermute | solution.py:400
  71.4 0.0 all-to-all-done.1.own
  71.4 1.9 %collective-permute-start.3 = (bf16[4,1040,128]{2,1,0:T(8,128)(2,1)S(1)}, bf16[4,1040,128]{2,1,0:T(8,128)(2,1)S(1)}, u32[]{:S(2)}, u32[]{:S(2)}) collective-permute-start(bf16[4,1040,128]{2,1,0:T(8,128)(2,1)S(1)} %all-to-all-done.1.own), channel_id=1, source_target_pairs={{0,16},{16,0},{1,17},{17,1},{2,18},{18,2},{3,19},{19,3},{4,20},{20... | collective-permute-start | bytes 3194888 | tf_op jit(solution)/shard_map/ppermute | solution.py:400
  73.3 2.6 %collective-permute-done.3.other = bf16[4,1040,128]{2,1,0:T(8,128)(2,1)S(1)} collective-permute-done((bf16[4,1040,128]{2,1,0:T(8,128)(2,1)S(1)}, bf16[4,1040,128]{2,1,0:T(8,128)(2,1)S(1)}, u32[]{:S(2)}, u32[]{:S(2)}) %collective-permute-start.3) | collective-permute-done | bytes 1064992 | tf_op jit(solution)/shard_map/ppermute | solution.py:400
  76.0 5.9 %shard_map.104 = (bf16[32,512,512]{2,1,0:T(8,128)(2,1)}, f32[32,1,512]{2,1,0:T(1,128)S(1)}, f32[8,8,2,512]{3,2,1,0:T(2,128)}) custom-call(s32[32]{0:T(128)S(1)} %select_reduce_fusion.pairs, s32[4]{0:T(128)S(1)} %pad_add_fusion.meta, bf16[4,1040,128]{2,1,0:T(8,128)(2,1)S(1)} %all-to-all-done.1.own, bf16[4,1040,128]{2,1,0:T(8,128)(2,1)S(1)} %collective-permute-done.3.other, ...), custom_call_target="tpu_custom_call" | custom-call | tf_op jit(solution)/shard_map/pallas_call | solution.py:368
  81.8 4.6 %all-to-all-start.3 = ((f32[8,8,2,512]{3,2,1,0:T(2,128)}), f32[8,8,2,512]{3,2,1,0:T(2,128)S(1)}, u32[]{:S(2)}, u32[]{:S(2)}) async-start(f32[8,8,2,512]{3,2,1,0:T(2,128)} %get-tuple-element.32.stats_in), calls=%async_computation.3 | async-start | bytes 524288 | tf_op jit(solution)/shard_map/all_to_all | solution.py:449
  86.4 7.1 %shard_map.105 = (bf16[32,512,512]{2,1,0:T(8,128)(2,1)}, bf16[8,128,512]{2,1,0:T(8,128)(2,1)}) custom-call(s32[32]{0:T(128)S(1)} %select_reduce_fusion.pairs, s32[4]{0:T(128)S(1)} %pad_add_fusion.meta, bf16[4,1040,128]{2,1,0:T(8,128)(2,1)S(1)} %all-to-all-done.1.own, bf16[4,1040,128]{2,1,0:T(8,128)(2,1)S(1)} %collective-permute-done.3.other, ...), custom_call_target="tpu_custom_call" | custom-call | tf_op jit(solution)/shard_map/pallas_call | solution.py:368
  93.5 0.0 all-to-all-done.3.stats_in.stats_all
  93.5 4.5 %all-to-all-start.2 = ((bf16[8,128,512]{2,1,0:T(8,128)(2,1)}), bf16[8,128,512]{2,1,0:T(8,128)(2,1)S(1)}, u32[]{:S(2)}, u32[]{:S(2)}) async-start(bf16[8,128,512]{2,1,0:T(8,128)(2,1)} %get-tuple-element.34), calls=%async_computation.2 | async-start | bytes 2097152 | tf_op jit(solution)/shard_map/all_to_all | solution.py:462
  98.0 7.0 %shard_map.107 = (bf16[2,512,128]{2,1,0:T(8,128)(2,1)}, bf16[2,512,128]{2,1,0:T(8,128)(2,1)}, bf16[2,512,128]{2,1,0:T(8,128)(2,1)}) custom-call(s32[32]{0:T(128)S(1)} %select_reduce_fusion.pairs, s32[4]{0:T(128)S(1)} %pad_add_fusion.meta, bf16[4,1040,128]{2,1,0:T(8,128)(2,1)S(1)} %all-to-all-done.1.own, ...), custom_call_target="tpu_custom_call" | custom-call | tf_op jit(solution)/shard_map/pallas_call | solution.py:368
  105.0 7.0 %collective-permute-start.4 = (bf16[2,512,128]{2,1,0:T(8,128)(2,1)}, bf16[2,512,128]{2,1,0:T(8,128)(2,1)}, u32[]{:S(2)}, u32[]{:S(2)}) collective-permute-start(bf16[2,512,128]{2,1,0:T(8,128)(2,1)} %get-tuple-element.40), channel_id=1, source_target_pairs={{0,384},{128,0},{256,128},{384,256},{1,385},{129,1},{257,129},{385... | collective-permute-start | bytes 786440 | tf_op jit(solution)/shard_map/ppermute | solution.py:400
  112.0 1.9 %collective-permute-start.5 = (bf16[2,512,128]{2,1,0:T(8,128)(2,1)}, bf16[2,512,128]{2,1,0:T(8,128)(2,1)}, u32[]{:S(2)}, u32[]{:S(2)}) collective-permute-start(bf16[2,512,128]{2,1,0:T(8,128)(2,1)} %get-tuple-element.41), channel_id=1, source_target_pairs={{0,256},{128,384},{256,0},{384,128},{1,257},{129,385},{257,1},{385... | collective-permute-start | bytes 786440 | tf_op jit(solution)/shard_map/ppermute | solution.py:400
  114.0 2.8 %collective-permute-start.6 = (bf16[2,512,128]{2,1,0:T(8,128)(2,1)}, bf16[2,512,128]{2,1,0:T(8,128)(2,1)}, u32[]{:S(2)}, u32[]{:S(2)}) collective-permute-start(bf16[2,512,128]{2,1,0:T(8,128)(2,1)} %get-tuple-element.42), channel_id=1, source_target_pairs={{0,128},{128,256},{256,384},{384,0},{1,129},{129,257},{257,385},{3... | collective-permute-start | bytes 786440 | tf_op jit(solution)/shard_map/ppermute | solution.py:400
  116.7 4.3 %shard_map.108.kept = bf16[2,512,128]{2,1,0:T(8,128)(2,1)S(1)} custom-call(s32[32]{0:T(128)S(1)} %select_reduce_fusion.pairs, s32[4]{0:T(128)S(1)} %pad_add_fusion.meta, bf16[4,1040,128]{2,1,0:T(8,128)(2,1)S(1)} %all-to-all-done.1.own, bf16[4,1040,128]{2,1,0:T(8,128)(2,1)S(1)} %collective-permute-done.3.other, ...), custom_call_target="tpu_custom_call" | custom-call | tf_op jit(solution)/shard_map/pallas_call | solution.py:368
  121.0 0.0 copy-start.1
  121.0 0.7 copy-done.1
  121.7 0.0 all-to-all-done.2.dquery_in
  121.7 0.0 copy-start.2
  121.7 1.0 shard_map.106.query_grad
  122.7 1.4 collective-permute-done.4.first
  124.1 0.7 collective-permute-done.5.second
  124.8 5.7 %collective-permute-done.6.third = bf16[2,512,128]{2,1,0:T(8,128)(2,1)} collective-permute-done((bf16[2,512,128]{2,1,0:T(8,128)(2,1)}, bf16[2,512,128]{2,1,0:T(8,128)(2,1)}, u32[]{:S(2)}, u32[]{:S(2)}) %collective-permute-start.6) | collective-permute-done | bytes 262176 | tf_op jit(solution)/shard_map/ppermute | solution.py:400
  130.5 0.0 copy-done.2
  130.5 1.3 shard_map.109
  131.8 34.0 %all_to_all.25.grads = bf16[16,96,128]{2,1,0:T(8,128)(2,1)S(1)} all-to-all(bf16[16,96,128]{2,1,0:T(8,128)(2,1)S(1)} %shard_map.109), channel_id=1, replica_groups=mesh['x'=4,'y'=4,'c'=2,'h'=16] {'h'}, dimensions={0} | all-to-all | bytes 786432 | tf_op jit(solution)/shard_map/all_to_all | solution.py:504
  165.8 0.8 shard_map.110
  (12 shorter events, 0.1 us)
Async XLA Ops:
  0.6 17.7 %copy-start = (s32[32]{0:T(128)S(1)}, s32[32]{0:T(128)}, u32[]{:S(2)}) copy-start(s32[32]{0:T(128)} %param.15) | copy-start | bytes 388
  0.6 17.5 %copy-start.4 = (s32[32,16]{0,1:T(8,128)S(1)}, s32[32,16]{0,1:T(8,128)}, u32[]{:S(2)}) copy-start(s32[32,16]{0,1:T(8,128)} %param.13) | copy-start | bytes 6148
  2.9 16.6 %copy-start.3 = (s32[32]{0:T(128)S(1)}, s32[32]{0:T(128)}, u32[]{:S(2)}) copy-start(s32[32]{0:T(128)} %param.14) | copy-start | bytes 388
  2.9 46.0 %all-to-all-start = ((bf16[16,144,128]{2,1,0:T(8,128)(2,1)}), bf16[16,144,128]{2,1,0:T(8,128)(2,1)S(1)}, u32[]{:S(2)}, u32[]{:S(2)}) async-start(bf16[16,144,128]{2,1,0:T(8,128)(2,1)} %shard_map.103), calls=%async_computation | async-start | bytes 1179648 | tf_op jit(solution)/shard_map/all_to_all | solution.py:419
  50.4 21.0 %all-to-all-start.1 = ((bf16[4,1040,128]{2,1,0:T(8,128)(2,1)}), bf16[4,1040,128]{2,1,0:T(8,128)(2,1)S(1)}, u32[]{:S(2)}, u32[]{:S(2)}) async-start(bf16[4,1040,128]{2,1,0:T(8,128)(2,1)} %broadcast_in_dim.12), calls=%async_computation.1 | async-start | bytes 2129920 | tf_op jit(solution)/shard_map/all_to_all | solution.py:431
  55.1 11.4 %collective-permute-start = (bf16[1024,128]{1,0:T(8,128)(2,1)S(1)}, bf16[1024,128]{1,0:T(8,128)(2,1)S(1)}, u32[]{:S(2)}, u32[]{:S(2)}) collective-permute-start(bf16[1024,128]{1,0:T(8,128)(2,1)S(1)} %pad_maximum_fusion.kv0), channel_id=1, source_target_pairs={{0,128},{128,256},{256,384},{384,0},{1,129},{129,257},{257,385},{3... | collective-permute-start | bytes 786440 | tf_op jit(solution)/shard_map/ppermute | solution.py:400
  58.5 9.9 %collective-permute-start.1 = (bf16[1024,128]{1,0:T(8,128)(2,1)S(1)}, bf16[1024,128]{1,0:T(8,128)(2,1)S(1)}, u32[]{:S(2)}, u32[]{:S(2)}) collective-permute-start(bf16[1024,128]{1,0:T(8,128)(2,1)S(1)} %pad_maximum_fusion.kv0), channel_id=1, source_target_pairs={{0,256},{128,384},{256,0},{384,128},{1,257},{129,385},{257,1},{385... | collective-permute-start | bytes 786440 | tf_op jit(solution)/shard_map/ppermute | solution.py:400
  63.1 8.3 %collective-permute-start.2 = (bf16[1024,128]{1,0:T(8,128)(2,1)S(1)}, bf16[1024,128]{1,0:T(8,128)(2,1)S(1)}, u32[]{:S(2)}, u32[]{:S(2)}) collective-permute-start(bf16[1024,128]{1,0:T(8,128)(2,1)S(1)} %pad_maximum_fusion.kv0), channel_id=1, source_target_pairs={{0,384},{128,0},{256,128},{384,256},{1,385},{129,1},{257,129},{385... | collective-permute-start | bytes 786440 | tf_op jit(solution)/shard_map/ppermute | solution.py:400
  71.4 4.6 %collective-permute-start.3 = (bf16[4,1040,128]{2,1,0:T(8,128)(2,1)S(1)}, bf16[4,1040,128]{2,1,0:T(8,128)(2,1)S(1)}, u32[]{:S(2)}, u32[]{:S(2)}) collective-permute-start(bf16[4,1040,128]{2,1,0:T(8,128)(2,1)S(1)} %all-to-all-done.1.own), channel_id=1, source_target_pairs={{0,16},{16,0},{1,17},{17,1},{2,18},{18,2},{3,19},{19,3},{4,20},{20... | collective-permute-start | bytes 3194888 | tf_op jit(solution)/shard_map/ppermute | solution.py:400
  81.8 11.6 %all-to-all-start.3 = ((f32[8,8,2,512]{3,2,1,0:T(2,128)}), f32[8,8,2,512]{3,2,1,0:T(2,128)S(1)}, u32[]{:S(2)}, u32[]{:S(2)}) async-start(f32[8,8,2,512]{3,2,1,0:T(2,128)} %get-tuple-element.32.stats_in), calls=%async_computation.3 | async-start | bytes 524288 | tf_op jit(solution)/shard_map/all_to_all | solution.py:449
  93.5 28.3 %all-to-all-start.2 = ((bf16[8,128,512]{2,1,0:T(8,128)(2,1)}), bf16[8,128,512]{2,1,0:T(8,128)(2,1)S(1)}, u32[]{:S(2)}, u32[]{:S(2)}) async-start(bf16[8,128,512]{2,1,0:T(8,128)(2,1)} %get-tuple-element.34), calls=%async_computation.2 | async-start | bytes 2097152 | tf_op jit(solution)/shard_map/all_to_all | solution.py:462
  105.0 19.1 %collective-permute-start.4 = (bf16[2,512,128]{2,1,0:T(8,128)(2,1)}, bf16[2,512,128]{2,1,0:T(8,128)(2,1)}, u32[]{:S(2)}, u32[]{:S(2)}) collective-permute-start(bf16[2,512,128]{2,1,0:T(8,128)(2,1)} %get-tuple-element.40), channel_id=1, source_target_pairs={{0,384},{128,0},{256,128},{384,256},{1,385},{129,1},{257,129},{385... | collective-permute-start | bytes 786440 | tf_op jit(solution)/shard_map/ppermute | solution.py:400
  112.0 12.7 %collective-permute-start.5 = (bf16[2,512,128]{2,1,0:T(8,128)(2,1)}, bf16[2,512,128]{2,1,0:T(8,128)(2,1)}, u32[]{:S(2)}, u32[]{:S(2)}) collective-permute-start(bf16[2,512,128]{2,1,0:T(8,128)(2,1)} %get-tuple-element.41), channel_id=1, source_target_pairs={{0,256},{128,384},{256,0},{384,128},{1,257},{129,385},{257,1},{385... | collective-permute-start | bytes 786440 | tf_op jit(solution)/shard_map/ppermute | solution.py:400
  114.0 16.6 %collective-permute-start.6 = (bf16[2,512,128]{2,1,0:T(8,128)(2,1)}, bf16[2,512,128]{2,1,0:T(8,128)(2,1)}, u32[]{:S(2)}, u32[]{:S(2)}) collective-permute-start(bf16[2,512,128]{2,1,0:T(8,128)(2,1)} %get-tuple-element.42), channel_id=1, source_target_pairs={{0,128},{128,256},{256,384},{384,0},{1,129},{129,257},{257,385},{3... | collective-permute-start | bytes 786440 | tf_op jit(solution)/shard_map/ppermute | solution.py:400
  121.0 0.7 copy-start.1
  121.7 8.8 %copy-start.2 = (bf16[2,512,128]{2,1,0:T(8,128)(2,1)S(1)}, bf16[2,512,128]{2,1,0:T(8,128)(2,1)}, u32[]{:S(2)}) copy-start(bf16[2,512,128]{2,1,0:T(8,128)(2,1)} %copy-done.1) | copy-start | bytes 786436

commit v10 on v8

--- a/solution.py
+++ b/solution.py
@@ -508,7 +508,7 @@
         out_shape=shape((HEADS, 3 * ROWS, HD), bf16),
         scratch_shapes=[pltpu.VMEM((NK, 2, BLK, HD), bf16), pltpu.VMEM((BLK, HD), bf16), dma((5,))],
         compiler_params=params(12),
-    )(query_grad, kept, arrived[1], arrived[2], arrived[3])
+    )(query_grad, kept, arrived[2], arrived[1], arrived[3])
     grads = lax.all_to_all(grads, "h", 0, 0, tiled=True)
 
     return pl.pallas_call(

time: 167 us -> 165 us (0.988)
  waiting for transfers between devices: 37 us -> 32.5 us
  Pallas kernels: 27.4 us -> 31.6 us
  blocking collectives: 33.9 us -> 32.2 us
    ppermute x7, waiting for transfers between devices: 12.9 us -> 8.5 us  [shifted(): lax.ppermute(array, axis, [(i, (i + by) % size) for i in range(size)])]
    pallas_call x4, Pallas kernels: 22 us -> 26.3 us  [over_pairs(): pl.pallas_call(kernel, grid_spec=pltpu.PrefetchScalarGridSpec(num_scalar_...]
    all_to_all x1, blocking collectives: 33.9 us -> 32.2 us  [on_device(): grads = lax.all_to_all(grads, 'h', 0, 0, tiled=True)]
  transfers between devices with their start and end apart: 11 -> 11, of which waited for: 6 -> 6; matrix products, arithmetic and copies ran while one was open for 4% -> 4% of each run, Pallas kernels for 11% -> 13%
where the time goes in v10:
time: 165 us; the launch traced here: 162 us
  starting transfers between devices  56.3 us (34%)
  waiting for transfers between devices  32.5 us (20%)
  blocking collectives  32.2 us (20%)
  Pallas kernels  31.6 us (19%)
  local copies, waits for them, and re-layouts  4.72 us (3%)
  other arithmetic  3.4 us (2%)
    all_to_all x1, blocking collectives, on_device(): grads = lax.all_to_all(grads, 'h', 0, 0, tiled=True)  32.2 us
    pallas_call x4, Pallas kernels, over_pairs(): pl.pallas_call(kernel, grid_spec=pltpu.PrefetchScalarGridSpec(num_scalar_...  26.3 us
    ppermute x7, starting transfers between devices, shifted(): lax.ppermute(array, axis, [(i, (i + by) % size) for i in range(size)])  24.8 us
    all_to_all x1, waiting for transfers between devices, on_device(): packed = lax.all_to_all(packed, 'h', 0, 0, tiled=True)  24 us
    all_to_all x1, starting transfers between devices, on_device(): packed = lax.all_to_all(packed, 'h', 0, 0, tiled=True)  15.2 us
    ppermute x7, waiting for transfers between devices, shifted(): lax.ppermute(array, axis, [(i, (i + by) % size) for i in range(size)])  8.5 us
    all_to_all x1, starting transfers between devices, on_device(): stats_all = lax.all_to_all(stats, ('y', 'c'), 0, 0, tiled=True)  5.94 us
    all_to_all x1, starting transfers between devices, on_device(): dquery = lax.all_to_all(dquery, ('y', 'c'), 0, 0, tiled=True)  5.7 us
  transfers between devices with their start and end apart: 11, of which 6 were waited for; matrix products, arithmetic and copies ran while one was open for 4% of the time, Pallas kernels for 13%

profile of v10, /device:TPU:24, one launch (start us, length us, event | category | flops | bytes accessed | tf_op | source)
XLA Modules:
  0.0 162.3 jit_solution(1358120743760043035)
XLA Ops:
  0.6 0.0 copy-start
  0.6 0.0 copy-start.4
  0.7 2.3 %shard_map.103 = bf16[16,144,128]{2,1,0:T(8,128)(2,1)} custom-call(bf16[32,2048]{1,0:T(8,128)(2,1)} %query_in.1, bf16[32,2048]{1,0:T(8,128)(2,1)} %key_in.1, bf16[32,2048]{1,0:T(8,128)(2,1)} %value_in.1, bf16[32,2048]{1,0:T(8,128)(2,1)} %output_in.1, bf16[32,2048]{1,0:T(8,128)(2,1)} %grad_in.1), custom_call_target="tpu_custom_call" | custom-call | tf_op jit(solution)/shard_map/pallas_call | solution.py:419
  2.9 0.0 copy-start.3
  2.9 15.2 %all-to-all-start = ((bf16[16,144,128]{2,1,0:T(8,128)(2,1)}), bf16[16,144,128]{2,1,0:T(8,128)(2,1)S(1)}, u32[]{:S(2)}, u32[]{:S(2)}) async-start(bf16[16,144,128]{2,1,0:T(8,128)(2,1)} %shard_map.103), calls=%async_computation | async-start | bytes 1179648 | tf_op jit(solution)/shard_map/all_to_all | solution.py:427
  18.2 0.0 copy-done.4
  18.2 0.1 copy.14
  18.3 0.0 copy-done
  18.3 0.6 gather_fusion
  19.0 0.6 gather_fusion.1
  19.5 0.0 copy-done.3
  19.5 0.6 gather_fusion.3
  20.2 0.6 gather_fusion.2
  20.8 0.1 iota_compare_fusion.1
  20.9 0.2 and_reduce_fusion
  21.1 0.1 and.87
  21.2 0.7 convert_reduce_fusion.1
  22.6 0.6 fusion.8
  23.3 1.4 pad_add_fusion.meta
  24.6 0.1 convert_reduce_fusion
  24.8 0.2 select_reduce_fusion.pairs
  24.9 24.0 %all-to-all-done = bf16[16,144,128]{2,1,0:T(8,128)(2,1)S(1)} async-done(((bf16[16,144,128]{2,1,0:T(8,128)(2,1)}), bf16[16,144,128]{2,1,0:T(8,128)(2,1)S(1)}, u32[]{:S(2)}, u32[]{:S(2)}) %all-to-all-start) | async-done | bytes 589856 | tf_op jit(solution)/shard_map/all_to_all | solution.py:427
  49.1 0.1 reshape.218
  49.1 0.1 concatenate.6
  49.2 1.1 broadcast_in_dim.12
  50.4 4.7 %all-to-all-start.1 = ((bf16[4,1040,128]{2,1,0:T(8,128)(2,1)}), bf16[4,1040,128]{2,1,0:T(8,128)(2,1)S(1)}, u32[]{:S(2)}, u32[]{:S(2)}) async-start(bf16[4,1040,128]{2,1,0:T(8,128)(2,1)} %broadcast_in_dim.12), calls=%async_computation.1 | async-start | bytes 2129920 | tf_op jit(solution)/shard_map/all_to_all | solution.py:439
  55.1 3.4 %collective-permute-start = (bf16[1024,128]{1,0:T(8,128)(2,1)S(1)}, bf16[1024,128]{1,0:T(8,128)(2,1)S(1)}, u32[]{:S(2)}, u32[]{:S(2)}) collective-permute-start(bf16[1024,128]{1,0:T(8,128)(2,1)S(1)} %pad_maximum_fusion.kv0), channel_id=1, source_target_pairs={{0,128},{128,256},{256,384},{384,0},{1,129},{129,257},{257,385},{3... | collective-permute-start | bytes 786440 | tf_op jit(solution)/shard_map/ppermute | solution.py:408
  58.5 4.6 %collective-permute-start.1 = (bf16[1024,128]{1,0:T(8,128)(2,1)S(1)}, bf16[1024,128]{1,0:T(8,128)(2,1)S(1)}, u32[]{:S(2)}, u32[]{:S(2)}) collective-permute-start(bf16[1024,128]{1,0:T(8,128)(2,1)S(1)} %pad_maximum_fusion.kv0), channel_id=1, source_target_pairs={{0,256},{128,384},{256,0},{384,128},{1,257},{129,385},{257,1},{385... | collective-permute-start | bytes 786440 | tf_op jit(solution)/shard_map/ppermute | solution.py:408
  63.1 3.3 %collective-permute-start.2 = (bf16[1024,128]{1,0:T(8,128)(2,1)S(1)}, bf16[1024,128]{1,0:T(8,128)(2,1)S(1)}, u32[]{:S(2)}, u32[]{:S(2)}) collective-permute-start(bf16[1024,128]{1,0:T(8,128)(2,1)S(1)} %pad_maximum_fusion.kv0), channel_id=1, source_target_pairs={{0,384},{128,0},{256,128},{384,256},{1,385},{129,1},{257,129},{385... | collective-permute-start | bytes 786440 | tf_op jit(solution)/shard_map/ppermute | solution.py:408
  66.5 0.0 collective-permute-done.kv1
  66.5 1.9 %collective-permute-done.1.kv2 = bf16[1024,128]{1,0:T(8,128)(2,1)S(1)} collective-permute-done((bf16[1024,128]{1,0:T(8,128)(2,1)S(1)}, bf16[1024,128]{1,0:T(8,128)(2,1)S(1)}, u32[]{:S(2)}, u32[]{:S(2)}) %collective-permute-start.1) | collective-permute-done | bytes 262176 | tf_op jit(solution)/shard_map/ppermute | solution.py:408
  68.3 3.0 %collective-permute-done.2.kv3 = bf16[1024,128]{1,0:T(8,128)(2,1)S(1)} collective-permute-done((bf16[1024,128]{1,0:T(8,128)(2,1)S(1)}, bf16[1024,128]{1,0:T(8,128)(2,1)S(1)}, u32[]{:S(2)}, u32[]{:S(2)}) %collective-permute-start.2) | collective-permute-done | bytes 262176 | tf_op jit(solution)/shard_map/ppermute | solution.py:408
  71.4 0.0 all-to-all-done.1.own
  71.4 1.9 %collective-permute-start.3 = (bf16[4,1040,128]{2,1,0:T(8,128)(2,1)S(1)}, bf16[4,1040,128]{2,1,0:T(8,128)(2,1)S(1)}, u32[]{:S(2)}, u32[]{:S(2)}) collective-permute-start(bf16[4,1040,128]{2,1,0:T(8,128)(2,1)S(1)} %all-to-all-done.1.own), channel_id=1, source_target_pairs={{0,16},{16,0},{1,17},{17,1},{2,18},{18,2},{3,19},{19,3},{4,20},{20... | collective-permute-start | bytes 3194888 | tf_op jit(solution)/shard_map/ppermute | solution.py:408
  73.3 2.6 %collective-permute-done.3.other = bf16[4,1040,128]{2,1,0:T(8,128)(2,1)S(1)} collective-permute-done((bf16[4,1040,128]{2,1,0:T(8,128)(2,1)S(1)}, bf16[4,1040,128]{2,1,0:T(8,128)(2,1)S(1)}, u32[]{:S(2)}, u32[]{:S(2)}) %collective-permute-start.3) | collective-permute-done | bytes 1064992 | tf_op jit(solution)/shard_map/ppermute | solution.py:408
  76.0 5.9 %shard_map.104 = (bf16[32,512,512]{2,1,0:T(8,128)(2,1)}, f32[32,1,512]{2,1,0:T(1,128)S(1)}, f32[8,8,2,512]{3,2,1,0:T(2,128)}) custom-call(s32[32]{0:T(128)S(1)} %select_reduce_fusion.pairs, s32[4]{0:T(128)S(1)} %pad_add_fusion.meta, bf16[4,1040,128]{2,1,0:T(8,128)(2,1)S(1)} %all-to-all-done.1.own, bf16[4,1040,128]{2,1,0:T(8,128)(2,1)S(1)} %collective-permute-done.3.other, ...), custom_call_target="tpu_custom_call" | custom-call | tf_op jit(solution)/shard_map/pallas_call | solution.py:376
  81.9 5.9 %all-to-all-start.3 = ((f32[8,8,2,512]{3,2,1,0:T(2,128)}), f32[8,8,2,512]{3,2,1,0:T(2,128)S(1)}, u32[]{:S(2)}, u32[]{:S(2)}) async-start(f32[8,8,2,512]{3,2,1,0:T(2,128)} %get-tuple-element.32.stats_in), calls=%async_computation.3 | async-start | bytes 524288 | tf_op jit(solution)/shard_map/all_to_all | solution.py:457
  87.8 7.1 %shard_map.105 = (bf16[32,512,512]{2,1,0:T(8,128)(2,1)}, bf16[8,128,512]{2,1,0:T(8,128)(2,1)}) custom-call(s32[32]{0:T(128)S(1)} %select_reduce_fusion.pairs, s32[4]{0:T(128)S(1)} %pad_add_fusion.meta, bf16[4,1040,128]{2,1,0:T(8,128)(2,1)S(1)} %all-to-all-done.1.own, bf16[4,1040,128]{2,1,0:T(8,128)(2,1)S(1)} %collective-permute-done.3.other, ...), custom_call_target="tpu_custom_call" | custom-call | tf_op jit(solution)/shard_map/pallas_call | solution.py:376
  94.9 0.0 all-to-all-done.3.stats_in.stats_all
  94.9 5.7 %all-to-all-start.2 = ((bf16[8,128,512]{2,1,0:T(8,128)(2,1)}), bf16[8,128,512]{2,1,0:T(8,128)(2,1)S(1)}, u32[]{:S(2)}, u32[]{:S(2)}) async-start(bf16[8,128,512]{2,1,0:T(8,128)(2,1)} %get-tuple-element.34), calls=%async_computation.2 | async-start | bytes 2097152 | tf_op jit(solution)/shard_map/all_to_all | solution.py:470
  100.6 7.2 %shard_map.107 = (bf16[2,512,128]{2,1,0:T(8,128)(2,1)}, bf16[2,512,128]{2,1,0:T(8,128)(2,1)}, bf16[2,512,128]{2,1,0:T(8,128)(2,1)}) custom-call(s32[32]{0:T(128)S(1)} %select_reduce_fusion.pairs, s32[4]{0:T(128)S(1)} %pad_add_fusion.meta, bf16[4,1040,128]{2,1,0:T(8,128)(2,1)S(1)} %all-to-all-done.1.own, ...), custom_call_target="tpu_custom_call" | custom-call | tf_op jit(solution)/shard_map/pallas_call | solution.py:376
  107.8 3.3 %collective-permute-start.4 = (bf16[2,512,128]{2,1,0:T(8,128)(2,1)}, bf16[2,512,128]{2,1,0:T(8,128)(2,1)}, u32[]{:S(2)}, u32[]{:S(2)}) collective-permute-start(bf16[2,512,128]{2,1,0:T(8,128)(2,1)} %get-tuple-element.40), channel_id=1, source_target_pairs={{0,256},{128,384},{256,0},{384,128},{1,257},{129,385},{257,1},{385... | collective-permute-start | bytes 786440 | tf_op jit(solution)/shard_map/ppermute | solution.py:408
  111.1 5.4 %collective-permute-start.5 = (bf16[2,512,128]{2,1,0:T(8,128)(2,1)}, bf16[2,512,128]{2,1,0:T(8,128)(2,1)}, u32[]{:S(2)}, u32[]{:S(2)}) collective-permute-start(bf16[2,512,128]{2,1,0:T(8,128)(2,1)} %get-tuple-element.41), channel_id=1, source_target_pairs={{0,384},{128,0},{256,128},{384,256},{1,385},{129,1},{257,129},{385... | collective-permute-start | bytes 786440 | tf_op jit(solution)/shard_map/ppermute | solution.py:408
  116.5 2.8 %collective-permute-start.6 = (bf16[2,512,128]{2,1,0:T(8,128)(2,1)}, bf16[2,512,128]{2,1,0:T(8,128)(2,1)}, u32[]{:S(2)}, u32[]{:S(2)}) collective-permute-start(bf16[2,512,128]{2,1,0:T(8,128)(2,1)} %get-tuple-element.42), channel_id=1, source_target_pairs={{0,128},{128,256},{256,384},{384,0},{1,129},{129,257},{257,385},{3... | collective-permute-start | bytes 786440 | tf_op jit(solution)/shard_map/ppermute | solution.py:408
  119.3 6.1 %shard_map.108.kept = bf16[2,512,128]{2,1,0:T(8,128)(2,1)S(1)} custom-call(s32[32]{0:T(128)S(1)} %select_reduce_fusion.pairs, s32[4]{0:T(128)S(1)} %pad_add_fusion.meta, bf16[4,1040,128]{2,1,0:T(8,128)(2,1)S(1)} %all-to-all-done.1.own, bf16[4,1040,128]{2,1,0:T(8,128)(2,1)S(1)} %collective-permute-done.3.other, ...), custom_call_target="tpu_custom_call" | custom-call | tf_op jit(solution)/shard_map/pallas_call | solution.py:376
  125.4 0.0 copy-start.1
  125.4 0.7 copy-done.1
  126.1 0.0 all-to-all-done.2.dquery_in
  126.1 0.0 copy-start.2
  126.1 1.0 shard_map.106.query_grad
  127.1 0.0 collective-permute-done.4.first
  127.1 0.7 collective-permute-done.5.second
  127.7 0.3 collective-permute-done.6.third
  128.0 0.0 copy-done.2
  128.0 1.3 shard_map.109
  129.3 32.2 %all_to_all.25.grads = bf16[16,96,128]{2,1,0:T(8,128)(2,1)S(1)} all-to-all(bf16[16,96,128]{2,1,0:T(8,128)(2,1)S(1)} %shard_map.109), channel_id=1, replica_groups=mesh['x'=4,'y'=4,'c'=2,'h'=16] {'h'}, dimensions={0} | all-to-all | bytes 786432 | tf_op jit(solution)/shard_map/all_to_all | solution.py:512
  161.5 0.8 shard_map.110
  (12 shorter events, 0.1 us)
Async XLA Ops:
  0.6 17.7 %copy-start = (s32[32]{0:T(128)S(1)}, s32[32]{0:T(128)}, u32[]{:S(2)}) copy-start(s32[32]{0:T(128)} %param.15) | copy-start | bytes 388
  0.6 17.5 %copy-start.4 = (s32[32,16]{0,1:T(8,128)S(1)}, s32[32,16]{0,1:T(8,128)}, u32[]{:S(2)}) copy-start(s32[32,16]{0,1:T(8,128)} %param.13) | copy-start | bytes 6148
  2.9 16.6 %copy-start.3 = (s32[32]{0:T(128)S(1)}, s32[32]{0:T(128)}, u32[]{:S(2)}) copy-start(s32[32]{0:T(128)} %param.14) | copy-start | bytes 388
  2.9 46.0 %all-to-all-start = ((bf16[16,144,128]{2,1,0:T(8,128)(2,1)}), bf16[16,144,128]{2,1,0:T(8,128)(2,1)S(1)}, u32[]{:S(2)}, u32[]{:S(2)}) async-start(bf16[16,144,128]{2,1,0:T(8,128)(2,1)} %shard_map.103), calls=%async_computation | async-start | bytes 1179648 | tf_op jit(solution)/shard_map/all_to_all | solution.py:427
  50.4 21.0 %all-to-all-start.1 = ((bf16[4,1040,128]{2,1,0:T(8,128)(2,1)}), bf16[4,1040,128]{2,1,0:T(8,128)(2,1)S(1)}, u32[]{:S(2)}, u32[]{:S(2)}) async-start(bf16[4,1040,128]{2,1,0:T(8,128)(2,1)} %broadcast_in_dim.12), calls=%async_computation.1 | async-start | bytes 2129920 | tf_op jit(solution)/shard_map/all_to_all | solution.py:439
  55.1 11.4 %collective-permute-start = (bf16[1024,128]{1,0:T(8,128)(2,1)S(1)}, bf16[1024,128]{1,0:T(8,128)(2,1)S(1)}, u32[]{:S(2)}, u32[]{:S(2)}) collective-permute-start(bf16[1024,128]{1,0:T(8,128)(2,1)S(1)} %pad_maximum_fusion.kv0), channel_id=1, source_target_pairs={{0,128},{128,256},{256,384},{384,0},{1,129},{129,257},{257,385},{3... | collective-permute-start | bytes 786440 | tf_op jit(solution)/shard_map/ppermute | solution.py:408
  58.5 9.9 %collective-permute-start.1 = (bf16[1024,128]{1,0:T(8,128)(2,1)S(1)}, bf16[1024,128]{1,0:T(8,128)(2,1)S(1)}, u32[]{:S(2)}, u32[]{:S(2)}) collective-permute-start(bf16[1024,128]{1,0:T(8,128)(2,1)S(1)} %pad_maximum_fusion.kv0), channel_id=1, source_target_pairs={{0,256},{128,384},{256,0},{384,128},{1,257},{129,385},{257,1},{385... | collective-permute-start | bytes 786440 | tf_op jit(solution)/shard_map/ppermute | solution.py:408
  63.1 8.3 %collective-permute-start.2 = (bf16[1024,128]{1,0:T(8,128)(2,1)S(1)}, bf16[1024,128]{1,0:T(8,128)(2,1)S(1)}, u32[]{:S(2)}, u32[]{:S(2)}) collective-permute-start(bf16[1024,128]{1,0:T(8,128)(2,1)S(1)} %pad_maximum_fusion.kv0), channel_id=1, source_target_pairs={{0,384},{128,0},{256,128},{384,256},{1,385},{129,1},{257,129},{385... | collective-permute-start | bytes 786440 | tf_op jit(solution)/shard_map/ppermute | solution.py:408
  71.4 4.6 %collective-permute-start.3 = (bf16[4,1040,128]{2,1,0:T(8,128)(2,1)S(1)}, bf16[4,1040,128]{2,1,0:T(8,128)(2,1)S(1)}, u32[]{:S(2)}, u32[]{:S(2)}) collective-permute-start(bf16[4,1040,128]{2,1,0:T(8,128)(2,1)S(1)} %all-to-all-done.1.own), channel_id=1, source_target_pairs={{0,16},{16,0},{1,17},{17,1},{2,18},{18,2},{3,19},{19,3},{4,20},{20... | collective-permute-start | bytes 3194888 | tf_op jit(solution)/shard_map/ppermute | solution.py:408
  81.9 13.0 %all-to-all-start.3 = ((f32[8,8,2,512]{3,2,1,0:T(2,128)}), f32[8,8,2,512]{3,2,1,0:T(2,128)S(1)}, u32[]{:S(2)}, u32[]{:S(2)}) async-start(f32[8,8,2,512]{3,2,1,0:T(2,128)} %get-tuple-element.32.stats_in), calls=%async_computation.3 | async-start | bytes 524288 | tf_op jit(solution)/shard_map/all_to_all | solution.py:457
  94.9 31.2 %all-to-all-start.2 = ((bf16[8,128,512]{2,1,0:T(8,128)(2,1)}), bf16[8,128,512]{2,1,0:T(8,128)(2,1)S(1)}, u32[]{:S(2)}, u32[]{:S(2)}) async-start(bf16[8,128,512]{2,1,0:T(8,128)(2,1)} %get-tuple-element.34), calls=%async_computation.2 | async-start | bytes 2097152 | tf_op jit(solution)/shard_map/all_to_all | solution.py:470
  107.8 19.3 %collective-permute-start.4 = (bf16[2,512,128]{2,1,0:T(8,128)(2,1)}, bf16[2,512,128]{2,1,0:T(8,128)(2,1)}, u32[]{:S(2)}, u32[]{:S(2)}) collective-permute-start(bf16[2,512,128]{2,1,0:T(8,128)(2,1)} %get-tuple-element.40), channel_id=1, source_target_pairs={{0,256},{128,384},{256,0},{384,128},{1,257},{129,385},{257,1},{385... | collective-permute-start | bytes 786440 | tf_op jit(solution)/shard_map/ppermute | solution.py:408
  111.1 16.6 %collective-permute-start.5 = (bf16[2,512,128]{2,1,0:T(8,128)(2,1)}, bf16[2,512,128]{2,1,0:T(8,128)(2,1)}, u32[]{:S(2)}, u32[]{:S(2)}) collective-permute-start(bf16[2,512,128]{2,1,0:T(8,128)(2,1)} %get-tuple-element.41), channel_id=1, source_target_pairs={{0,384},{128,0},{256,128},{384,256},{1,385},{129,1},{257,129},{385... | collective-permute-start | bytes 786440 | tf_op jit(solution)/shard_map/ppermute | solution.py:408
  116.5 11.5 %collective-permute-start.6 = (bf16[2,512,128]{2,1,0:T(8,128)(2,1)}, bf16[2,512,128]{2,1,0:T(8,128)(2,1)}, u32[]{:S(2)}, u32[]{:S(2)}) collective-permute-start(bf16[2,512,128]{2,1,0:T(8,128)(2,1)} %get-tuple-element.42), channel_id=1, source_target_pairs={{0,128},{128,256},{256,384},{384,0},{1,129},{129,257},{257,385},{3... | collective-permute-start | bytes 786440 | tf_op jit(solution)/shard_map/ppermute | solution.py:408
  125.4 0.7 copy-start.1
  126.1 1.9 %copy-start.2 = (bf16[2,512,128]{2,1,0:T(8,128)(2,1)S(1)}, bf16[2,512,128]{2,1,0:T(8,128)(2,1)}, u32[]{:S(2)}) copy-start(bf16[2,512,128]{2,1,0:T(8,128)(2,1)} %copy-done.1) | copy-start | bytes 786436
